TPU v7x, 512 devices: a whole 4x4x16 slice. The times are simulated.
512 devices in a mesh: dp: 16 (over y, x_hi, core), segment: 2 (over x_lo), tensor: 16 (over z).
Axes of the slice: x: 4 (x_hi: 2, x_lo: 2; x = x_hi * 2 + x_lo), y: 4, z: 16, core: 2. Of those that a mesh axis runs over, the one named last changes fastest.
Arguments:
- queries: bfloat16 [16, 256, 4096], P('dp', None, ('segment', 'tensor')), may hold values from -3 to 3
- encoded: bfloat16 [16, 256, 8192], P('dp', None, ('segment', 'tensor')), may hold values from -8 to 8
- neighbour_ids: int32 [16, 8], P('dp'), may hold values from 0 to 7, each once within a row
- key_weight: bfloat16 [8192, 4096], P('dp', ('segment', 'tensor')), may hold values from -0.0625 to 0.0625
- value_weight: bfloat16 [8192, 4096], P('dp', ('segment', 'tensor')), may hold values from -0.0625 to 0.0625
- grad_context: bfloat16 [16, 256, 4096], P('dp', None, ('segment', 'tensor')), may hold values from -3 to 3
Outputs:
- context: bfloat16 [16, 256, 4096], P('dp', None, ('segment', 'tensor'))
- grad_queries: bfloat16 [16, 256, 4096], P('dp', None, ('segment', 'tensor'))
- grad_encoded: bfloat16 [16, 256, 8192], P('dp', None, ('segment', 'tensor'))
- grad_key_weight: bfloat16 [8192, 4096], P('dp', ('segment', 'tensor'))
- grad_value_weight: bfloat16 [8192, 4096], P('dp', ('segment', 'tensor'))
Inputs may be any that keep to these rules, and one draw needn't show every extreme that they name: `neighbour_ids`: each row lists, at position u * 2 + j, the pool entry retrieved as neighbour j of span u; every one of the 8 entries appears exactly once in a row.
All inputs are finite; a program needn't handle non-finite values.
Results may differ from a plain program's by a relative error of at most 0.03.
Values may be sent and summed in bfloat16 or wider, within the bound.
No kernel may reach another device: no remote copies, remote signals or barrier semaphores. Data moves between devices by JAX's collectives and lax.ppermute only.
A program may use at most 64 MiB of HBM per device.

v0:
```python
import math

import jax
import jax.numpy as jnp
from jax import lax
from jax.sharding import PartitionSpec as P

HD = 128
CLEN = 64
NEIGH = 2
NTOK = 32
SPANS = 4


def to_blocks(row_data):
    padding = jnp.zeros((CLEN - 1,) + row_data.shape[1:], row_data.dtype)
    joined = jnp.concatenate([row_data[CLEN - 1 :], padding], 0)
    return joined.reshape((SPANS, CLEN) + row_data.shape[1:])


def from_blocks(blocks):
    flattened = blocks.reshape((SPANS * CLEN,) + blocks.shape[2:])
    padding = jnp.zeros((CLEN - 1,) + flattened.shape[1:], flattened.dtype)
    return jnp.concatenate([padding, flattened[: SPANS * CLEN - (CLEN - 1)]], 0)


def per_device(queries, encoded, neighbour_ids, key_weight, value_weight, grad_context):
    inverse_root = 1.0 / math.sqrt(HD)
    columns = queries.shape[2]
    heads_here = columns // HD
    seq_rows = SPANS * CLEN
    pool_rows = SPANS * NEIGH * NTOK
    enc_full = lax.all_gather(encoded, ("segment", "tensor"), axis=2, tiled=True)[0]
    stacked = jnp.concatenate([key_weight, value_weight], axis=1)
    full_weights = lax.all_gather(stacked, "dp", axis=0, tiled=True)
    key_value = jnp.dot(enc_full, full_weights, preferred_element_type=jnp.float32)
    keys = key_value[:, :columns].astype(jnp.bfloat16)
    values = key_value[:, columns:].astype(jnp.bfloat16)
    entries = neighbour_ids[0]
    span_keys = jnp.take(keys.reshape(SPANS * NEIGH, NTOK, heads_here, HD), entries, axis=0)
    span_keys = span_keys.reshape(SPANS, NEIGH * NTOK, heads_here, HD)
    span_values = jnp.take(values.reshape(SPANS * NEIGH, NTOK, heads_here, HD), entries, axis=0)
    span_values = span_values.reshape(SPANS, NEIGH * NTOK, heads_here, HD)
    query_blocks = to_blocks(queries[0].reshape(seq_rows, heads_here, HD))
    grad_blocks = to_blocks(grad_context[0].reshape(seq_rows, heads_here, HD))
    scores = (
        jnp.einsum("uihd,ukhd->uhik", query_blocks, span_keys, preferred_element_type=jnp.float32)
        * inverse_root
    )
    exponent = jnp.exp(scores)
    probs = exponent / jnp.sum(exponent, -1, keepdims=True)
    attn_weights = probs.astype(jnp.bfloat16)
    context = jnp.einsum(
        "uhik,ukhd->uihd", attn_weights, span_values, preferred_element_type=jnp.float32
    )
    context = from_blocks(context).reshape(seq_rows, columns).astype(jnp.bfloat16)
    dprob = jnp.einsum(
        "uihd,ukhd->uhik", grad_blocks, span_values, preferred_element_type=jnp.float32
    )
    scaled_grad = (
        probs * (dprob - jnp.sum(probs * dprob, -1, keepdims=True)) * inverse_root
    ).astype(jnp.bfloat16)
    query_grad = jnp.einsum(
        "uhik,ukhd->uihd", scaled_grad, span_keys, preferred_element_type=jnp.float32
    )
    query_grad = from_blocks(query_grad).reshape(seq_rows, columns).astype(jnp.bfloat16)
    grad_span_keys = jnp.einsum(
        "uhik,uihd->ukhd", scaled_grad, query_blocks, preferred_element_type=jnp.float32
    ).astype(jnp.bfloat16)
    grad_span_values = jnp.einsum(
        "uhik,uihd->ukhd", attn_weights, grad_blocks, preferred_element_type=jnp.float32
    ).astype(jnp.bfloat16)
    inverse_order = jnp.argsort(entries)
    grad_keys = jnp.take(
        grad_span_keys.reshape(SPANS * NEIGH, NTOK, heads_here, HD), inverse_order, axis=0
    )
    grad_values = jnp.take(
        grad_span_values.reshape(SPANS * NEIGH, NTOK, heads_here, HD), inverse_order, axis=0
    )
    grad_both = jnp.concatenate(
        [grad_keys.reshape(pool_rows, columns), grad_values.reshape(pool_rows, columns)], axis=1
    )
    weight_grad = lax.psum_scatter(
        lax.dot_general(
            enc_full, grad_both, (((0,), (0,)), ((), ())), preferred_element_type=jnp.float32
        ).astype(jnp.bfloat16),
        "dp",
        scatter_dimension=0,
        tiled=True,
    ).astype(jnp.float32)
    grad_key_weight = weight_grad[:, :columns].astype(jnp.bfloat16)
    grad_value_weight = weight_grad[:, columns:].astype(jnp.bfloat16)
    partial_grad = lax.dot_general(
        grad_both, full_weights, (((1,), (1,)), ((), ())), preferred_element_type=jnp.float32
    )
    own_width = encoded.shape[2]
    summed = lax.psum(partial_grad.astype(jnp.bfloat16), ("segment", "tensor")).astype(jnp.float32)
    own_grad = lax.dynamic_slice_in_dim(
        summed, lax.axis_index(("segment", "tensor")) * own_width, own_width, 1
    )
    grad_encoded = own_grad.astype(jnp.bfloat16)[None]
    return (context[None], query_grad[None], grad_encoded, grad_key_weight, grad_value_weight)


def solution(mesh):
    return jax.shard_map(
        per_device,
        mesh=mesh,
        in_specs=(
            P("dp", None, ("segment", "tensor")),
            P("dp", None, ("segment", "tensor")),
            P("dp", None),
            P("dp", ("segment", "tensor")),
            P("dp", ("segment", "tensor")),
            P("dp", None, ("segment", "tensor")),
        ),
        out_specs=(
            P("dp", None, ("segment", "tensor")),
            P("dp", None, ("segment", "tensor")),
            P("dp", None, ("segment", "tensor")),
            P("dp", ("segment", "tensor")),
            P("dp", ("segment", "tensor")),
        ),
        check_vma=False,
    )
```

profile of v0, /device:TPU:6, one launch (start us, length us, event | category | flops | bytes accessed | tf_op | source)
XLA Modules:
  0.0 621.6 jit_solution(5283445690138395958)
XLA Ops:
  7.2 0.0 all-gather.3.cloned.1.call-start
  7.2 1.7 pad_maximum_fusion
  8.9 0.0 all-gather.3.cloned.1.call-update
  8.9 0.0 all-gather.5.cloned.1.call-start
  9.0 0.7 all-gather.5.cloned.1.call-update
  9.7 0.0 all-reduce.6.cloned.1.call-start
  9.7 0.8 slice_bitcast_fusion.1
  10.6 0.8 slice_bitcast_fusion
  11.4 1.6 sort.17
  13.0 0.7 compare_select_fusion.1
  13.7 0.7 compare_and_fusion.1
  14.4 70.5 %all-gather.3.cloned.1.call-done = bf16[8192,256]{1,0:T(8,128)(2,1)} async-done(((bf16[512,256]{1,0:T(8,128)(2,1)}), bf16[8192,256]{1,0:T(8,128)(2,1)}) %all-gather.3.cloned.1.call-update) | async-done | bytes 4194320 | tf_op jit(solution)/shard_map/all_gather | solution.py:35
  84.9 144.0 %all-gather.5.cloned.1.call-done = bf16[1,256,8192]{2,1,0:T(8,128)(2,1)} async-done(((bf16[1,256,256]{2,1,0:T(8,128)(2,1)}), bf16[1,256,8192]{2,1,0:T(8,128)(2,1)}) %all-gather.5.cloned.1.call-update) | async-done | bytes 4194320 | tf_op jit(solution)/shard_map/all_gather | solution.py:33
  228.9 4.7 fusion.12
  233.6 0.6 gather_fusion.1
  234.2 0.6 gather_fusion
  234.7 0.1 bitcast_select_fusion.2
  234.8 0.2 fusion.22
  235.0 0.2 fusion.9
  235.2 0.1 fusion.38
  235.4 0.2 convolution_convert_fusion.2
  235.5 0.2 convolution_convert_fusion.3
  235.7 0.6 gather_fusion.3
  236.3 0.6 gather_fusion.2
  236.8 0.1 bitcast_select_fusion.1
  236.9 5.5 convolution_convert_fusion.1
  242.4 0.0 all-reduce.6.cloned.1.call-update
  242.4 0.0 reduce-scatter.2.cloned.1.call-start
  242.5 5.4 fusion.1
  247.9 0.0 reduce-scatter.2.cloned.1.call-update
  247.9 0.2 convolution_convert_fusion.5
  248.2 0.2 convolution_convert_fusion.4
  248.4 0.7 pad_bitcast_fusion
  249.1 262.1 %all-reduce.6.cloned.1.call-done = bf16[256,8192]{1,0:T(8,128)(2,1)} async-done(((bf16[256,8192]{1,0:T(8,128)(2,1)}), bf16[256,8192]{1,0:T(8,128)(2,1)}) %all-reduce.6.cloned.1.call-update) | async-done | bytes 4194320 | tf_op jit(solution)/shard_map/psum | solution.py:97
  511.2 1.6 fusion.20
  512.7 99.8 %reduce-scatter.2.cloned.1.call-done = bf16[512,256]{0,1:T(8,128)(2,1)} async-done(((bf16[8192,256]{0,1:T(8,128)(2,1)}), bf16[512,256]{0,1:T(8,128)(2,1)}) %reduce-scatter.2.cloned.1.call-update) | async-done | bytes 262160 | tf_op jit(solution)/shard_map/reduce_scatter | solution.py:83
  612.6 1.0 fusion.36
  613.5 0.8 copy.14
  614.3 0.8 copy.13
  (10 shorter events, 0.1 us)
Async XLA Ops:
  7.2 77.7 %all-gather.3.cloned.1.call-start = ((), (), s32[]{:S(2)}) async-start(), calls=%async_computation.1 | async-start | bytes 4456448 | tf_op jit(solution)/shard_map/all_gather | solution.py:35
  8.9 219.9 %all-gather.5.cloned.1.call-start = ((), (), s32[]{:S(2)}) async-start(), calls=%async_computation.2 | async-start | bytes 4325376 | tf_op jit(solution)/shard_map/all_gather | solution.py:33
  9.7 501.5 %all-reduce.6.cloned.1.call-start = ((), (), s32[]{:S(2)}) async-start(), calls=%async_computation.3 | async-start | bytes 8388608 | tf_op jit(solution)/shard_map/psum | solution.py:97
  242.4 370.1 %reduce-scatter.2.cloned.1.call-start = ((), (), s32[]{:S(2)}) async-start(), calls=%async_computation.4 | async-start | bytes 4456448 | tf_op jit(solution)/shard_map/reduce_scatter | solution.py:83
Sparse Core Ops, SparseCore 0:
  11.3 73.4 all-gather.2
  86.9 141.9 all-gather.4
  242.5 268.5 all-reduce.5
  515.9 96.6 reduce-scatter.1
where the time goes:
time: 623 us; the launch traced here: 622 us
  waiting for transfers between devices  577 us (93%)
  matrix products  16.9 us (3%)
  between operations  13.9 us (2%)
  local copies, waits for them, and re-layouts  7.13 us (1%)
  other arithmetic  6.38 us (1%)
    psum x1, waiting for transfers between devices, per_device(): lax.psum(partial_grad.astype(jnp.bfloat16), ('segment', 'tensor'))  262 us
    all_gather x1, waiting for transfers between devices, per_device(): lax.all_gather(encoded, ('segment', 'tensor'), axis=2, tiled=True)[0]  144 us
    reduce_scatter x1, waiting for transfers between devices, per_device(): lax.psum_scatter(lax.dot_general(enc_full, grad_both, (((0,), (0,)), ((),...  99.8 us
    all_gather x1, waiting for transfers between devices, per_device(): full_weights = lax.all_gather(stacked, 'dp', axis=0, tiled=True)  70.5 us
  transfers between devices with their start and end apart: 4, of which 4 were waited for; matrix products, arithmetic and copies ran while one was open for 2% of the time, Pallas kernels for 0%

commit v1 on v0

v1 whole, which is shorter than its diff:
```python
import math

import jax
import jax.numpy as jnp
from jax import lax
from jax.experimental import pallas as pl
from jax.experimental.pallas import tpu as pltpu
from jax.sharding import Mesh, PartitionSpec as P

HD = 128
CLEN = 64
NTOK = 32
SPANS = 4
ROWS = 256
BLOCK = 256
DEPTH = 512
WIDE = 256
PIECES = 8
Z = 16
BF16 = jnp.bfloat16
F32 = jnp.float32
AXES = ("yh", "yl", "xh", "c", "s", "z")
DP = ("yh", "yl", "xh", "c")
HEADS = ("s", "z")
VMEM_LIMIT = 40 * 1024 * 1024


def dot(a, b, contract):
    return lax.dot_general(a, b, ((contract[:1], contract[1:]), ((), ())), preferred_element_type=F32)


def kernel_call(body, out_shape, n_smem, n_vmem, scratch=(), flops=0, bytes_accessed=0):
    smem = pl.BlockSpec(memory_space=pltpu.SMEM)
    vmem = pl.BlockSpec(memory_space=pltpu.VMEM)
    return pl.pallas_call(
        body,
        out_shape=out_shape,
        in_specs=[smem] * n_smem + [vmem] * n_vmem,
        out_specs=jax.tree.map(lambda _: vmem, out_shape),
        scratch_shapes=list(scratch),
        compiler_params=pltpu.CompilerParams(vmem_limit_bytes=VMEM_LIMIT),
        cost_estimate=pl.CostEstimate(
            flops=flops, bytes_accessed=bytes_accessed, transcendentals=0
        ),
    )


def project_body(me, enc, *refs):
    weights, own, other = refs[:PIECES], refs[PIECES], refs[PIECES + 1]
    total = jnp.zeros((ROWS, 2 * WIDE), F32)
    for piece in range(PIECES):
        place = jnp.bitwise_xor(me[0], piece) * 2
        for part in range(2):
            rows = weights[piece][part * BLOCK : (part + 1) * BLOCK, :]
            total = total + dot(enc[place + part], rows, (1, 0))
    own[...] = total[:, :WIDE]
    other[...] = total[:, WIDE:].astype(BF16)


def attention_body(ids, own, arrived, queries, grads, context, grad_queries, grad_kv, kv, forward, back):
    inverse_root = 1.0 / math.sqrt(HD)
    kv[...] = (own[...] + arrived[...].astype(F32)).astype(BF16)
    row = lax.broadcasted_iota(jnp.int32, (ROWS, HD), 0)

    def to_blocks(x):
        shifted = pltpu.roll(x.astype(F32), ROWS - (CLEN - 1), 0)
        return jnp.where(row < ROWS - (CLEN - 1), shifted, 0.0).astype(BF16)

    def from_blocks(x):
        return jnp.where(row >= CLEN - 1, pltpu.roll(x, CLEN - 1, 0), 0.0).astype(BF16)

    query_blocks = to_blocks(queries[...])
    grad_blocks = to_blocks(grads[...])
    for span in range(SPANS):
        starts = [pl.multiple_of(ids[0, span * 2 + j] * NTOK, NTOK) for j in range(2)]
        taken = jnp.concatenate([kv[pl.ds(start, NTOK), :] for start in starts], axis=0)
        span_keys, span_values = taken[:, :HD], taken[:, HD:]
        q = query_blocks[span * CLEN : (span + 1) * CLEN, :]
        g = grad_blocks[span * CLEN : (span + 1) * CLEN, :]
        exponent = jnp.exp(dot(q, span_keys, (1, 1)) * inverse_root)
        probs = exponent / jnp.sum(exponent, -1, keepdims=True)
        attn = probs.astype(BF16)
        dprob = dot(g, span_values, (1, 1))
        scaled = (
            probs * (dprob - jnp.sum(probs * dprob, -1, keepdims=True)) * inverse_root
        ).astype(BF16)
        forward[span * CLEN : (span + 1) * CLEN, :] = dot(attn, span_values, (1, 0))
        back[span * CLEN : (span + 1) * CLEN, :] = dot(scaled, span_keys, (1, 0))
        grad_rows = jnp.concatenate([dot(scaled, q, (0, 0)), dot(attn, g, (0, 0))], axis=1)
        grad_rows = grad_rows.astype(BF16)
        for j in range(2):
            grad_kv[pl.ds(starts[j], NTOK), :] = grad_rows[j * NTOK : (j + 1) * NTOK, :]
    context[...] = from_blocks(forward[...])
    grad_queries[...] = from_blocks(back[...])


def encoder_grad_body(me, grad_own, grad_other, *refs):
    weights, out = refs[:PIECES], refs[PIECES]
    grad = jnp.concatenate([grad_own[...], grad_other[...]], axis=1)
    for piece in range(PIECES):
        place = jnp.bitwise_xor(me[0], piece) * 2
        for part in range(2):
            rows = weights[piece][part * BLOCK : (part + 1) * BLOCK, :]
            out[place + part] = dot(grad, rows, (1, 1)).astype(BF16)


def weight_grad_body(me, enc, grad_own, grad_other, *outs):
    grad = jnp.concatenate([grad_own[...], grad_other[...]], axis=1)
    for piece in range(PIECES):
        place = jnp.bitwise_xor(me[0], piece) * 2
        for part in range(2):
            outs[piece][part * BLOCK : (part + 1) * BLOCK, :] = dot(
                enc[place + part], grad, (0, 0)
            ).astype(BF16)


def swap(x, axis):
    return lax.ppermute(x, axis, [(0, 1), (1, 0)])


def at(y, s):
    return y * 2 + s


FIRST = [(at(y, y // 2), at(3 - y, y // 2)) for y in range(4)] + [
    (at(y, 1 - y // 2), at(y, y // 2)) for y in range(4)
]
SECOND = [(at(y, 1 - y // 2), at(3 - y, y // 2)) for y in range(4)]
YS = ("yh", "yl", "s")


def reverse(pairs):
    return [(b, a) for a, b in pairs]


def diagonal(x):
    return lax.ppermute(x, ("yl", "xh"), [(i, 3 - i) for i in range(4)])


def per_device(queries, encoded, neighbour_ids, key_weight, value_weight, grad_context):
    enc = lax.all_gather(encoded[0], "z", axis=0, tiled=False)

    home = lax.axis_index("yh") == lax.axis_index("s")
    low = jnp.where(home, lax.axis_index("yl"), 1 - lax.axis_index("yl"))
    me = (low * 4 + lax.axis_index("xh") * 2 + lax.axis_index("c")).astype(jnp.int32).reshape(1)

    stacked = jnp.concatenate([key_weight, value_weight], axis=1)
    first = lax.ppermute(stacked, YS, FIRST)
    second = lax.ppermute(stacked, YS, SECOND)
    mine = jnp.concatenate(
        [jnp.where(home, stacked, first), jnp.where(home, first, second)], axis=1
    )
    gathered = [mine, swap(mine, "xh"), swap(mine, "yl"), diagonal(mine)]
    weights = []
    for piece in gathered:
        weights += [piece, swap(piece, "c")]

    half_flops = 2 * ROWS * (PIECES * DEPTH) * (2 * WIDE)
    half_bytes = 2 * (Z * ROWS * BLOCK + PIECES * DEPTH * 2 * WIDE)
    tile = jax.ShapeDtypeStruct((ROWS, WIDE), BF16)
    own, other = kernel_call(
        project_body,
        (jax.ShapeDtypeStruct((ROWS, WIDE), F32), tile),
        1,
        1 + PIECES,
        flops=half_flops,
        bytes_accessed=half_bytes,
    )(me, enc, *weights)
    arrived = swap(other, "s")

    head = jax.ShapeDtypeStruct((ROWS, HD), BF16)
    context, grad_queries, grad_own = kernel_call(
        attention_body,
        (head, head, tile),
        1,
        4,
        scratch=(
            pltpu.VMEM((ROWS, WIDE), BF16),
            pltpu.VMEM((ROWS, HD), F32),
            pltpu.VMEM((ROWS, HD), F32),
        ),
        flops=2 * ROWS * CLEN * HD * 6,
        bytes_accessed=1 << 20,
    )(neighbour_ids, own, arrived, queries[0], grad_context[0])
    grad_other = swap(grad_own, "s")

    enc_terms = kernel_call(
        encoder_grad_body,
        jax.ShapeDtypeStruct((Z, ROWS, BLOCK), BF16),
        1,
        2 + PIECES,
        flops=half_flops,
        bytes_accessed=half_bytes,
    )(me, grad_own, grad_other, *weights)
    grad_encoded = lax.psum_scatter(enc_terms, "z", scatter_dimension=0, tiled=False)

    terms = kernel_call(
        weight_grad_body,
        (jax.ShapeDtypeStruct((DEPTH, 2 * WIDE), BF16),) * PIECES,
        1,
        3,
        flops=half_flops,
        bytes_accessed=half_bytes,
    )(me, enc, grad_own, grad_other)

    def add(*parts):
        total = parts[0].astype(F32)
        for part in parts[1:]:
            total = total + part.astype(F32)
        return total.astype(BF16)

    pairs = [add(terms[2 * i], swap(terms[2 * i + 1], "c")) for i in range(4)]
    mine = add(pairs[0], swap(pairs[1], "xh"), swap(pairs[2], "yl"), diagonal(pairs[3]))
    for_same, for_other = mine[:, :WIDE], mine[:, WIDE:]
    first = lax.ppermute(jnp.where(home, for_other, for_same), YS, reverse(FIRST))
    second = lax.ppermute(for_other, YS, reverse(SECOND))
    weight_grad = add(jnp.where(home, for_same, second), first)
    return (
        context[None],
        grad_queries[None],
        grad_encoded[None],
        weight_grad[:, :HD],
        weight_grad[:, HD:],
    )


def solution(mesh):
    grid = Mesh(mesh.devices.reshape(2, 2, 2, 2, 2, Z), AXES)
    return jax.shard_map(
        per_device,
        mesh=grid,
        in_specs=(
            P(DP, None, HEADS),
            P(DP, None, HEADS),
            P(DP, None),
            P(DP, HEADS),
            P(DP, HEADS),
            P(DP, None, HEADS),
        ),
        out_specs=(
            P(DP, None, HEADS),
            P(DP, None, HEADS),
            P(DP, None, HEADS),
            P(DP, HEADS),
            P(DP, HEADS),
        ),
        check_vma=False,
    )
```

time: 623 us -> 190 us (0.30)
  waiting for transfers between devices: 577 us -> 101 us
  starting transfers between devices: 0.16 us -> 57.1 us
  matrix products: 16.9 us -> 0 us
  Pallas kernels: 0 us -> 10.3 us
    psum x1 -> x0, waiting for transfers between devices: 262 us -> none  [per_device(): lax.psum(partial_grad.astype(jnp.bfloat16), ('segment', 'tensor'))]
    all_gather x2 -> x1, waiting for transfers between devices: 214 us -> 25.2 us  [per_device(): enc = lax.all_gather(encoded[0], 'z', axis=0, tiled=False)]
    reduce_scatter x1, waiting for transfers between devices: 99.8 us -> 14.3 us  [per_device(): lax.psum_scatter(enc_terms, 'z', scatter_dimension=0, tiled=False)]
    ppermute x0 -> x20, waiting for transfers between devices: none -> 60.5 us  [the longest x14 36.6 us: swap(): return lax.ppermute(x, axis, [(0, 1), (1, 0)])]
    ppermute x0 -> x20, starting transfers between devices: none -> 57 us  [the longest x14 37.1 us: swap(): return lax.ppermute(x, axis, [(0, 1), (1, 0)])]
    dot_general x9 -> x0, matrix products: 16.7 us -> none  [the longest x1 5.45 us: per_device(): lax.dot_general(grad_both, full_weights, (((1,), (1,)), ((), ())), prefer...]
    pallas_call x0 -> x4, Pallas kernels: none -> 10.3 us  [the longest x1 3.82 us: per_device(): kernel_call(encoder_grad_body, jax.ShapeDtypeStruct((Z, ROWS, BLOCK), BF1...]
  transfers between devices with their start and end apart: 4 -> 22, of which waited for: 4 -> 13; matrix products, arithmetic and copies ran while one was open for 2% -> 2% of each run, Pallas kernels for 0% -> 1%
where the time goes in v1:
time: 190 us; the launch traced here: 189 us
  waiting for transfers between devices  101 us (53%)
  starting transfers between devices  57.1 us (30%)
  between operations  14.4 us (8%)
  Pallas kernels  10.3 us (5%)
  local copies, waits for them, and re-layouts  5.75 us (3%)
    ppermute x14, starting transfers between devices, swap(): return lax.ppermute(x, axis, [(0, 1), (1, 0)])  37.1 us
    ppermute x14, waiting for transfers between devices, swap(): return lax.ppermute(x, axis, [(0, 1), (1, 0)])  36.6 us
    all_gather x1, waiting for transfers between devices, per_device(): enc = lax.all_gather(encoded[0], 'z', axis=0, tiled=False)  25.2 us
    reduce_scatter x1, waiting for transfers between devices, per_device(): lax.psum_scatter(enc_terms, 'z', scatter_dimension=0, tiled=False)  14.3 us
    ppermute x2, starting transfers between devices, diagonal(): return lax.ppermute(x, ('yl', 'xh'), [(i, 3 - i) for i in range(4)])  6.96 us
    ppermute x2, waiting for transfers between devices, diagonal(): return lax.ppermute(x, ('yl', 'xh'), [(i, 3 - i) for i in range(4)])  6.52 us
    ppermute x1, waiting for transfers between devices, per_device(): second = lax.ppermute(stacked, YS, SECOND)  6.06 us
    ppermute x1, starting transfers between devices, per_device(): second = lax.ppermute(stacked, YS, SECOND)  5.19 us
  transfers between devices with their start and end apart: 22, of which 13 were waited for; matrix products, arithmetic and copies ran while one was open for 2% of the time, Pallas kernels for 1%

profile of v1, /device:TPU:6, one launch (start us, length us, event | category | flops | bytes accessed | tf_op | source)
XLA Modules:
  0.0 189.2 jit_solution(10636090744788799439)
XLA Ops:
  7.2 0.7 all-gather.2.cloned.1.call-update
  7.9 0.9 constant_dynamic-update-slice_fusion.1
  8.9 0.9 constant_dynamic-update-slice_fusion
  9.8 5.2 %collective-permute-start.1 = (bf16[512,256]{1,0:T(8,128)(2,1)S(1)}, bf16[512,256]{1,0:T(8,128)(2,1)S(1)}, u32[]{:S(2)}, u32[]{:S(2)}) collective-permute-start(bf16[512,256]{1,0:T(8,128)(2,1)S(1)} %constant_dynamic-update-slice_fusion), channel_id=1, source_target_pairs={{16,384},{144,256},{256,144},{384,16},{17,385},{145,257},{257,145}... | collective-permute-start | bytes 786440 | tf_op jit(solution)/shard_map/ppermute | solution.py:149
  15.0 1.9 %collective-permute-start = (bf16[512,256]{1,0:T(8,128)(2,1)S(1)}, bf16[512,256]{1,0:T(8,128)(2,1)S(1)}, u32[]{:S(2)}, u32[]{:S(2)}) collective-permute-start(bf16[512,256]{1,0:T(8,128)(2,1)S(1)} %constant_dynamic-update-slice_fusion), channel_id=1, source_target_pairs={{0,384},{128,256},{272,144},{400,16},{16,0},{144,128},{256,272},{3... | collective-permute-start | bytes 786440 | tf_op jit(solution)/shard_map/ppermute | solution.py:148
  16.9 6.1 %collective-permute-done.1 = bf16[512,256]{1,0:T(8,128)(2,1)S(1)} collective-permute-done((bf16[512,256]{1,0:T(8,128)(2,1)S(1)}, bf16[512,256]{1,0:T(8,128)(2,1)S(1)}, u32[]{:S(2)}, u32[]{:S(2)}) %collective-permute-start.1) | collective-permute-done | bytes 262176 | tf_op jit(solution)/shard_map/ppermute | solution.py:149
  23.0 4.5 %collective-permute-done = bf16[512,256]{1,0:T(8,128)(2,1)S(1)} collective-permute-done((bf16[512,256]{1,0:T(8,128)(2,1)S(1)}, bf16[512,256]{1,0:T(8,128)(2,1)S(1)}, u32[]{:S(2)}, u32[]{:S(2)}) %collective-permute-start) | collective-permute-done | bytes 262176 | tf_op jit(solution)/shard_map/ppermute | solution.py:148
  27.6 3.1 %collective-permute-start.7 = (bf16[512,512]{1,0:T(8,128)(2,1)S(1)}, bf16[512,512]{1,0:T(8,128)(2,1)S(1)}, u32[]{:S(2)}, u32[]{:S(2)}) collective-permute-start(bf16[512,512]{1,0:T(8,128)(2,1)S(1)} %pad_maximum_fusion.refs_0_), channel_id=1, source_target_pairs={{0,192},{64,128},{128,64},{192,0},{1,193},{65,129},{129,65},{193,1... | collective-permute-start | bytes 1572872 | tf_op jit(solution)/shard_map/ppermute | solution.py:137
  30.7 3.6 %collective-permute-start.5 = (bf16[512,512]{1,0:T(8,128)(2,1)S(1)}, bf16[512,512]{1,0:T(8,128)(2,1)S(1)}, u32[]{:S(2)}, u32[]{:S(2)}) collective-permute-start(bf16[512,512]{1,0:T(8,128)(2,1)S(1)} %pad_maximum_fusion.refs_0_), channel_id=1, source_target_pairs={{0,128},{128,0},{1,129},{129,1},{2,130},{130,2},{3,131},{131,3},{4... | collective-permute-start | bytes 1572872 | tf_op jit(solution)/shard_map/ppermute | solution.py:118
  34.3 4.0 %collective-permute-start.3 = (bf16[512,512]{1,0:T(8,128)(2,1)S(1)}, bf16[512,512]{1,0:T(8,128)(2,1)S(1)}, u32[]{:S(2)}, u32[]{:S(2)}) collective-permute-start(bf16[512,512]{1,0:T(8,128)(2,1)S(1)} %pad_maximum_fusion.refs_0_), channel_id=1, source_target_pairs={{0,64},{64,0},{1,65},{65,1},{2,66},{66,2},{3,67},{67,3},{4,68},{68... | collective-permute-start | bytes 1572872 | tf_op jit(solution)/shard_map/ppermute | solution.py:118
  38.3 1.9 %collective-permute-start.2 = (bf16[512,512]{1,0:T(8,128)(2,1)S(1)}, bf16[512,512]{1,0:T(8,128)(2,1)S(1)}, u32[]{:S(2)}, u32[]{:S(2)}) collective-permute-start(bf16[512,512]{1,0:T(8,128)(2,1)S(1)} %pad_maximum_fusion.refs_0_), channel_id=1, source_target_pairs={{0,32},{32,0},{1,33},{33,1},{2,34},{34,2},{3,35},{35,3},{4,36},{36... | collective-permute-start | bytes 1572872 | tf_op jit(solution)/shard_map/ppermute | solution.py:118
  40.2 6.5 %collective-permute-done.7.refs_6_ = bf16[512,512]{1,0:T(8,128)(2,1)S(1)} collective-permute-done((bf16[512,512]{1,0:T(8,128)(2,1)S(1)}, bf16[512,512]{1,0:T(8,128)(2,1)S(1)}, u32[]{:S(2)}, u32[]{:S(2)}) %collective-permute-start.7) | collective-permute-done | bytes 524320 | tf_op jit(solution)/shard_map/ppermute | solution.py:137
  46.8 1.9 %collective-permute-start.8 = (bf16[512,512]{1,0:T(8,128)(2,1)S(1)}, bf16[512,512]{1,0:T(8,128)(2,1)S(1)}, u32[]{:S(2)}, u32[]{:S(2)}) collective-permute-start(bf16[512,512]{1,0:T(8,128)(2,1)S(1)} %collective-permute-done.7.refs_6_), channel_id=1, source_target_pairs={{0,32},{32,0},{1,33},{33,1},{2,34},{34,2},{3,35},{35,3},{4,36},{36... | collective-permute-start | bytes 1572872 | tf_op jit(solution)/shard_map/ppermute | solution.py:118
  48.7 7.8 %collective-permute-done.5.refs_4_ = bf16[512,512]{1,0:T(8,128)(2,1)S(1)} collective-permute-done((bf16[512,512]{1,0:T(8,128)(2,1)S(1)}, bf16[512,512]{1,0:T(8,128)(2,1)S(1)}, u32[]{:S(2)}, u32[]{:S(2)}) %collective-permute-start.5) | collective-permute-done | bytes 524320 | tf_op jit(solution)/shard_map/ppermute | solution.py:118
  56.5 1.9 %collective-permute-start.6 = (bf16[512,512]{1,0:T(8,128)(2,1)S(1)}, bf16[512,512]{1,0:T(8,128)(2,1)}, u32[]{:S(2)}, u32[]{:S(2)}) collective-permute-start(bf16[512,512]{1,0:T(8,128)(2,1)S(1)} %collective-permute-done.5.refs_4_), channel_id=1, source_target_pairs={{0,32},{32,0},{1,33},{33,1},{2,34},{34,2},{3,35},{35,3},{4,36},{36... | collective-permute-start | bytes 1572872 | tf_op jit(solution)/shard_map/ppermute | solution.py:118
  58.4 2.4 %collective-permute-start.4 = (bf16[512,512]{1,0:T(8,128)(2,1)S(1)}, bf16[512,512]{1,0:T(8,128)(2,1)}, u32[]{:S(2)}, u32[]{:S(2)}) collective-permute-start(bf16[512,512]{1,0:T(8,128)(2,1)S(1)} %collective-permute-done.3.refs_2_), channel_id=1, source_target_pairs={{0,32},{32,0},{1,33},{33,1},{2,34},{34,2},{3,35},{35,3},{4,36},{36... | collective-permute-start | bytes 1572872 | tf_op jit(solution)/shard_map/ppermute | solution.py:118
  60.9 1.6 collective-permute-done.4.refs_3_
  62.5 25.2 %all-gather.2.cloned.1.call-done.enc = bf16[16,256,256]{2,1,0:T(8,128)(2,1)} async-done(((bf16[1,256,256]{2,1,0:T(8,128)(2,1)}), bf16[16,256,256]{2,1,0:T(8,128)(2,1)}) %all-gather.2.cloned.1.call-update) | async-done | bytes 2097168 | tf_op jit(solution)/shard_map/all_gather | solution.py:141
  87.8 1.6 copy-done
  89.4 2.5 %shard_map.101 = (f32[256,256]{1,0:T(8,128)S(1)}, bf16[256,256]{1,0:T(8,128)(2,1)S(1)}) custom-call(s32[1]{0:T(128)} %bitcast.me, bf16[16,256,256]{2,1,0:T(8,128)(2,1)S(1)} %copy-done, bf16[512,512]{1,0:T(8,128)(2,1)S(1)} %pad_maximum_fusion.refs_0_, bf16[512,512]{1,0:T(8,128)(2,1)S(1)} %collective-permute-done.2.refs_1_, ...), custom_call_target="tpu_custom_call" | custom-call | flops 1073741824 | bytes 6291456 | tf_op jit(solution)/shard_map/pallas_call | solution.py:161
  91.8 2.9 %collective-permute-start.9 = (bf16[256,256]{1,0:T(8,128)(2,1)S(1)}, bf16[256,256]{1,0:T(8,128)(2,1)S(1)}, u32[]{:S(2)}, u32[]{:S(2)}) collective-permute-start(bf16[256,256]{1,0:T(8,128)(2,1)S(1)} %get-tuple-element.19), channel_id=1, source_target_pairs={{0,16},{16,0},{1,17},{17,1},{2,18},{18,2},{3,19},{19,3},{4,20},{20... | collective-permute-start | bytes 393224 | tf_op jit(solution)/shard_map/ppermute | solution.py:118
  94.8 3.9 %collective-permute-done.9.arrived = bf16[256,256]{1,0:T(8,128)(2,1)S(1)} collective-permute-done((bf16[256,256]{1,0:T(8,128)(2,1)S(1)}, bf16[256,256]{1,0:T(8,128)(2,1)S(1)}, u32[]{:S(2)}, u32[]{:S(2)}) %collective-permute-start.9) | collective-permute-done | bytes 131104 | tf_op jit(solution)/shard_map/ppermute | solution.py:118
  98.7 2.7 %shard_map.102 = (bf16[256,128]{1,0:T(8,128)(2,1)}, bf16[256,128]{1,0:T(8,128)(2,1)}, bf16[256,256]{1,0:T(8,128)(2,1)S(1)}) custom-call(s32[1,8]{1,0:T(1,128)S(1)} %copy-done.4, f32[256,256]{1,0:T(8,128)S(1)} %get-tuple-element.18.own, bf16[256,256]{1,0:T(8,128)(2,1)S(1)} %collective-permute-done.9.arrived, bf16[256,128]{1,0:T(8,128)(2,1)S(1)} %bitcast.5, ...), custom_call_target="tpu_custom_call" | custom-call | flops 25165824 | bytes 1048576 | tf_op jit(solution)/shard_map/pallas_call | solution.py:172
  101.4 2.9 %collective-permute-start.10 = (bf16[256,256]{1,0:T(8,128)(2,1)S(1)}, bf16[256,256]{1,0:T(8,128)(2,1)S(1)}, u32[]{:S(2)}, u32[]{:S(2)}) collective-permute-start(bf16[256,256]{1,0:T(8,128)(2,1)S(1)} %get-tuple-element.22.grad_own), channel_id=1, source_target_pairs={{0,16},{16,0},{1,17},{17,1},{2,18},{18,2},{3,19},{19,3},{4,20},{20... | collective-permute-start | bytes 393224 | tf_op jit(solution)/shard_map/ppermute | solution.py:118
  104.3 3.9 %collective-permute-done.10.grad_other = bf16[256,256]{1,0:T(8,128)(2,1)S(1)} collective-permute-done((bf16[256,256]{1,0:T(8,128)(2,1)S(1)}, bf16[256,256]{1,0:T(8,128)(2,1)S(1)}, u32[]{:S(2)}, u32[]{:S(2)}) %collective-permute-start.10) | collective-permute-done | bytes 131104 | tf_op jit(solution)/shard_map/ppermute | solution.py:118
  108.3 3.8 %shard_map.103 = bf16[16,256,256]{2,1,0:T(8,128)(2,1)} custom-call(s32[1]{0:T(128)} %bitcast.me, bf16[256,256]{1,0:T(8,128)(2,1)S(1)} %get-tuple-element.22.grad_own, bf16[256,256]{1,0:T(8,128)(2,1)S(1)} %collective-permute-done.10.grad_other, bf16[512,512]{1,0:T(8,128)(2,1)S(1)} %pad_maximum_fusion.refs_0_, ...), custom_call_target="tpu_custom_call" | custom-call | flops 1073741824 | bytes 6291456 | tf_op jit(solution)/shard_map/pallas_call | solution.py:187
  112.1 1.6 copy-done.1
  113.7 1.3 shard_map.104
  115.0 1.9 %collective-permute-start.12 = (bf16[512,512]{1,0:T(8,128)(2,1)S(1)}, bf16[512,512]{1,0:T(8,128)(2,1)S(1)}, u32[]{:S(2)}, u32[]{:S(2)}) collective-permute-start(bf16[512,512]{1,0:T(8,128)(2,1)S(1)} %get-tuple-element.26), channel_id=1, source_target_pairs={{0,32},{32,0},{1,33},{33,1},{2,34},{34,2},{3,35},{35,3},{4,36},{36... | collective-permute-start | bytes 1572872 | tf_op jit(solution)/shard_map/ppermute | solution.py:118
  116.9 2.4 %collective-permute-start.14 = (bf16[512,512]{1,0:T(8,128)(2,1)S(1)}, bf16[512,512]{1,0:T(8,128)(2,1)S(1)}, u32[]{:S(2)}, u32[]{:S(2)}) collective-permute-start(bf16[512,512]{1,0:T(8,128)(2,1)S(1)} %get-tuple-element.28), channel_id=1, source_target_pairs={{0,32},{32,0},{1,33},{33,1},{2,34},{34,2},{3,35},{35,3},{4,36},{36... | collective-permute-start | bytes 1572872 | tf_op jit(solution)/shard_map/ppermute | solution.py:118
  119.3 1.9 %collective-permute-start.11 = (bf16[512,512]{1,0:T(8,128)(2,1)S(1)}, bf16[512,512]{1,0:T(8,128)(2,1)S(1)}, u32[]{:S(2)}, u32[]{:S(2)}) collective-permute-start(bf16[512,512]{1,0:T(8,128)(2,1)S(1)} %get-tuple-element.24), channel_id=1, source_target_pairs={{0,32},{32,0},{1,33},{33,1},{2,34},{34,2},{3,35},{35,3},{4,36},{36... | collective-permute-start | bytes 1572872 | tf_op jit(solution)/shard_map/ppermute | solution.py:118
  121.2 2.4 %collective-permute-start.16 = (bf16[512,512]{1,0:T(8,128)(2,1)S(1)}, bf16[512,512]{1,0:T(8,128)(2,1)S(1)}, u32[]{:S(2)}, u32[]{:S(2)}) collective-permute-start(bf16[512,512]{1,0:T(8,128)(2,1)S(1)} %get-tuple-element.30), channel_id=1, source_target_pairs={{0,32},{32,0},{1,33},{33,1},{2,34},{34,2},{3,35},{35,3},{4,36},{36... | collective-permute-start | bytes 1572872 | tf_op jit(solution)/shard_map/ppermute | solution.py:118
  123.7 0.1 add_convert_fusion.3
  123.8 3.5 %collective-permute-start.13 = (bf16[512,512]{1,0:T(8,128)(2,1)S(1)}, bf16[512,512]{1,0:T(8,128)(2,1)S(1)}, u32[]{:S(2)}, u32[]{:S(2)}) collective-permute-start(bf16[512,512]{1,0:T(8,128)(2,1)S(1)} %add_convert_fusion.3), channel_id=1, source_target_pairs={{0,64},{64,0},{1,65},{65,1},{2,66},{66,2},{3,67},{67,3},{4,68},{68... | collective-permute-start | bytes 1572872 | tf_op jit(solution)/shard_map/ppermute | solution.py:118
  127.4 0.1 add_convert_fusion.2
  127.5 3.3 %collective-permute-start.15 = (bf16[512,512]{1,0:T(8,128)(2,1)S(1)}, bf16[512,512]{1,0:T(8,128)(2,1)S(1)}, u32[]{:S(2)}, u32[]{:S(2)}) collective-permute-start(bf16[512,512]{1,0:T(8,128)(2,1)S(1)} %add_convert_fusion.2), channel_id=1, source_target_pairs={{0,128},{128,0},{1,129},{129,1},{2,130},{130,2},{3,131},{131,3},{4... | collective-permute-start | bytes 1572872 | tf_op jit(solution)/shard_map/ppermute | solution.py:118
  130.9 0.1 add_convert_fusion.1
  131.0 3.8 %collective-permute-start.17 = (bf16[512,512]{1,0:T(8,128)(2,1)S(1)}, bf16[512,512]{1,0:T(8,128)(2,1)S(1)}, u32[]{:S(2)}, u32[]{:S(2)}) collective-permute-start(bf16[512,512]{1,0:T(8,128)(2,1)S(1)} %add_convert_fusion.1), channel_id=1, source_target_pairs={{0,192},{64,128},{128,64},{192,0},{1,193},{65,129},{129,65},{193,1... | collective-permute-start | bytes 1572872 | tf_op jit(solution)/shard_map/ppermute | solution.py:137
  134.9 7.1 %collective-permute-done.13 = bf16[512,512]{1,0:T(8,128)(2,1)S(1)} collective-permute-done((bf16[512,512]{1,0:T(8,128)(2,1)S(1)}, bf16[512,512]{1,0:T(8,128)(2,1)S(1)}, u32[]{:S(2)}, u32[]{:S(2)}) %collective-permute-start.13) | collective-permute-done | bytes 524320 | tf_op jit(solution)/shard_map/ppermute | solution.py:118
  142.0 12.2 %collective-permute-done.15 = bf16[512,512]{1,0:T(8,128)(2,1)S(1)} collective-permute-done((bf16[512,512]{1,0:T(8,128)(2,1)S(1)}, bf16[512,512]{1,0:T(8,128)(2,1)S(1)}, u32[]{:S(2)}, u32[]{:S(2)}) %collective-permute-start.15) | collective-permute-done | bytes 524320 | tf_op jit(solution)/shard_map/ppermute | solution.py:118
  154.2 0.3 add_convert_fusion
  154.6 3.9 %collective-permute-start.18 = (bf16[512,256]{1,0:T(8,128)(2,1)S(1)}, bf16[512,256]{1,0:T(8,128)(2,1)S(1)}, u32[]{:S(2)}, u32[]{:S(2)}) collective-permute-start(bf16[512,256]{1,0:T(8,128)(2,1)S(1)} %get-tuple-element.31), channel_id=1, source_target_pairs={{384,16},{256,144},{144,256},{16,384},{385,17},{257,145},{145,257}... | collective-permute-start | bytes 786440 | tf_op jit(solution)/shard_map/ppermute | solution.py:216
  158.5 1.9 %collective-permute-start.19 = (bf16[512,256]{1,0:T(8,128)(2,1)S(1)}, bf16[512,256]{1,0:T(8,128)(2,1)S(1)}, u32[]{:S(2)}, u32[]{:S(2)}) collective-permute-start(bf16[512,256]{1,0:T(8,128)(2,1)S(1)} %get-tuple-element.32), channel_id=1, source_target_pairs={{384,0},{256,128},{144,272},{16,400},{0,16},{128,144},{272,256},{4... | collective-permute-start | bytes 786440 | tf_op jit(solution)/shard_map/ppermute | solution.py:215
  160.5 4.9 %collective-permute-done.18 = bf16[512,256]{1,0:T(8,128)(2,1)S(1)} collective-permute-done((bf16[512,256]{1,0:T(8,128)(2,1)S(1)}, bf16[512,256]{1,0:T(8,128)(2,1)S(1)}, u32[]{:S(2)}, u32[]{:S(2)}) %collective-permute-start.18) | collective-permute-done | bytes 262176 | tf_op jit(solution)/shard_map/ppermute | solution.py:216
  165.4 1.9 collective-permute-done.19
  167.3 0.1 add_convert_fusion.5
  167.4 0.7 fusion.1
  168.1 14.3 %reduce-scatter.2.cloned.1.call-done = bf16[1,256,256]{2,1,0:T(8,128)(2,1)} async-done(((bf16[16,256,256]{2,1,0:T(8,128)(2,1)}), bf16[1,256,256]{2,1,0:T(8,128)(2,1)}) %reduce-scatter.2.cloned.1.call-update) | async-done | bytes 131088 | tf_op jit(solution)/shard_map/reduce_scatter | solution.py:195
  (23 shorter events, 0.2 us)
Async XLA Ops:
  7.2 80.6 %all-gather.2.cloned.1.call-start = ((), (), s32[]{:S(2)}) async-start(), calls=%async_computation.1 | async-start | bytes 2228224 | tf_op jit(solution)/shard_map/all_gather | solution.py:141
  7.9 174.5 %reduce-scatter.2.cloned.1.call-start = ((), (), s32[]{:S(2)}) async-start(), calls=%async_computation.2 | async-start | bytes 2228224 | tf_op jit(solution)/shard_map/reduce_scatter | solution.py:195
  9.8 13.2 %collective-permute-start.1 = (bf16[512,256]{1,0:T(8,128)(2,1)S(1)}, bf16[512,256]{1,0:T(8,128)(2,1)S(1)}, u32[]{:S(2)}, u32[]{:S(2)}) collective-permute-start(bf16[512,256]{1,0:T(8,128)(2,1)S(1)} %constant_dynamic-update-slice_fusion), channel_id=1, source_target_pairs={{16,384},{144,256},{256,144},{384,16},{17,385},{145,257},{257,145}... | collective-permute-start | bytes 786440 | tf_op jit(solution)/shard_map/ppermute | solution.py:149
  15.0 12.5 %collective-permute-start = (bf16[512,256]{1,0:T(8,128)(2,1)S(1)}, bf16[512,256]{1,0:T(8,128)(2,1)S(1)}, u32[]{:S(2)}, u32[]{:S(2)}) collective-permute-start(bf16[512,256]{1,0:T(8,128)(2,1)S(1)} %constant_dynamic-update-slice_fusion), channel_id=1, source_target_pairs={{0,384},{128,256},{272,144},{400,16},{16,0},{144,128},{256,272},{3... | collective-permute-start | bytes 786440 | tf_op jit(solution)/shard_map/ppermute | solution.py:148
  27.6 19.2 %collective-permute-start.7 = (bf16[512,512]{1,0:T(8,128)(2,1)S(1)}, bf16[512,512]{1,0:T(8,128)(2,1)S(1)}, u32[]{:S(2)}, u32[]{:S(2)}) collective-permute-start(bf16[512,512]{1,0:T(8,128)(2,1)S(1)} %pad_maximum_fusion.refs_0_), channel_id=1, source_target_pairs={{0,192},{64,128},{128,64},{192,0},{1,193},{65,129},{129,65},{193,1... | collective-permute-start | bytes 1572872 | tf_op jit(solution)/shard_map/ppermute | solution.py:137
  30.7 25.8 %collective-permute-start.5 = (bf16[512,512]{1,0:T(8,128)(2,1)S(1)}, bf16[512,512]{1,0:T(8,128)(2,1)S(1)}, u32[]{:S(2)}, u32[]{:S(2)}) collective-permute-start(bf16[512,512]{1,0:T(8,128)(2,1)S(1)} %pad_maximum_fusion.refs_0_), channel_id=1, source_target_pairs={{0,128},{128,0},{1,129},{129,1},{2,130},{130,2},{3,131},{131,3},{4... | collective-permute-start | bytes 1572872 | tf_op jit(solution)/shard_map/ppermute | solution.py:118
  34.3 24.2 %collective-permute-start.3 = (bf16[512,512]{1,0:T(8,128)(2,1)S(1)}, bf16[512,512]{1,0:T(8,128)(2,1)S(1)}, u32[]{:S(2)}, u32[]{:S(2)}) collective-permute-start(bf16[512,512]{1,0:T(8,128)(2,1)S(1)} %pad_maximum_fusion.refs_0_), channel_id=1, source_target_pairs={{0,64},{64,0},{1,65},{65,1},{2,66},{66,2},{3,67},{67,3},{4,68},{68... | collective-permute-start | bytes 1572872 | tf_op jit(solution)/shard_map/ppermute | solution.py:118
  38.3 22.6 %collective-permute-start.2 = (bf16[512,512]{1,0:T(8,128)(2,1)S(1)}, bf16[512,512]{1,0:T(8,128)(2,1)S(1)}, u32[]{:S(2)}, u32[]{:S(2)}) collective-permute-start(bf16[512,512]{1,0:T(8,128)(2,1)S(1)} %pad_maximum_fusion.refs_0_), channel_id=1, source_target_pairs={{0,32},{32,0},{1,33},{33,1},{2,34},{34,2},{3,35},{35,3},{4,36},{36... | collective-permute-start | bytes 1572872 | tf_op jit(solution)/shard_map/ppermute | solution.py:118
  46.8 14.1 %collective-permute-start.8 = (bf16[512,512]{1,0:T(8,128)(2,1)S(1)}, bf16[512,512]{1,0:T(8,128)(2,1)S(1)}, u32[]{:S(2)}, u32[]{:S(2)}) collective-permute-start(bf16[512,512]{1,0:T(8,128)(2,1)S(1)} %collective-permute-done.7.refs_6_), channel_id=1, source_target_pairs={{0,32},{32,0},{1,33},{33,1},{2,34},{34,2},{3,35},{35,3},{4,36},{36... | collective-permute-start | bytes 1572872 | tf_op jit(solution)/shard_map/ppermute | solution.py:118
  56.5 4.4 %collective-permute-start.6 = (bf16[512,512]{1,0:T(8,128)(2,1)S(1)}, bf16[512,512]{1,0:T(8,128)(2,1)}, u32[]{:S(2)}, u32[]{:S(2)}) collective-permute-start(bf16[512,512]{1,0:T(8,128)(2,1)S(1)} %collective-permute-done.5.refs_4_), channel_id=1, source_target_pairs={{0,32},{32,0},{1,33},{33,1},{2,34},{34,2},{3,35},{35,3},{4,36},{36... | collective-permute-start | bytes 1572872 | tf_op jit(solution)/shard_map/ppermute | solution.py:118
  58.4 4.1 %collective-permute-start.4 = (bf16[512,512]{1,0:T(8,128)(2,1)S(1)}, bf16[512,512]{1,0:T(8,128)(2,1)}, u32[]{:S(2)}, u32[]{:S(2)}) collective-permute-start(bf16[512,512]{1,0:T(8,128)(2,1)S(1)} %collective-permute-done.3.refs_2_), channel_id=1, source_target_pairs={{0,32},{32,0},{1,33},{33,1},{2,34},{34,2},{3,35},{35,3},{4,36},{36... | collective-permute-start | bytes 1572872 | tf_op jit(solution)/shard_map/ppermute | solution.py:118
  87.8 1.6 copy-start
  89.3 9.4 %copy-start.2 = (bf16[1,256,128]{2,1,0:T(8,128)(2,1)S(1)}, bf16[1,256,128]{2,1,0:T(8,128)(2,1)}, u32[]{:S(2)}) copy-start(bf16[1,256,128]{2,1,0:T(8,128)(2,1)} %param.6) | copy-start | bytes 196612
  89.3 9.4 %copy-start.3 = (bf16[1,256,128]{2,1,0:T(8,128)(2,1)S(1)}, bf16[1,256,128]{2,1,0:T(8,128)(2,1)}, u32[]{:S(2)}) copy-start(bf16[1,256,128]{2,1,0:T(8,128)(2,1)} %param.11) | copy-start | bytes 196612
  89.3 9.4 %copy-start.4 = (s32[1,8]{1,0:T(1,128)S(1)}, s32[1,8]{1,0:T(1,128)}, u32[]{:S(2)}) copy-start(s32[1,8]{1,0:T(1,128)} %ids.1) | copy-start | bytes 100
  91.8 6.9 %collective-permute-start.9 = (bf16[256,256]{1,0:T(8,128)(2,1)S(1)}, bf16[256,256]{1,0:T(8,128)(2,1)S(1)}, u32[]{:S(2)}, u32[]{:S(2)}) collective-permute-start(bf16[256,256]{1,0:T(8,128)(2,1)S(1)} %get-tuple-element.19), channel_id=1, source_target_pairs={{0,16},{16,0},{1,17},{17,1},{2,18},{18,2},{3,19},{19,3},{4,20},{20... | collective-permute-start | bytes 393224 | tf_op jit(solution)/shard_map/ppermute | solution.py:118
  101.4 6.8 %collective-permute-start.10 = (bf16[256,256]{1,0:T(8,128)(2,1)S(1)}, bf16[256,256]{1,0:T(8,128)(2,1)S(1)}, u32[]{:S(2)}, u32[]{:S(2)}) collective-permute-start(bf16[256,256]{1,0:T(8,128)(2,1)S(1)} %get-tuple-element.22.grad_own), channel_id=1, source_target_pairs={{0,16},{16,0},{1,17},{17,1},{2,18},{18,2},{3,19},{19,3},{4,20},{20... | collective-permute-start | bytes 393224 | tf_op jit(solution)/shard_map/ppermute | solution.py:118
  112.1 1.6 copy-start.1
  115.0 8.7 %collective-permute-start.12 = (bf16[512,512]{1,0:T(8,128)(2,1)S(1)}, bf16[512,512]{1,0:T(8,128)(2,1)S(1)}, u32[]{:S(2)}, u32[]{:S(2)}) collective-permute-start(bf16[512,512]{1,0:T(8,128)(2,1)S(1)} %get-tuple-element.26), channel_id=1, source_target_pairs={{0,32},{32,0},{1,33},{33,1},{2,34},{34,2},{3,35},{35,3},{4,36},{36... | collective-permute-start | bytes 1572872 | tf_op jit(solution)/shard_map/ppermute | solution.py:118
  116.9 10.5 %collective-permute-start.14 = (bf16[512,512]{1,0:T(8,128)(2,1)S(1)}, bf16[512,512]{1,0:T(8,128)(2,1)S(1)}, u32[]{:S(2)}, u32[]{:S(2)}) collective-permute-start(bf16[512,512]{1,0:T(8,128)(2,1)S(1)} %get-tuple-element.28), channel_id=1, source_target_pairs={{0,32},{32,0},{1,33},{33,1},{2,34},{34,2},{3,35},{35,3},{4,36},{36... | collective-permute-start | bytes 1572872 | tf_op jit(solution)/shard_map/ppermute | solution.py:118
  119.3 15.5 %collective-permute-start.11 = (bf16[512,512]{1,0:T(8,128)(2,1)S(1)}, bf16[512,512]{1,0:T(8,128)(2,1)S(1)}, u32[]{:S(2)}, u32[]{:S(2)}) collective-permute-start(bf16[512,512]{1,0:T(8,128)(2,1)S(1)} %get-tuple-element.24), channel_id=1, source_target_pairs={{0,32},{32,0},{1,33},{33,1},{2,34},{34,2},{3,35},{35,3},{4,36},{36... | collective-permute-start | bytes 1572872 | tf_op jit(solution)/shard_map/ppermute | solution.py:118
  121.2 9.6 %collective-permute-start.16 = (bf16[512,512]{1,0:T(8,128)(2,1)S(1)}, bf16[512,512]{1,0:T(8,128)(2,1)S(1)}, u32[]{:S(2)}, u32[]{:S(2)}) collective-permute-start(bf16[512,512]{1,0:T(8,128)(2,1)S(1)} %get-tuple-element.30), channel_id=1, source_target_pairs={{0,32},{32,0},{1,33},{33,1},{2,34},{34,2},{3,35},{35,3},{4,36},{36... | collective-permute-start | bytes 1572872 | tf_op jit(solution)/shard_map/ppermute | solution.py:118
  123.8 18.2 %collective-permute-start.13 = (bf16[512,512]{1,0:T(8,128)(2,1)S(1)}, bf16[512,512]{1,0:T(8,128)(2,1)S(1)}, u32[]{:S(2)}, u32[]{:S(2)}) collective-permute-start(bf16[512,512]{1,0:T(8,128)(2,1)S(1)} %add_convert_fusion.3), channel_id=1, source_target_pairs={{0,64},{64,0},{1,65},{65,1},{2,66},{66,2},{3,67},{67,3},{4,68},{68... | collective-permute-start | bytes 1572872 | tf_op jit(solution)/shard_map/ppermute | solution.py:118
  127.5 26.7 %collective-permute-start.15 = (bf16[512,512]{1,0:T(8,128)(2,1)S(1)}, bf16[512,512]{1,0:T(8,128)(2,1)S(1)}, u32[]{:S(2)}, u32[]{:S(2)}) collective-permute-start(bf16[512,512]{1,0:T(8,128)(2,1)S(1)} %add_convert_fusion.2), channel_id=1, source_target_pairs={{0,128},{128,0},{1,129},{129,1},{2,130},{130,2},{3,131},{131,3},{4... | collective-permute-start | bytes 1572872 | tf_op jit(solution)/shard_map/ppermute | solution.py:118
  131.0 23.2 %collective-permute-start.17 = (bf16[512,512]{1,0:T(8,128)(2,1)S(1)}, bf16[512,512]{1,0:T(8,128)(2,1)S(1)}, u32[]{:S(2)}, u32[]{:S(2)}) collective-permute-start(bf16[512,512]{1,0:T(8,128)(2,1)S(1)} %add_convert_fusion.1), channel_id=1, source_target_pairs={{0,192},{64,128},{128,64},{192,0},{1,193},{65,129},{129,65},{193,1... | collective-permute-start | bytes 1572872 | tf_op jit(solution)/shard_map/ppermute | solution.py:137
  154.6 10.8 %collective-permute-start.18 = (bf16[512,256]{1,0:T(8,128)(2,1)S(1)}, bf16[512,256]{1,0:T(8,128)(2,1)S(1)}, u32[]{:S(2)}, u32[]{:S(2)}) collective-permute-start(bf16[512,256]{1,0:T(8,128)(2,1)S(1)} %get-tuple-element.31), channel_id=1, source_target_pairs={{384,16},{256,144},{144,256},{16,384},{385,17},{257,145},{145,257}... | collective-permute-start | bytes 786440 | tf_op jit(solution)/shard_map/ppermute | solution.py:216
  158.5 8.7 %collective-permute-start.19 = (bf16[512,256]{1,0:T(8,128)(2,1)S(1)}, bf16[512,256]{1,0:T(8,128)(2,1)S(1)}, u32[]{:S(2)}, u32[]{:S(2)}) collective-permute-start(bf16[512,256]{1,0:T(8,128)(2,1)S(1)} %get-tuple-element.32), channel_id=1, source_target_pairs={{384,0},{256,128},{144,272},{16,400},{0,16},{128,144},{272,256},{4... | collective-permute-start | bytes 786440 | tf_op jit(solution)/shard_map/ppermute | solution.py:215
Sparse Core Ops, SparseCore 0:
  10.1 77.6 all-gather.1
  112.2 70.1 reduce-scatter.1

commit v2 on v1

v2 whole, which is shorter than its diff:
```python
import math

import jax
import jax.numpy as jnp
from jax import lax
from jax.experimental import pallas as pl
from jax.experimental.pallas import tpu as pltpu
from jax.sharding import Mesh, PartitionSpec as P

HD = 128
CLEN = 64
NTOK = 32
SPANS = 4
ROWS = 256
BLOCK = 256
WIDE = 256
PIECES = 8
GROUP = 4
BF16 = jnp.bfloat16
F32 = jnp.float32
AXES = ("yh", "yl", "xh", "c", "s", "zr", "z0")
DP = ("yh", "yl", "xh", "c")
HEADS = ("s", "zr", "z0")
SENDERS = ("yh", "yl", "xh")
VMEM_LIMIT = 40 * 1024 * 1024


def dot(a, b, contract):
    return lax.dot_general(a, b, ((contract[:1], contract[1:]), ((), ())), preferred_element_type=F32)


def kernel_call(body, out_shape, n_smem, n_vmem, scratch=(), flops=0, bytes_accessed=0):
    smem = pl.BlockSpec(memory_space=pltpu.SMEM)
    vmem = pl.BlockSpec(memory_space=pltpu.VMEM)
    return pl.pallas_call(
        body,
        out_shape=out_shape,
        in_specs=[smem] * n_smem + [vmem] * n_vmem,
        out_specs=jax.tree.map(lambda _: vmem, out_shape),
        scratch_shapes=list(scratch),
        compiler_params=pltpu.CompilerParams(vmem_limit_bytes=VMEM_LIMIT),
        cost_estimate=pl.CostEstimate(
            flops=flops, bytes_accessed=bytes_accessed, transcendentals=0
        ),
    )


def project_body(me, enc, *refs):
    weights, out = refs[:PIECES], refs[PIECES]
    for head in range(GROUP):
        columns = slice(head * WIDE, (head + 1) * WIDE)
        total = jnp.zeros((ROWS, WIDE), F32)
        for piece in range(PIECES):
            block = enc[jnp.bitwise_xor(me[0], piece)]
            total = total + dot(block, weights[piece][:, columns], (1, 0))
        out[jnp.bitwise_xor(me[1], head)] = total.astype(BF16)


def attention_body(ids, arrived, queries, grads, context, grad_queries, grad_kv, kv, forward, back):
    inverse_root = 1.0 / math.sqrt(HD)
    total = arrived[0].astype(F32)
    for part in range(1, GROUP):
        total = total + arrived[part].astype(F32)
    kv[...] = total.astype(BF16)
    row = lax.broadcasted_iota(jnp.int32, (ROWS, HD), 0)

    def to_blocks(x):
        shifted = pltpu.roll(x.astype(F32), ROWS - (CLEN - 1), 0)
        return jnp.where(row < ROWS - (CLEN - 1), shifted, 0.0).astype(BF16)

    def from_blocks(x):
        return jnp.where(row >= CLEN - 1, pltpu.roll(x, CLEN - 1, 0), 0.0).astype(BF16)

    query_blocks = to_blocks(queries[...])
    grad_blocks = to_blocks(grads[...])
    for span in range(SPANS):
        starts = [pl.multiple_of(ids[0, span * 2 + j] * NTOK, NTOK) for j in range(2)]
        taken = jnp.concatenate([kv[pl.ds(start, NTOK), :] for start in starts], axis=0)
        span_keys, span_values = taken[:, :HD], taken[:, HD:]
        q = query_blocks[span * CLEN : (span + 1) * CLEN, :]
        g = grad_blocks[span * CLEN : (span + 1) * CLEN, :]
        exponent = jnp.exp(dot(q, span_keys, (1, 1)) * inverse_root)
        probs = exponent / jnp.sum(exponent, -1, keepdims=True)
        attn = probs.astype(BF16)
        dprob = dot(g, span_values, (1, 1))
        scaled = (
            probs * (dprob - jnp.sum(probs * dprob, -1, keepdims=True)) * inverse_root
        ).astype(BF16)
        forward[span * CLEN : (span + 1) * CLEN, :] = dot(attn, span_values, (1, 0))
        back[span * CLEN : (span + 1) * CLEN, :] = dot(scaled, span_keys, (1, 0))
        grad_rows = jnp.concatenate([dot(scaled, q, (0, 0)), dot(attn, g, (0, 0))], axis=1)
        grad_rows = grad_rows.astype(BF16)
        for j in range(2):
            grad_kv[pl.ds(starts[j], NTOK), :] = grad_rows[j * NTOK : (j + 1) * NTOK, :]
    context[...] = from_blocks(forward[...])
    grad_queries[...] = from_blocks(back[...])


def heads_in_order(me, grads):
    return jnp.concatenate([grads[jnp.bitwise_xor(me[1], h)] for h in range(GROUP)], axis=1)


def encoder_grad_body(me, grads, *refs):
    weights, out = refs[:PIECES], refs[PIECES]
    grad = heads_in_order(me, grads)
    for piece in range(PIECES):
        out[jnp.bitwise_xor(me[0], piece)] = dot(grad, weights[piece][...], (1, 1)).astype(BF16)


def walk(me, near, far):
    for rest in range(4):
        for other in range(2):
            place = rest * 2 + jnp.bitwise_xor(me[2], other)
            yield place, rest, (far if other else near)


def slot(me, rest, head):
    along_s = head % 2
    sender = jnp.bitwise_xor(me[3], along_s) * 4 + (rest ^ (2 * along_s))
    return jnp.bitwise_xor(sender, me[4]) * 2 + head // 2


def weight_grad_body(me, enc, grads, near, far):
    grad = heads_in_order(me, grads)
    for place, rest, part in walk(me, near, far):
        total = dot(enc[place], grad, (0, 0)).astype(BF16)
        for head in range(GROUP):
            part[slot(me, rest, head)] = total[:, head * WIDE : (head + 1) * WIDE]


def swap(x, axis):
    return lax.ppermute(x, axis, [(0, 1), (1, 0)])


def diagonal(x):
    return lax.ppermute(x, ("yl", "xh"), [(i, 3 - i) for i in range(4)])


Y_AXES = ("yh", "yl", "s", "z0")


def exchange(home_to, other_to, flip):
    pairs = []
    for y in range(4):
        home = y // 2
        target = {"home": y, "away": 3 - y}
        for z in range(2):
            if home_to:
                pairs.append(((y, home, z), (target[home_to], home, z ^ flip)))
            if other_to:
                pairs.append(((y, 1 - home, z), (target[other_to], home, z ^ flip)))
    place = lambda at: at[0] * 4 + at[1] * 2 + at[2]
    return [(place(source), place(target)) for source, target in pairs]


EXCHANGES = [
    exchange("away", "home", 0),
    exchange(None, "away", 0),
    exchange("home", "away", 1),
    exchange("away", "home", 1),
]


def send(x, pairs):
    return lax.ppermute(x, Y_AXES, pairs)


def hop(x, by):
    return lax.ppermute(x, SENDERS, [(i, i ^ by) for i in range(8)])


def turned(flip):
    pairs = []
    for yh in range(2):
        for yl in range(2):
            for s in range(2):
                for z in range(2):
                    target = (s, yl if yh == s else 1 - yl, yh, z ^ flip)
                    pairs.append(((yh, yl, s, z), target))
    place = lambda at: ((at[0] * 2 + at[1]) * 2 + at[2]) * 2 + at[3]
    return [(place(source), place(target)) for source, target in pairs]


def turn_back(x, flip):
    pairs = [(target, source) for source, target in turned(flip)]
    return lax.ppermute(x, Y_AXES, pairs)


def per_device(queries, encoded, neighbour_ids, key_weight, value_weight, grad_context):
    enc = lax.all_gather(encoded[0], "zr", axis=0, tiled=False)

    home = lax.axis_index("yh") == lax.axis_index("s")
    low = jnp.where(home, lax.axis_index("yl"), 1 - lax.axis_index("yl"))
    block = low * 4 + lax.axis_index("xh") * 2 + lax.axis_index("c")
    own_head = lax.axis_index("z0") * 2 + lax.axis_index("s")
    places = [block, own_head, lax.axis_index("c"), lax.axis_index("s"), lax.axis_index(SENDERS)]
    me = jnp.stack(places).astype(jnp.int32)
    even = lax.axis_index("z0") == 0

    upper = jnp.concatenate([key_weight[:BLOCK], value_weight[:BLOCK]], axis=1)
    lower = jnp.concatenate([key_weight[BLOCK:], value_weight[BLOCK:]], axis=1)
    keep, give = jnp.where(even, upper, lower), jnp.where(even, lower, upper)
    got = [
        send(x, pairs) for x, pairs in zip((keep, keep, give, give), EXCHANGES, strict=True)
    ]
    mine = jnp.concatenate(
        [
            jnp.where(home, keep, got[0]),
            jnp.where(home, got[0], got[1]),
            jnp.where(home, got[2], got[3]),
            jnp.where(home, got[3], got[2]),
        ],
        axis=1,
    )
    gathered = [mine, swap(mine, "xh"), swap(mine, "yl"), diagonal(mine)]
    weights = []
    for piece in gathered:
        weights += [piece, swap(piece, "c")]

    flops = 2 * ROWS * (PIECES * BLOCK) * (GROUP * WIDE)
    moved = 2 * PIECES * BLOCK * (ROWS + GROUP * WIDE)
    group = jax.ShapeDtypeStruct((GROUP, ROWS, WIDE), BF16)
    terms = kernel_call(project_body, group, 1, 1 + PIECES, flops=flops, bytes_accessed=moved)(
        me, enc, *weights
    )
    arrived = lax.all_to_all(terms, ("z0", "s"), 0, 0, tiled=True)

    head = jax.ShapeDtypeStruct((ROWS, HD), BF16)
    context, grad_queries, grad_own = kernel_call(
        attention_body,
        (head, head, jax.ShapeDtypeStruct((ROWS, WIDE), BF16)),
        1,
        3,
        scratch=(
            pltpu.VMEM((ROWS, WIDE), BF16),
            pltpu.VMEM((ROWS, HD), F32),
            pltpu.VMEM((ROWS, HD), F32),
        ),
        flops=2 * ROWS * CLEN * HD * 6,
        bytes_accessed=1 << 20,
    )(neighbour_ids, arrived, queries[0], grad_context[0])
    grads = lax.all_gather(grad_own, ("z0", "s"), axis=0, tiled=False)

    enc_terms = kernel_call(
        encoder_grad_body,
        jax.ShapeDtypeStruct((PIECES, ROWS, BLOCK), BF16),
        1,
        1 + PIECES,
        flops=flops,
        bytes_accessed=moved,
    )(me, grads, *weights)
    grad_encoded = lax.psum_scatter(enc_terms, "zr", scatter_dimension=0, tiled=False)

    part = jax.ShapeDtypeStruct((2 * PIECES, BLOCK, WIDE), BF16)
    near, far = kernel_call(
        weight_grad_body, (part, part), 1, 2, flops=flops, bytes_accessed=moved
    )(me, enc, grads)
    near = (near.astype(F32) + swap(far, "c").astype(F32)).astype(BF16)
    near = near.reshape(8, 2, BLOCK, WIDE)
    parts = [near[0]] + [hop(near[k], k) for k in range(1, 8)]
    total = parts[0].astype(F32)
    for part in parts[1:]:
        total = total + part.astype(F32)
    total = total.astype(BF16)
    kept, given = turn_back(total[0], 0), turn_back(total[1], 1)
    upper, lower = jnp.where(even, kept, given), jnp.where(even, given, kept)
    weight_grad = jnp.concatenate([upper, lower], axis=0)
    return (
        context[None],
        grad_queries[None],
        grad_encoded[None],
        weight_grad[:, :HD],
        weight_grad[:, HD:],
    )


def solution(mesh):
    grid = Mesh(mesh.devices.reshape(2, 2, 2, 2, 2, 8, 2), AXES)
    return jax.shard_map(
        per_device,
        mesh=grid,
        in_specs=(
            P(DP, None, HEADS),
            P(DP, None, HEADS),
            P(DP, None),
            P(DP, HEADS),
            P(DP, HEADS),
            P(DP, None, HEADS),
        ),
        out_specs=(
            P(DP, None, HEADS),
            P(DP, None, HEADS),
            P(DP, None, HEADS),
            P(DP, HEADS),
            P(DP, HEADS),
        ),
        check_vma=False,
    )
```

time: 190 us -> 175 us (0.921)
  waiting for transfers between devices: 101 us -> 45 us
  blocking collectives: 0 us -> 23.3 us
  starting transfers between devices: 57.1 us -> 72.4 us
  local copies, waits for them, and re-layouts: 5.75 us -> 2.46 us
  other arithmetic: 0.99 us -> 3.4 us
    ppermute x4 -> x13, starting transfers between devices: 13 us -> 49.7 us  [the longest x7 27.5 us: hop(): return lax.ppermute(x, SENDERS, [(i, i ^ by) for i in range(8)])]
    ppermute x14 -> x7, waiting for transfers between devices: 36.6 us -> 9.3 us  [swap(): return lax.ppermute(x, axis, [(0, 1), (1, 0)])]
    all_gather x1, waiting for transfers between devices: 25.2 us -> 3.32 us  [per_device(): enc = lax.all_gather(encoded[0], 'zr', axis=0, tiled=False)]
    ppermute x14 -> x7, starting transfers between devices: 37.1 us -> 20.7 us  [swap(): return lax.ppermute(x, axis, [(0, 1), (1, 0)])]
    reduce_scatter x1, waiting for transfers between devices: 14.3 us -> 0.01 us  [per_device(): lax.psum_scatter(enc_terms, 'zr', scatter_dimension=0, tiled=False)]
    all_gather x0 -> x1, blocking collectives: none -> 13.8 us  [per_device(): grads = lax.all_gather(grad_own, ('z0', 's'), axis=0, tiled=False)]
    ppermute x4 -> x13, waiting for transfers between devices: 17.3 us -> 27.1 us  [the longest x7 14.1 us: hop(): return lax.ppermute(x, SENDERS, [(i, i ^ by) for i in range(8)])]
    all_to_all x0 -> x1, blocking collectives: none -> 9.52 us  [per_device(): arrived = lax.all_to_all(terms, ('z0', 's'), 0, 0, tiled=True)]
  transfers between devices with their start and end apart: 22 -> 23, of which waited for: 13 -> 13; matrix products, arithmetic and copies ran while one was open for 2% -> 3% of each run, Pallas kernels for 1% -> 2%
where the time goes in v2:
time: 175 us; the launch traced here: 173 us
  starting transfers between devices  72.4 us (41%)
  waiting for transfers between devices  45 us (26%)
  blocking collectives  23.3 us (13%)
  between operations  14.5 us (8%)
  Pallas kernels  12.1 us (7%)
  other arithmetic  3.4 us (2%)
  local copies, waits for them, and re-layouts  2.46 us (1%)
    ppermute x7, starting transfers between devices, hop(): return lax.ppermute(x, SENDERS, [(i, i ^ by) for i in range(8)])  27.5 us
    ppermute x7, starting transfers between devices, swap(): return lax.ppermute(x, axis, [(0, 1), (1, 0)])  20.7 us
    ppermute x7, waiting for transfers between devices, hop(): return lax.ppermute(x, SENDERS, [(i, i ^ by) for i in range(8)])  14.1 us
    all_gather x1, blocking collectives, per_device(): grads = lax.all_gather(grad_own, ('z0', 's'), axis=0, tiled=False)  13.8 us
    ppermute x4, starting transfers between devices, send(): return lax.ppermute(x, Y_AXES, pairs)  13.5 us
    all_to_all x1, blocking collectives, per_device(): arrived = lax.all_to_all(terms, ('z0', 's'), 0, 0, tiled=True)  9.52 us
    ppermute x7, waiting for transfers between devices, swap(): return lax.ppermute(x, axis, [(0, 1), (1, 0)])  9.3 us
    ppermute x2, starting transfers between devices, turn_back(): return lax.ppermute(x, Y_AXES, pairs)  8.62 us
  transfers between devices with their start and end apart: 23, of which 13 were waited for; matrix products, arithmetic and copies ran while one was open for 3% of the time, Pallas kernels for 2%

profile of v2, /device:TPU:6, one launch (start us, length us, event | category | flops | bytes accessed | tf_op | source)
XLA Modules:
  0.0 173.1 jit_solution(2366856555435377357)
XLA Ops:
  7.2 0.7 all-gather.3.cloned.1.call-update
  8.0 1.0 fusion.2
  9.0 4.1 %collective-permute-start.3 = (bf16[256,256]{1,0:T(8,128)(2,1)S(1)}, bf16[256,256]{1,0:T(8,128)(2,1)S(1)}, u32[]{:S(2)}, u32[]{:S(2)}) collective-permute-start(bf16[256,256]{1,0:T(8,128)(2,1)S(1)} %get-tuple-element.29), channel_id=1, source_target_pairs={{0,385},{16,1},{1,384},{17,0},{128,257},{144,129},{129,256},{145,1... | collective-permute-start | bytes 393224 | tf_op jit(solution)/shard_map/ppermute | solution.py:165
  13.1 5.1 %collective-permute-start.2 = (bf16[256,256]{1,0:T(8,128)(2,1)S(1)}, bf16[256,256]{1,0:T(8,128)(2,1)S(1)}, u32[]{:S(2)}, u32[]{:S(2)}) collective-permute-start(bf16[256,256]{1,0:T(8,128)(2,1)S(1)} %get-tuple-element.29), channel_id=1, source_target_pairs={{0,1},{16,385},{1,0},{17,384},{128,129},{144,257},{129,128},{145,2... | collective-permute-start | bytes 393224 | tf_op jit(solution)/shard_map/ppermute | solution.py:165
  18.2 2.4 %collective-permute-start.1 = (bf16[256,256]{1,0:T(8,128)(2,1)S(1)}, bf16[256,256]{1,0:T(8,128)(2,1)S(1)}, u32[]{:S(2)}, u32[]{:S(2)}) collective-permute-start(bf16[256,256]{1,0:T(8,128)(2,1)S(1)} %get-tuple-element.28), channel_id=1, source_target_pairs={{16,384},{17,385},{144,256},{145,257},{256,144},{257,145},{384,16}... | collective-permute-start | bytes 393224 | tf_op jit(solution)/shard_map/ppermute | solution.py:165
  20.6 1.9 %collective-permute-start = (bf16[256,256]{1,0:T(8,128)(2,1)S(1)}, bf16[256,256]{1,0:T(8,128)(2,1)S(1)}, u32[]{:S(2)}, u32[]{:S(2)}) collective-permute-start(bf16[256,256]{1,0:T(8,128)(2,1)S(1)} %get-tuple-element.28), channel_id=1, source_target_pairs={{0,384},{16,0},{1,385},{17,1},{128,256},{144,128},{129,257},{145,1... | collective-permute-start | bytes 393224 | tf_op jit(solution)/shard_map/ppermute | solution.py:165
  22.5 0.4 collective-permute-done.2
  23.0 5.4 %collective-permute-done.1 = bf16[256,256]{1,0:T(8,128)(2,1)S(1)} collective-permute-done((bf16[256,256]{1,0:T(8,128)(2,1)S(1)}, bf16[256,256]{1,0:T(8,128)(2,1)S(1)}, u32[]{:S(2)}, u32[]{:S(2)}) %collective-permute-start.1) | collective-permute-done | bytes 131104 | tf_op jit(solution)/shard_map/ppermute | solution.py:165
  28.3 1.4 collective-permute-done
  29.9 1.9 %collective-permute-start.9 = (bf16[256,1024]{1,0:T(8,128)(2,1)S(1)}, bf16[256,1024]{1,0:T(8,128)(2,1)S(1)}, u32[]{:S(2)}, u32[]{:S(2)}) collective-permute-start(bf16[256,1024]{1,0:T(8,128)(2,1)S(1)} %pad_maximum_fusion.refs_0_), channel_id=1, source_target_pairs={{0,192},{64,128},{128,64},{192,0},{1,193},{65,129},{129,65},{193,1... | collective-permute-start | bytes 1572872 | tf_op jit(solution)/shard_map/ppermute | solution.py:136
  31.8 8.8 %collective-permute-start.7 = (bf16[256,1024]{1,0:T(8,128)(2,1)S(1)}, bf16[256,1024]{1,0:T(8,128)(2,1)S(1)}, u32[]{:S(2)}, u32[]{:S(2)}) collective-permute-start(bf16[256,1024]{1,0:T(8,128)(2,1)S(1)} %pad_maximum_fusion.refs_0_), channel_id=1, source_target_pairs={{0,128},{128,0},{1,129},{129,1},{2,130},{130,2},{3,131},{131,3},{4... | collective-permute-start | bytes 1572872 | tf_op jit(solution)/shard_map/ppermute | solution.py:132
  40.5 1.9 %collective-permute-start.5 = (bf16[256,1024]{1,0:T(8,128)(2,1)S(1)}, bf16[256,1024]{1,0:T(8,128)(2,1)S(1)}, u32[]{:S(2)}, u32[]{:S(2)}) collective-permute-start(bf16[256,1024]{1,0:T(8,128)(2,1)S(1)} %pad_maximum_fusion.refs_0_), channel_id=1, source_target_pairs={{0,64},{64,0},{1,65},{65,1},{2,66},{66,2},{3,67},{67,3},{4,68},{68... | collective-permute-start | bytes 1572872 | tf_op jit(solution)/shard_map/ppermute | solution.py:132
  42.5 1.9 %collective-permute-start.4 = (bf16[256,1024]{1,0:T(8,128)(2,1)S(1)}, bf16[256,1024]{1,0:T(8,128)(2,1)S(1)}, u32[]{:S(2)}, u32[]{:S(2)}) collective-permute-start(bf16[256,1024]{1,0:T(8,128)(2,1)S(1)} %pad_maximum_fusion.refs_0_), channel_id=1, source_target_pairs={{0,32},{32,0},{1,33},{33,1},{2,34},{34,2},{3,35},{35,3},{4,36},{36... | collective-permute-start | bytes 1572872 | tf_op jit(solution)/shard_map/ppermute | solution.py:132
  44.4 4.7 %collective-permute-done.9.refs_6_ = bf16[256,1024]{1,0:T(8,128)(2,1)S(1)} collective-permute-done((bf16[256,1024]{1,0:T(8,128)(2,1)S(1)}, bf16[256,1024]{1,0:T(8,128)(2,1)S(1)}, u32[]{:S(2)}, u32[]{:S(2)}) %collective-permute-start.9) | collective-permute-done | bytes 524320 | tf_op jit(solution)/shard_map/ppermute | solution.py:136
  49.1 1.9 %collective-permute-start.10 = (bf16[256,1024]{1,0:T(8,128)(2,1)S(1)}, bf16[256,1024]{1,0:T(8,128)(2,1)S(1)}, u32[]{:S(2)}, u32[]{:S(2)}) collective-permute-start(bf16[256,1024]{1,0:T(8,128)(2,1)S(1)} %collective-permute-done.9.refs_6_), channel_id=1, source_target_pairs={{0,32},{32,0},{1,33},{33,1},{2,34},{34,2},{3,35},{35,3},{4,36},{36... | collective-permute-start | bytes 1572872 | tf_op jit(solution)/shard_map/ppermute | solution.py:132
  51.0 7.0 %collective-permute-done.7.refs_4_ = bf16[256,1024]{1,0:T(8,128)(2,1)S(1)} collective-permute-done((bf16[256,1024]{1,0:T(8,128)(2,1)S(1)}, bf16[256,1024]{1,0:T(8,128)(2,1)S(1)}, u32[]{:S(2)}, u32[]{:S(2)}) %collective-permute-start.7) | collective-permute-done | bytes 524320 | tf_op jit(solution)/shard_map/ppermute | solution.py:132
  57.9 1.9 %collective-permute-start.8 = (bf16[256,1024]{1,0:T(8,128)(2,1)S(1)}, bf16[256,1024]{1,0:T(8,128)(2,1)}, u32[]{:S(2)}, u32[]{:S(2)}) collective-permute-start(bf16[256,1024]{1,0:T(8,128)(2,1)S(1)} %collective-permute-done.7.refs_4_), channel_id=1, source_target_pairs={{0,32},{32,0},{1,33},{33,1},{2,34},{34,2},{3,35},{35,3},{4,36},{36... | collective-permute-start | bytes 1572872 | tf_op jit(solution)/shard_map/ppermute | solution.py:132
  59.9 2.4 %collective-permute-start.6 = (bf16[256,1024]{1,0:T(8,128)(2,1)S(1)}, bf16[256,1024]{1,0:T(8,128)(2,1)}, u32[]{:S(2)}, u32[]{:S(2)}) collective-permute-start(bf16[256,1024]{1,0:T(8,128)(2,1)S(1)} %collective-permute-done.5.refs_2_), channel_id=1, source_target_pairs={{0,32},{32,0},{1,33},{33,1},{2,34},{34,2},{3,35},{35,3},{4,36},{36... | collective-permute-start | bytes 1572872 | tf_op jit(solution)/shard_map/ppermute | solution.py:132
  62.3 0.1 stack.23.me
  62.4 1.5 collective-permute-done.6.refs_3_
  63.9 3.3 %all-gather.3.cloned.1.call-done.enc = bf16[8,256,256]{2,1,0:T(8,128)(2,1)} async-done(((bf16[1,256,256]{2,1,0:T(8,128)(2,1)}), bf16[8,256,256]{2,1,0:T(8,128)(2,1)}) %all-gather.3.cloned.1.call-update) | async-done | bytes 1048592 | tf_op jit(solution)/shard_map/all_gather | solution.py:190
  67.3 1.2 copy-done.8
  68.5 2.5 %shard_map.101 = bf16[4,256,256]{2,1,0:T(8,128)(2,1)S(1)} custom-call(s32[5]{0:T(128)S(1)} %stack.23.me, bf16[8,256,256]{2,1,0:T(8,128)(2,1)S(1)} %copy-done.8, bf16[256,1024]{1,0:T(8,128)(2,1)S(1)} %pad_maximum_fusion.refs_0_, bf16[256,1024]{1,0:T(8,128)(2,1)S(1)} %collective-permute-done.4.refs_1_, bf16[256,1024]{1,0:T(8,128)(2,1)S(1)} %collective-permute-done.5.refs_2_, ...), custom_call_target="tpu_custom_call" | custom-call | flops 1073741824 | bytes 5242880 | tf_op jit(solution)/shard_map/pallas_call | solution.py:223
  71.1 9.5 %all_to_all.5.arrived = bf16[4,256,256]{2,1,0:T(8,128)(2,1)S(1)} all-to-all(bf16[4,256,256]{2,1,0:T(8,128)(2,1)S(1)} %shard_map.101), channel_id=1, replica_groups=mesh['yh'=2,'yl'=2,'xh'=2,'c'=2,'s'=2,'zr'=8,'z0'=2] {'z0','s'}, dimensions={0} | all-to-all | bytes 1048576 | tf_op jit(solution)/shard_map/all_to_all | solution.py:226
  80.6 2.8 %shard_map.102 = (bf16[256,128]{1,0:T(8,128)(2,1)}, bf16[256,128]{1,0:T(8,128)(2,1)}, bf16[256,256]{1,0:T(8,128)(2,1)S(1)}) custom-call(s32[1,8]{1,0:T(1,128)S(1)} %copy-done.12, bf16[4,256,256]{2,1,0:T(8,128)(2,1)S(1)} %all_to_all.5.arrived, bf16[256,128]{1,0:T(8,128)(2,1)S(1)} %bitcast.16, bf16[256,128]{1,0:T(8,128)(2,1)S(1)} %bitcast.17), custom_call_target="tpu_custom_call" | custom-call | flops 25165824 | bytes 1048576 | tf_op jit(solution)/shard_map/pallas_call | solution.py:229
  83.4 13.8 %all-gather = bf16[1024,256]{1,0:T(8,128)(2,1)S(1)} all-gather(bf16[256,256]{1,0:T(8,128)(2,1)S(1)} %get-tuple-element.12), channel_id=2, replica_groups=mesh['yh'=2,'yl'=2,'xh'=2,'c'=2,'s'=2,'zr'=8,'z0'=2] {'z0','s'}, dimensions={0}, use_global_device_ids=true | all-gather | bytes 655360 | tf_op jit(solution)/shard_map/all_gather | solution.py:242
  97.2 3.2 %shard_map.104 = (bf16[16,256,256]{2,1,0:T(8,128)(2,1)S(1)}, bf16[16,256,256]{2,1,0:T(8,128)(2,1)}) custom-call(s32[5]{0:T(128)S(1)} %stack.23.me, bf16[8,256,256]{2,1,0:T(8,128)(2,1)S(1)} %copy-done.9, bf16[4,256,256]{2,1,0:T(8,128)(2,1)S(1)} %bitcast.14), custom_call_target="tpu_custom_call" | custom-call | flops 1073741824 | bytes 5242880 | tf_op jit(solution)/shard_map/pallas_call | solution.py:255
  100.4 1.9 %collective-permute-start.11 = (bf16[16,256,256]{2,1,0:T(8,128)(2,1)}, bf16[16,256,256]{2,1,0:T(8,128)(2,1)}, u32[]{:S(2)}, u32[]{:S(2)}) collective-permute-start(bf16[16,256,256]{2,1,0:T(8,128)(2,1)} %get-tuple-element.14), channel_id=1, source_target_pairs={{0,32},{32,0},{1,33},{33,1},{2,34},{34,2},{3,35},{35,3},{4,36},{36... | collective-permute-start | bytes 6291464 | tf_op jit(solution)/shard_map/ppermute | solution.py:132
  102.4 3.6 %shard_map.103 = bf16[8,256,256]{2,1,0:T(8,128)(2,1)} custom-call(s32[5]{0:T(128)S(1)} %stack.23.me, bf16[4,256,256]{2,1,0:T(8,128)(2,1)S(1)} %bitcast.15, bf16[256,1024]{1,0:T(8,128)(2,1)S(1)} %pad_maximum_fusion.refs_0_, bf16[256,1024]{1,0:T(8,128)(2,1)S(1)} %copy-done.5, bf16[256,1024]{1,0:T(8,128)(2,1)S(1)} %copy-done.3, ...), custom_call_target="tpu_custom_call" | custom-call | flops 1073741824 | bytes 5242880 | tf_op jit(solution)/shard_map/pallas_call | solution.py:244
  106.0 0.8 collective-permute-done.11
  106.8 2.2 %add_convert_fusion = bf16[16,256,256]{2,1,0:T(8,128)(2,1)S(1)} fusion(bf16[16,256,256]{2,1,0:T(8,128)(2,1)} %collective-permute-done.11, bf16[16,256,256]{2,1,0:T(8,128)(2,1)S(1)} %get-tuple-element.13), kind=kLoop, calls=%fused_computation | loop fusion | flops 4194304 | bytes 6291456 | tf_op jit(solution)/shard_map/convert_element_type | solution.py:258
  109.0 0.1 fusion.1
  109.1 5.4 %collective-permute-start.12 = (bf16[2,256,256]{2,1,0:T(8,128)(2,1)S(1)}, bf16[2,256,256]{2,1,0:T(8,128)(2,1)S(1)}, u32[]{:S(2)}, u32[]{:S(2)}) collective-permute-start(bf16[2,256,256]{2,1,0:T(8,128)(2,1)S(1)} %get-tuple-element.15), channel_id=1, source_target_pairs={{0,64},{64,0},{128,192},{192,128},{256,320},{320,256},{384,448},{4... | collective-permute-start | bytes 786440 | tf_op jit(solution)/shard_map/ppermute | solution.py:169
  114.5 3.6 %collective-permute-start.18 = (bf16[2,256,256]{2,1,0:T(8,128)(2,1)S(1)}, bf16[2,256,256]{2,1,0:T(8,128)(2,1)S(1)}, u32[]{:S(2)}, u32[]{:S(2)}) collective-permute-start(bf16[2,256,256]{2,1,0:T(8,128)(2,1)S(1)} %get-tuple-element.16), channel_id=1, source_target_pairs={{0,448},{64,384},{128,320},{192,256},{256,192},{320,128},{384,64},... | collective-permute-start | bytes 786440 | tf_op jit(solution)/shard_map/ppermute | solution.py:169
  118.1 3.0 %collective-permute-start.17 = (bf16[2,256,256]{2,1,0:T(8,128)(2,1)S(1)}, bf16[2,256,256]{2,1,0:T(8,128)(2,1)S(1)}, u32[]{:S(2)}, u32[]{:S(2)}) collective-permute-start(bf16[2,256,256]{2,1,0:T(8,128)(2,1)S(1)} %get-tuple-element.17), channel_id=1, source_target_pairs={{0,384},{64,448},{128,256},{192,320},{256,128},{320,192},{384,0},{... | collective-permute-start | bytes 786440 | tf_op jit(solution)/shard_map/ppermute | solution.py:169
  121.1 3.7 %collective-permute-start.16 = (bf16[2,256,256]{2,1,0:T(8,128)(2,1)S(1)}, bf16[2,256,256]{2,1,0:T(8,128)(2,1)S(1)}, u32[]{:S(2)}, u32[]{:S(2)}) collective-permute-start(bf16[2,256,256]{2,1,0:T(8,128)(2,1)S(1)} %get-tuple-element.18), channel_id=1, source_target_pairs={{0,320},{64,256},{128,448},{192,384},{256,64},{320,0},{384,192},{4... | collective-permute-start | bytes 786440 | tf_op jit(solution)/shard_map/ppermute | solution.py:169
  124.8 6.5 %collective-permute-start.15 = (bf16[2,256,256]{2,1,0:T(8,128)(2,1)S(1)}, bf16[2,256,256]{2,1,0:T(8,128)(2,1)S(1)}, u32[]{:S(2)}, u32[]{:S(2)}) collective-permute-start(bf16[2,256,256]{2,1,0:T(8,128)(2,1)S(1)} %get-tuple-element.19), channel_id=1, source_target_pairs={{0,256},{64,320},{128,384},{192,448},{256,0},{320,64},{384,128},{4... | collective-permute-start | bytes 786440 | tf_op jit(solution)/shard_map/ppermute | solution.py:169
  131.4 1.9 %collective-permute-start.14 = (bf16[2,256,256]{2,1,0:T(8,128)(2,1)S(1)}, bf16[2,256,256]{2,1,0:T(8,128)(2,1)S(1)}, u32[]{:S(2)}, u32[]{:S(2)}) collective-permute-start(bf16[2,256,256]{2,1,0:T(8,128)(2,1)S(1)} %get-tuple-element.20), channel_id=1, source_target_pairs={{0,192},{64,128},{128,64},{192,0},{256,448},{320,384},{384,320},{4... | collective-permute-start | bytes 786440 | tf_op jit(solution)/shard_map/ppermute | solution.py:169
  133.3 3.4 %collective-permute-start.13 = (bf16[2,256,256]{2,1,0:T(8,128)(2,1)S(1)}, bf16[2,256,256]{2,1,0:T(8,128)(2,1)S(1)}, u32[]{:S(2)}, u32[]{:S(2)}) collective-permute-start(bf16[2,256,256]{2,1,0:T(8,128)(2,1)S(1)} %get-tuple-element.21), channel_id=1, source_target_pairs={{0,128},{64,192},{128,0},{192,64},{256,384},{320,448},{384,256},{4... | collective-permute-start | bytes 786440 | tf_op jit(solution)/shard_map/ppermute | solution.py:169
  136.7 4.8 %collective-permute-done.17 = bf16[2,256,256]{2,1,0:T(8,128)(2,1)S(1)} collective-permute-done((bf16[2,256,256]{2,1,0:T(8,128)(2,1)S(1)}, bf16[2,256,256]{2,1,0:T(8,128)(2,1)S(1)}, u32[]{:S(2)}, u32[]{:S(2)}) %collective-permute-start.17) | collective-permute-done | bytes 262176 | tf_op jit(solution)/shard_map/ppermute | solution.py:169
  141.6 4.4 %collective-permute-done.15 = bf16[2,256,256]{2,1,0:T(8,128)(2,1)S(1)} collective-permute-done((bf16[2,256,256]{2,1,0:T(8,128)(2,1)S(1)}, bf16[2,256,256]{2,1,0:T(8,128)(2,1)S(1)}, u32[]{:S(2)}, u32[]{:S(2)}) %collective-permute-start.15) | collective-permute-done | bytes 262176 | tf_op jit(solution)/shard_map/ppermute | solution.py:169
  146.0 4.8 %collective-permute-done.13 = bf16[2,256,256]{2,1,0:T(8,128)(2,1)S(1)} collective-permute-done((bf16[2,256,256]{2,1,0:T(8,128)(2,1)S(1)}, bf16[2,256,256]{2,1,0:T(8,128)(2,1)S(1)}, u32[]{:S(2)}, u32[]{:S(2)}) %collective-permute-start.13) | collective-permute-done | bytes 262176 | tf_op jit(solution)/shard_map/ppermute | solution.py:169
  150.8 0.3 add_convert_fusion.1
  151.1 3.6 %collective-permute-start.20 = (bf16[256,256]{1,0:T(8,128)(2,1)S(1)}, bf16[256,256]{1,0:T(8,128)(2,1)S(1)}, u32[]{:S(2)}, u32[]{:S(2)}) collective-permute-start(bf16[256,256]{1,0:T(8,128)(2,1)S(1)} %get-tuple-element.26), channel_id=1, source_target_pairs={{1,0},{0,1},{385,16},{384,17},{129,128},{128,129},{257,144},{256,1... | collective-permute-start | bytes 393224 | tf_op jit(solution)/shard_map/ppermute | solution.py:186
  154.8 5.0 %collective-permute-start.19 = (bf16[256,256]{1,0:T(8,128)(2,1)S(1)}, bf16[256,256]{1,0:T(8,128)(2,1)S(1)}, u32[]{:S(2)}, u32[]{:S(2)}) collective-permute-start(bf16[256,256]{1,0:T(8,128)(2,1)S(1)} %get-tuple-element.27), channel_id=1, source_target_pairs={{0,0},{1,1},{384,16},{385,17},{128,128},{129,129},{256,144},{257,1... | collective-permute-start | bytes 393224 | tf_op jit(solution)/shard_map/ppermute | solution.py:186
  159.8 3.1 %collective-permute-done.20 = bf16[256,256]{1,0:T(8,128)(2,1)S(1)} collective-permute-done((bf16[256,256]{1,0:T(8,128)(2,1)S(1)}, bf16[256,256]{1,0:T(8,128)(2,1)S(1)}, u32[]{:S(2)}, u32[]{:S(2)}) %collective-permute-start.20) | collective-permute-done | bytes 131104 | tf_op jit(solution)/shard_map/ppermute | solution.py:186
  162.8 2.7 %collective-permute-done.19 = bf16[256,256]{1,0:T(8,128)(2,1)S(1)} collective-permute-done((bf16[256,256]{1,0:T(8,128)(2,1)S(1)}, bf16[256,256]{1,0:T(8,128)(2,1)S(1)}, u32[]{:S(2)}, u32[]{:S(2)}) %collective-permute-start.19) | collective-permute-done | bytes 131104 | tf_op jit(solution)/shard_map/ppermute | solution.py:186
  165.6 0.7 pad_maximum_fusion.1
  (44 shorter events, 0.4 us)
Async XLA Ops:
  7.2 60.1 %all-gather.3.cloned.1.call-start = ((), (), s32[]{:S(2)}) async-start(), calls=%async_computation.2 | async-start | bytes 1179648 | tf_op jit(solution)/shard_map/all_gather | solution.py:190
  7.9 158.4 %reduce-scatter.2.cloned.1.call-start = ((), (), s32[]{:S(2)}) async-start(), calls=%async_computation.3 | async-start | bytes 1179648 | tf_op jit(solution)/shard_map/reduce_scatter | solution.py:252
  9.0 13.6 %collective-permute-start.3 = (bf16[256,256]{1,0:T(8,128)(2,1)S(1)}, bf16[256,256]{1,0:T(8,128)(2,1)S(1)}, u32[]{:S(2)}, u32[]{:S(2)}) collective-permute-start(bf16[256,256]{1,0:T(8,128)(2,1)S(1)} %get-tuple-element.29), channel_id=1, source_target_pairs={{0,385},{16,1},{1,384},{17,0},{128,257},{144,129},{129,256},{145,1... | collective-permute-start | bytes 393224 | tf_op jit(solution)/shard_map/ppermute | solution.py:165
  13.1 9.9 %collective-permute-start.2 = (bf16[256,256]{1,0:T(8,128)(2,1)S(1)}, bf16[256,256]{1,0:T(8,128)(2,1)S(1)}, u32[]{:S(2)}, u32[]{:S(2)}) collective-permute-start(bf16[256,256]{1,0:T(8,128)(2,1)S(1)} %get-tuple-element.29), channel_id=1, source_target_pairs={{0,1},{16,385},{1,0},{17,384},{128,129},{144,257},{129,128},{145,2... | collective-permute-start | bytes 393224 | tf_op jit(solution)/shard_map/ppermute | solution.py:165
  18.2 10.1 %collective-permute-start.1 = (bf16[256,256]{1,0:T(8,128)(2,1)S(1)}, bf16[256,256]{1,0:T(8,128)(2,1)S(1)}, u32[]{:S(2)}, u32[]{:S(2)}) collective-permute-start(bf16[256,256]{1,0:T(8,128)(2,1)S(1)} %get-tuple-element.28), channel_id=1, source_target_pairs={{16,384},{17,385},{144,256},{145,257},{256,144},{257,145},{384,16}... | collective-permute-start | bytes 393224 | tf_op jit(solution)/shard_map/ppermute | solution.py:165
  20.6 9.2 %collective-permute-start = (bf16[256,256]{1,0:T(8,128)(2,1)S(1)}, bf16[256,256]{1,0:T(8,128)(2,1)S(1)}, u32[]{:S(2)}, u32[]{:S(2)}) collective-permute-start(bf16[256,256]{1,0:T(8,128)(2,1)S(1)} %get-tuple-element.28), channel_id=1, source_target_pairs={{0,384},{16,0},{1,385},{17,1},{128,256},{144,128},{129,257},{145,1... | collective-permute-start | bytes 393224 | tf_op jit(solution)/shard_map/ppermute | solution.py:165
  29.9 19.2 %collective-permute-start.9 = (bf16[256,1024]{1,0:T(8,128)(2,1)S(1)}, bf16[256,1024]{1,0:T(8,128)(2,1)S(1)}, u32[]{:S(2)}, u32[]{:S(2)}) collective-permute-start(bf16[256,1024]{1,0:T(8,128)(2,1)S(1)} %pad_maximum_fusion.refs_0_), channel_id=1, source_target_pairs={{0,192},{64,128},{128,64},{192,0},{1,193},{65,129},{129,65},{193,1... | collective-permute-start | bytes 1572872 | tf_op jit(solution)/shard_map/ppermute | solution.py:136
  31.8 26.2 %collective-permute-start.7 = (bf16[256,1024]{1,0:T(8,128)(2,1)S(1)}, bf16[256,1024]{1,0:T(8,128)(2,1)S(1)}, u32[]{:S(2)}, u32[]{:S(2)}) collective-permute-start(bf16[256,1024]{1,0:T(8,128)(2,1)S(1)} %pad_maximum_fusion.refs_0_), channel_id=1, source_target_pairs={{0,128},{128,0},{1,129},{129,1},{2,130},{130,2},{3,131},{131,3},{4... | collective-permute-start | bytes 1572872 | tf_op jit(solution)/shard_map/ppermute | solution.py:132
  40.5 19.3 %collective-permute-start.5 = (bf16[256,1024]{1,0:T(8,128)(2,1)S(1)}, bf16[256,1024]{1,0:T(8,128)(2,1)S(1)}, u32[]{:S(2)}, u32[]{:S(2)}) collective-permute-start(bf16[256,1024]{1,0:T(8,128)(2,1)S(1)} %pad_maximum_fusion.refs_0_), channel_id=1, source_target_pairs={{0,64},{64,0},{1,65},{65,1},{2,66},{66,2},{3,67},{67,3},{4,68},{68... | collective-permute-start | bytes 1572872 | tf_op jit(solution)/shard_map/ppermute | solution.py:132
  42.5 20.0 %collective-permute-start.4 = (bf16[256,1024]{1,0:T(8,128)(2,1)S(1)}, bf16[256,1024]{1,0:T(8,128)(2,1)S(1)}, u32[]{:S(2)}, u32[]{:S(2)}) collective-permute-start(bf16[256,1024]{1,0:T(8,128)(2,1)S(1)} %pad_maximum_fusion.refs_0_), channel_id=1, source_target_pairs={{0,32},{32,0},{1,33},{33,1},{2,34},{34,2},{3,35},{35,3},{4,36},{36... | collective-permute-start | bytes 1572872 | tf_op jit(solution)/shard_map/ppermute | solution.py:132
  49.1 13.4 %collective-permute-start.10 = (bf16[256,1024]{1,0:T(8,128)(2,1)S(1)}, bf16[256,1024]{1,0:T(8,128)(2,1)S(1)}, u32[]{:S(2)}, u32[]{:S(2)}) collective-permute-start(bf16[256,1024]{1,0:T(8,128)(2,1)S(1)} %collective-permute-done.9.refs_6_), channel_id=1, source_target_pairs={{0,32},{32,0},{1,33},{33,1},{2,34},{34,2},{3,35},{35,3},{4,36},{36... | collective-permute-start | bytes 1572872 | tf_op jit(solution)/shard_map/ppermute | solution.py:132
  57.9 13.1 %copy-start = (bf16[256,1024]{1,0:T(8,128)(2,1)}, bf16[256,1024]{1,0:T(8,128)(2,1)S(1)}, u32[]{:S(2)}) copy-start(bf16[256,1024]{1,0:T(8,128)(2,1)S(1)} %collective-permute-done.7.refs_4_) | copy-start | bytes 1572868
  57.9 4.5 %collective-permute-start.8 = (bf16[256,1024]{1,0:T(8,128)(2,1)S(1)}, bf16[256,1024]{1,0:T(8,128)(2,1)}, u32[]{:S(2)}, u32[]{:S(2)}) collective-permute-start(bf16[256,1024]{1,0:T(8,128)(2,1)S(1)} %collective-permute-done.7.refs_4_), channel_id=1, source_target_pairs={{0,32},{32,0},{1,33},{33,1},{2,34},{34,2},{3,35},{35,3},{4,36},{36... | collective-permute-start | bytes 1572872 | tf_op jit(solution)/shard_map/ppermute | solution.py:132
  59.9 11.2 %copy-start.2 = (bf16[256,1024]{1,0:T(8,128)(2,1)}, bf16[256,1024]{1,0:T(8,128)(2,1)S(1)}, u32[]{:S(2)}) copy-start(bf16[256,1024]{1,0:T(8,128)(2,1)S(1)} %collective-permute-done.5.refs_2_) | copy-start | bytes 1572868
  59.9 4.1 %collective-permute-start.6 = (bf16[256,1024]{1,0:T(8,128)(2,1)S(1)}, bf16[256,1024]{1,0:T(8,128)(2,1)}, u32[]{:S(2)}, u32[]{:S(2)}) collective-permute-start(bf16[256,1024]{1,0:T(8,128)(2,1)S(1)} %collective-permute-done.5.refs_2_), channel_id=1, source_target_pairs={{0,32},{32,0},{1,33},{33,1},{2,34},{34,2},{3,35},{35,3},{4,36},{36... | collective-permute-start | bytes 1572872 | tf_op jit(solution)/shard_map/ppermute | solution.py:132
  62.3 18.3 %copy-start.12 = (s32[1,8]{1,0:T(1,128)S(1)}, s32[1,8]{1,0:T(1,128)}, u32[]{:S(2)}) copy-start(s32[1,8]{1,0:T(1,128)} %ids.1) | copy-start | bytes 100
  62.4 8.7 %copy-start.4 = (bf16[256,1024]{1,0:T(8,128)(2,1)}, bf16[256,1024]{1,0:T(8,128)(2,1)S(1)}, u32[]{:S(2)}) copy-start(bf16[256,1024]{1,0:T(8,128)(2,1)S(1)} %collective-permute-done.4.refs_1_) | copy-start | bytes 1572868
  62.4 8.7 %copy-start.6 = (bf16[256,1024]{1,0:T(8,128)(2,1)}, bf16[256,1024]{1,0:T(8,128)(2,1)S(1)}, u32[]{:S(2)}) copy-start(bf16[256,1024]{1,0:T(8,128)(2,1)S(1)} %collective-permute-done.10.refs_7_) | copy-start | bytes 1572868
  67.3 1.2 copy-start.8
  68.5 12.1 %copy-start.10 = (bf16[1,256,128]{2,1,0:T(8,128)(2,1)S(1)}, bf16[1,256,128]{2,1,0:T(8,128)(2,1)}, u32[]{:S(2)}) copy-start(bf16[1,256,128]{2,1,0:T(8,128)(2,1)} %param.6) | copy-start | bytes 196612
  68.5 12.1 %copy-start.11 = (bf16[1,256,128]{2,1,0:T(8,128)(2,1)S(1)}, bf16[1,256,128]{2,1,0:T(8,128)(2,1)}, u32[]{:S(2)}) copy-start(bf16[1,256,128]{2,1,0:T(8,128)(2,1)} %param.11) | copy-start | bytes 196612
  71.1 26.1 %copy-start.9 = (bf16[8,256,256]{2,1,0:T(8,128)(2,1)S(1)}, bf16[8,256,256]{2,1,0:T(8,128)(2,1)}, u32[]{:S(2)}) copy-start(bf16[8,256,256]{2,1,0:T(8,128)(2,1)} %all-gather.3.cloned.1.call-done.enc) | copy-start | bytes 3145732
  97.2 5.1 %copy-start.1 = (bf16[256,1024]{1,0:T(8,128)(2,1)S(1)}, bf16[256,1024]{1,0:T(8,128)(2,1)}, u32[]{:S(2)}) copy-start(bf16[256,1024]{1,0:T(8,128)(2,1)} %copy-done) | copy-start | bytes 1572868
  97.2 5.1 %copy-start.3 = (bf16[256,1024]{1,0:T(8,128)(2,1)S(1)}, bf16[256,1024]{1,0:T(8,128)(2,1)}, u32[]{:S(2)}) copy-start(bf16[256,1024]{1,0:T(8,128)(2,1)} %copy-done.2) | copy-start | bytes 1572868
  97.2 5.1 %copy-start.5 = (bf16[256,1024]{1,0:T(8,128)(2,1)S(1)}, bf16[256,1024]{1,0:T(8,128)(2,1)}, u32[]{:S(2)}) copy-start(bf16[256,1024]{1,0:T(8,128)(2,1)} %copy-done.4) | copy-start | bytes 1572868
  97.2 5.1 %copy-start.7 = (bf16[256,1024]{1,0:T(8,128)(2,1)S(1)}, bf16[256,1024]{1,0:T(8,128)(2,1)}, u32[]{:S(2)}) copy-start(bf16[256,1024]{1,0:T(8,128)(2,1)} %copy-done.6) | copy-start | bytes 1572868
  100.4 6.4 %collective-permute-start.11 = (bf16[16,256,256]{2,1,0:T(8,128)(2,1)}, bf16[16,256,256]{2,1,0:T(8,128)(2,1)}, u32[]{:S(2)}, u32[]{:S(2)}) collective-permute-start(bf16[16,256,256]{2,1,0:T(8,128)(2,1)} %get-tuple-element.14), channel_id=1, source_target_pairs={{0,32},{32,0},{1,33},{33,1},{2,34},{34,2},{3,35},{35,3},{4,36},{36... | collective-permute-start | bytes 6291464 | tf_op jit(solution)/shard_map/ppermute | solution.py:132
  109.1 22.2 %collective-permute-start.12 = (bf16[2,256,256]{2,1,0:T(8,128)(2,1)S(1)}, bf16[2,256,256]{2,1,0:T(8,128)(2,1)S(1)}, u32[]{:S(2)}, u32[]{:S(2)}) collective-permute-start(bf16[2,256,256]{2,1,0:T(8,128)(2,1)S(1)} %get-tuple-element.15), channel_id=1, source_target_pairs={{0,64},{64,0},{128,192},{192,128},{256,320},{320,256},{384,448},{4... | collective-permute-start | bytes 786440 | tf_op jit(solution)/shard_map/ppermute | solution.py:169
  114.5 18.8 %collective-permute-start.18 = (bf16[2,256,256]{2,1,0:T(8,128)(2,1)S(1)}, bf16[2,256,256]{2,1,0:T(8,128)(2,1)S(1)}, u32[]{:S(2)}, u32[]{:S(2)}) collective-permute-start(bf16[2,256,256]{2,1,0:T(8,128)(2,1)S(1)} %get-tuple-element.16), channel_id=1, source_target_pairs={{0,448},{64,384},{128,320},{192,256},{256,192},{320,128},{384,64},... | collective-permute-start | bytes 786440 | tf_op jit(solution)/shard_map/ppermute | solution.py:169
  118.1 23.4 %collective-permute-start.17 = (bf16[2,256,256]{2,1,0:T(8,128)(2,1)S(1)}, bf16[2,256,256]{2,1,0:T(8,128)(2,1)S(1)}, u32[]{:S(2)}, u32[]{:S(2)}) collective-permute-start(bf16[2,256,256]{2,1,0:T(8,128)(2,1)S(1)} %get-tuple-element.17), channel_id=1, source_target_pairs={{0,384},{64,448},{128,256},{192,320},{256,128},{320,192},{384,0},{... | collective-permute-start | bytes 786440 | tf_op jit(solution)/shard_map/ppermute | solution.py:169
  121.1 20.5 %collective-permute-start.16 = (bf16[2,256,256]{2,1,0:T(8,128)(2,1)S(1)}, bf16[2,256,256]{2,1,0:T(8,128)(2,1)S(1)}, u32[]{:S(2)}, u32[]{:S(2)}) collective-permute-start(bf16[2,256,256]{2,1,0:T(8,128)(2,1)S(1)} %get-tuple-element.18), channel_id=1, source_target_pairs={{0,320},{64,256},{128,448},{192,384},{256,64},{320,0},{384,192},{4... | collective-permute-start | bytes 786440 | tf_op jit(solution)/shard_map/ppermute | solution.py:169
  124.8 21.1 %collective-permute-start.15 = (bf16[2,256,256]{2,1,0:T(8,128)(2,1)S(1)}, bf16[2,256,256]{2,1,0:T(8,128)(2,1)S(1)}, u32[]{:S(2)}, u32[]{:S(2)}) collective-permute-start(bf16[2,256,256]{2,1,0:T(8,128)(2,1)S(1)} %get-tuple-element.19), channel_id=1, source_target_pairs={{0,256},{64,320},{128,384},{192,448},{256,0},{320,64},{384,128},{4... | collective-permute-start | bytes 786440 | tf_op jit(solution)/shard_map/ppermute | solution.py:169
  131.4 14.6 %collective-permute-start.14 = (bf16[2,256,256]{2,1,0:T(8,128)(2,1)S(1)}, bf16[2,256,256]{2,1,0:T(8,128)(2,1)S(1)}, u32[]{:S(2)}, u32[]{:S(2)}) collective-permute-start(bf16[2,256,256]{2,1,0:T(8,128)(2,1)S(1)} %get-tuple-element.20), channel_id=1, source_target_pairs={{0,192},{64,128},{128,64},{192,0},{256,448},{320,384},{384,320},{4... | collective-permute-start | bytes 786440 | tf_op jit(solution)/shard_map/ppermute | solution.py:169
  133.3 17.5 %collective-permute-start.13 = (bf16[2,256,256]{2,1,0:T(8,128)(2,1)S(1)}, bf16[2,256,256]{2,1,0:T(8,128)(2,1)S(1)}, u32[]{:S(2)}, u32[]{:S(2)}) collective-permute-start(bf16[2,256,256]{2,1,0:T(8,128)(2,1)S(1)} %get-tuple-element.21), channel_id=1, source_target_pairs={{0,128},{64,192},{128,0},{192,64},{256,384},{320,448},{384,256},{4... | collective-permute-start | bytes 786440 | tf_op jit(solution)/shard_map/ppermute | solution.py:169
  151.1 11.7 %collective-permute-start.20 = (bf16[256,256]{1,0:T(8,128)(2,1)S(1)}, bf16[256,256]{1,0:T(8,128)(2,1)S(1)}, u32[]{:S(2)}, u32[]{:S(2)}) collective-permute-start(bf16[256,256]{1,0:T(8,128)(2,1)S(1)} %get-tuple-element.26), channel_id=1, source_target_pairs={{1,0},{0,1},{385,16},{384,17},{129,128},{128,129},{257,144},{256,1... | collective-permute-start | bytes 393224 | tf_op jit(solution)/shard_map/ppermute | solution.py:186
  154.8 10.8 %collective-permute-start.19 = (bf16[256,256]{1,0:T(8,128)(2,1)S(1)}, bf16[256,256]{1,0:T(8,128)(2,1)S(1)}, u32[]{:S(2)}, u32[]{:S(2)}) collective-permute-start(bf16[256,256]{1,0:T(8,128)(2,1)S(1)} %get-tuple-element.27), channel_id=1, source_target_pairs={{0,0},{1,1},{384,16},{385,17},{128,128},{129,129},{256,144},{257,1... | collective-permute-start | bytes 393224 | tf_op jit(solution)/shard_map/ppermute | solution.py:186
Sparse Core Ops, SparseCore 0:
  10.1 57.1 all-gather.2
  106.1 54.3 reduce-scatter.1

commit v3 on v2

--- a/solution.py
+++ b/solution.py
@@ -161,12 +161,19 @@
 ]
 
 
+def add(*parts):
+    total = parts[0].astype(F32)
+    for part in parts[1:]:
+        total = total + part.astype(F32)
+    return total.astype(BF16)
+
+
 def send(x, pairs):
     return lax.ppermute(x, Y_AXES, pairs)
 
 
 def hop(x, by):
-    return lax.ppermute(x, SENDERS, [(i, i ^ by) for i in range(8)])
+    return lax.ppermute(x, ("yh", "yl"), [(i, i ^ by) for i in range(4)])
 
 
 def turned(flip):
@@ -256,12 +263,9 @@
         weight_grad_body, (part, part), 1, 2, flops=flops, bytes_accessed=moved
     )(me, enc, grads)
     near = (near.astype(F32) + swap(far, "c").astype(F32)).astype(BF16)
-    near = near.reshape(8, 2, BLOCK, WIDE)
-    parts = [near[0]] + [hop(near[k], k) for k in range(1, 8)]
-    total = parts[0].astype(F32)
-    for part in parts[1:]:
-        total = total + part.astype(F32)
-    total = total.astype(BF16)
+    near = near.reshape(4, 4, BLOCK, WIDE)
+    near = add(near[0], hop(near[1], 1), hop(near[2], 2), hop(near[3], 3))
+    total = add(near[:2], swap(near[2:], "xh"))
     kept, given = turn_back(total[0], 0), turn_back(total[1], 1)
     upper, lower = jnp.where(even, kept, given), jnp.where(even, given, kept)
     weight_grad = jnp.concatenate([upper, lower], axis=0)

time: 175 us -> 174 us (level)
  starting transfers between devices: 72.4 us -> 59.4 us
  waiting for transfers between devices: 45 us -> 57.2 us
    ppermute x7 -> x3, starting transfers between devices: 27.5 us -> 9.82 us  [hop(): return lax.ppermute(x, ('yh', 'yl'), [(i, i ^ by) for i in range(4)])]
    ppermute x7 -> x3, waiting for transfers between devices: 14.1 us -> 21.1 us  [hop(): return lax.ppermute(x, ('yh', 'yl'), [(i, i ^ by) for i in range(4)])]
    ppermute x7 -> x8, waiting for transfers between devices: 9.3 us -> 15.3 us  [swap(): return lax.ppermute(x, axis, [(0, 1), (1, 0)])]
    ppermute x7 -> x8, starting transfers between devices: 20.7 us -> 25.4 us  [swap(): return lax.ppermute(x, axis, [(0, 1), (1, 0)])]
  transfers between devices with their start and end apart: 23 -> 20, of which waited for: 13 -> 13; matrix products, arithmetic and copies ran while one was open for 3% -> 3% of each run, Pallas kernels for 2% -> 2%
where the time goes in v3:
time: 174 us; the launch traced here: 172 us
  starting transfers between devices  59.4 us (34%)
  waiting for transfers between devices  57.2 us (33%)
  blocking collectives  23.3 us (13%)
  between operations  14.4 us (8%)
  Pallas kernels  12.1 us (7%)
  other arithmetic  3.45 us (2%)
  local copies, waits for them, and re-layouts  2.46 us (1%)
    ppermute x8, starting transfers between devices, swap(): return lax.ppermute(x, axis, [(0, 1), (1, 0)])  25.4 us
    ppermute x3, waiting for transfers between devices, hop(): return lax.ppermute(x, ('yh', 'yl'), [(i, i ^ by) for i in range(4)])  21.1 us
    ppermute x8, waiting for transfers between devices, swap(): return lax.ppermute(x, axis, [(0, 1), (1, 0)])  15.3 us
    all_gather x1, blocking collectives, per_device(): grads = lax.all_gather(grad_own, ('z0', 's'), axis=0, tiled=False)  13.8 us
    ppermute x4, starting transfers between devices, send(): return lax.ppermute(x, Y_AXES, pairs)  13.5 us
    ppermute x3, starting transfers between devices, hop(): return lax.ppermute(x, ('yh', 'yl'), [(i, i ^ by) for i in range(4)])  9.82 us
    all_to_all x1, blocking collectives, per_device(): arrived = lax.all_to_all(terms, ('z0', 's'), 0, 0, tiled=True)  9.52 us
    ppermute x2, starting transfers between devices, turn_back(): return lax.ppermute(x, Y_AXES, pairs)  8.67 us
  transfers between devices with their start and end apart: 20, of which 13 were waited for; matrix products, arithmetic and copies ran while one was open for 3% of the time, Pallas kernels for 2%

profile of v3, /device:TPU:6, one launch (start us, length us, event | category | flops | bytes accessed | tf_op | source)
XLA Modules:
  0.0 172.4 jit_solution(13740977120017294326)
XLA Ops:
  7.2 0.7 all-gather.3.cloned.1.call-update
  8.0 1.0 fusion.2
  8.9 0.1 broadcast_select_fusion.3
  9.0 4.1 %collective-permute-start.3 = (bf16[256,256]{1,0:T(8,128)(2,1)S(1)}, bf16[256,256]{1,0:T(8,128)(2,1)S(1)}, u32[]{:S(2)}, u32[]{:S(2)}) collective-permute-start(bf16[256,256]{1,0:T(8,128)(2,1)S(1)} %get-tuple-element.25), channel_id=1, source_target_pairs={{0,385},{16,1},{1,384},{17,0},{128,257},{144,129},{129,256},{145,1... | collective-permute-start | bytes 393224 | tf_op jit(solution)/shard_map/ppermute | solution.py:172
  13.1 5.1 %collective-permute-start.2 = (bf16[256,256]{1,0:T(8,128)(2,1)S(1)}, bf16[256,256]{1,0:T(8,128)(2,1)S(1)}, u32[]{:S(2)}, u32[]{:S(2)}) collective-permute-start(bf16[256,256]{1,0:T(8,128)(2,1)S(1)} %get-tuple-element.25), channel_id=1, source_target_pairs={{0,1},{16,385},{1,0},{17,384},{128,129},{144,257},{129,128},{145,2... | collective-permute-start | bytes 393224 | tf_op jit(solution)/shard_map/ppermute | solution.py:172
  18.2 2.4 %collective-permute-start.1 = (bf16[256,256]{1,0:T(8,128)(2,1)S(1)}, bf16[256,256]{1,0:T(8,128)(2,1)S(1)}, u32[]{:S(2)}, u32[]{:S(2)}) collective-permute-start(bf16[256,256]{1,0:T(8,128)(2,1)S(1)} %get-tuple-element.24), channel_id=1, source_target_pairs={{16,384},{17,385},{144,256},{145,257},{256,144},{257,145},{384,16}... | collective-permute-start | bytes 393224 | tf_op jit(solution)/shard_map/ppermute | solution.py:172
  20.6 1.9 %collective-permute-start = (bf16[256,256]{1,0:T(8,128)(2,1)S(1)}, bf16[256,256]{1,0:T(8,128)(2,1)S(1)}, u32[]{:S(2)}, u32[]{:S(2)}) collective-permute-start(bf16[256,256]{1,0:T(8,128)(2,1)S(1)} %get-tuple-element.24), channel_id=1, source_target_pairs={{0,384},{16,0},{1,385},{17,1},{128,256},{144,128},{129,257},{145,1... | collective-permute-start | bytes 393224 | tf_op jit(solution)/shard_map/ppermute | solution.py:172
  22.5 0.4 collective-permute-done.2
  23.0 5.4 %collective-permute-done.1 = bf16[256,256]{1,0:T(8,128)(2,1)S(1)} collective-permute-done((bf16[256,256]{1,0:T(8,128)(2,1)S(1)}, bf16[256,256]{1,0:T(8,128)(2,1)S(1)}, u32[]{:S(2)}, u32[]{:S(2)}) %collective-permute-start.1) | collective-permute-done | bytes 131104 | tf_op jit(solution)/shard_map/ppermute | solution.py:172
  28.3 1.4 collective-permute-done
  29.8 0.1 pad_maximum_fusion.refs_0_
  29.9 1.9 %collective-permute-start.9 = (bf16[256,1024]{1,0:T(8,128)(2,1)S(1)}, bf16[256,1024]{1,0:T(8,128)(2,1)S(1)}, u32[]{:S(2)}, u32[]{:S(2)}) collective-permute-start(bf16[256,1024]{1,0:T(8,128)(2,1)S(1)} %pad_maximum_fusion.refs_0_), channel_id=1, source_target_pairs={{0,192},{64,128},{128,64},{192,0},{1,193},{65,129},{129,65},{193,1... | collective-permute-start | bytes 1572872 | tf_op jit(solution)/shard_map/ppermute | solution.py:136
  31.8 8.8 %collective-permute-start.7 = (bf16[256,1024]{1,0:T(8,128)(2,1)S(1)}, bf16[256,1024]{1,0:T(8,128)(2,1)S(1)}, u32[]{:S(2)}, u32[]{:S(2)}) collective-permute-start(bf16[256,1024]{1,0:T(8,128)(2,1)S(1)} %pad_maximum_fusion.refs_0_), channel_id=1, source_target_pairs={{0,128},{128,0},{1,129},{129,1},{2,130},{130,2},{3,131},{131,3},{4... | collective-permute-start | bytes 1572872 | tf_op jit(solution)/shard_map/ppermute | solution.py:132
  40.5 1.9 %collective-permute-start.5 = (bf16[256,1024]{1,0:T(8,128)(2,1)S(1)}, bf16[256,1024]{1,0:T(8,128)(2,1)S(1)}, u32[]{:S(2)}, u32[]{:S(2)}) collective-permute-start(bf16[256,1024]{1,0:T(8,128)(2,1)S(1)} %pad_maximum_fusion.refs_0_), channel_id=1, source_target_pairs={{0,64},{64,0},{1,65},{65,1},{2,66},{66,2},{3,67},{67,3},{4,68},{68... | collective-permute-start | bytes 1572872 | tf_op jit(solution)/shard_map/ppermute | solution.py:132
  42.5 1.9 %collective-permute-start.4 = (bf16[256,1024]{1,0:T(8,128)(2,1)S(1)}, bf16[256,1024]{1,0:T(8,128)(2,1)S(1)}, u32[]{:S(2)}, u32[]{:S(2)}) collective-permute-start(bf16[256,1024]{1,0:T(8,128)(2,1)S(1)} %pad_maximum_fusion.refs_0_), channel_id=1, source_target_pairs={{0,32},{32,0},{1,33},{33,1},{2,34},{34,2},{3,35},{35,3},{4,36},{36... | collective-permute-start | bytes 1572872 | tf_op jit(solution)/shard_map/ppermute | solution.py:132
  44.4 4.7 %collective-permute-done.9.refs_6_ = bf16[256,1024]{1,0:T(8,128)(2,1)S(1)} collective-permute-done((bf16[256,1024]{1,0:T(8,128)(2,1)S(1)}, bf16[256,1024]{1,0:T(8,128)(2,1)S(1)}, u32[]{:S(2)}, u32[]{:S(2)}) %collective-permute-start.9) | collective-permute-done | bytes 524320 | tf_op jit(solution)/shard_map/ppermute | solution.py:136
  49.1 1.9 %collective-permute-start.10 = (bf16[256,1024]{1,0:T(8,128)(2,1)S(1)}, bf16[256,1024]{1,0:T(8,128)(2,1)S(1)}, u32[]{:S(2)}, u32[]{:S(2)}) collective-permute-start(bf16[256,1024]{1,0:T(8,128)(2,1)S(1)} %collective-permute-done.9.refs_6_), channel_id=1, source_target_pairs={{0,32},{32,0},{1,33},{33,1},{2,34},{34,2},{3,35},{35,3},{4,36},{36... | collective-permute-start | bytes 1572872 | tf_op jit(solution)/shard_map/ppermute | solution.py:132
  51.0 7.0 %collective-permute-done.7.refs_4_ = bf16[256,1024]{1,0:T(8,128)(2,1)S(1)} collective-permute-done((bf16[256,1024]{1,0:T(8,128)(2,1)S(1)}, bf16[256,1024]{1,0:T(8,128)(2,1)S(1)}, u32[]{:S(2)}, u32[]{:S(2)}) %collective-permute-start.7) | collective-permute-done | bytes 524320 | tf_op jit(solution)/shard_map/ppermute | solution.py:132
  57.9 1.9 %collective-permute-start.8 = (bf16[256,1024]{1,0:T(8,128)(2,1)S(1)}, bf16[256,1024]{1,0:T(8,128)(2,1)}, u32[]{:S(2)}, u32[]{:S(2)}) collective-permute-start(bf16[256,1024]{1,0:T(8,128)(2,1)S(1)} %collective-permute-done.7.refs_4_), channel_id=1, source_target_pairs={{0,32},{32,0},{1,33},{33,1},{2,34},{34,2},{3,35},{35,3},{4,36},{36... | collective-permute-start | bytes 1572872 | tf_op jit(solution)/shard_map/ppermute | solution.py:132
  59.9 2.4 %collective-permute-start.6 = (bf16[256,1024]{1,0:T(8,128)(2,1)S(1)}, bf16[256,1024]{1,0:T(8,128)(2,1)}, u32[]{:S(2)}, u32[]{:S(2)}) collective-permute-start(bf16[256,1024]{1,0:T(8,128)(2,1)S(1)} %collective-permute-done.5.refs_2_), channel_id=1, source_target_pairs={{0,32},{32,0},{1,33},{33,1},{2,34},{34,2},{3,35},{35,3},{4,36},{36... | collective-permute-start | bytes 1572872 | tf_op jit(solution)/shard_map/ppermute | solution.py:132
  62.3 0.1 stack.23.me
  62.4 1.5 collective-permute-done.6.refs_3_
  63.9 3.3 %all-gather.3.cloned.1.call-done.enc = bf16[8,256,256]{2,1,0:T(8,128)(2,1)} async-done(((bf16[1,256,256]{2,1,0:T(8,128)(2,1)}), bf16[8,256,256]{2,1,0:T(8,128)(2,1)}) %all-gather.3.cloned.1.call-update) | async-done | bytes 1048592 | tf_op jit(solution)/shard_map/all_gather | solution.py:197
  67.3 1.2 copy-done.8
  68.5 2.5 %shard_map.101 = bf16[4,256,256]{2,1,0:T(8,128)(2,1)S(1)} custom-call(s32[5]{0:T(128)S(1)} %stack.23.me, bf16[8,256,256]{2,1,0:T(8,128)(2,1)S(1)} %copy-done.8, bf16[256,1024]{1,0:T(8,128)(2,1)S(1)} %pad_maximum_fusion.refs_0_, bf16[256,1024]{1,0:T(8,128)(2,1)S(1)} %collective-permute-done.4.refs_1_, bf16[256,1024]{1,0:T(8,128)(2,1)S(1)} %collective-permute-done.5.refs_2_, ...), custom_call_target="tpu_custom_call" | custom-call | flops 1073741824 | bytes 5242880 | tf_op jit(solution)/shard_map/pallas_call | solution.py:230
  71.1 9.5 %all_to_all.5.arrived = bf16[4,256,256]{2,1,0:T(8,128)(2,1)S(1)} all-to-all(bf16[4,256,256]{2,1,0:T(8,128)(2,1)S(1)} %shard_map.101), channel_id=1, replica_groups=mesh['yh'=2,'yl'=2,'xh'=2,'c'=2,'s'=2,'zr'=8,'z0'=2] {'z0','s'}, dimensions={0} | all-to-all | bytes 1048576 | tf_op jit(solution)/shard_map/all_to_all | solution.py:233
  80.6 2.8 %shard_map.102 = (bf16[256,128]{1,0:T(8,128)(2,1)}, bf16[256,128]{1,0:T(8,128)(2,1)}, bf16[256,256]{1,0:T(8,128)(2,1)S(1)}) custom-call(s32[1,8]{1,0:T(1,128)S(1)} %copy-done.12, bf16[4,256,256]{2,1,0:T(8,128)(2,1)S(1)} %all_to_all.5.arrived, bf16[256,128]{1,0:T(8,128)(2,1)S(1)} %bitcast.16, bf16[256,128]{1,0:T(8,128)(2,1)S(1)} %bitcast.17), custom_call_target="tpu_custom_call" | custom-call | flops 25165824 | bytes 1048576 | tf_op jit(solution)/shard_map/pallas_call | solution.py:236
  83.4 13.8 %all-gather = bf16[1024,256]{1,0:T(8,128)(2,1)S(1)} all-gather(bf16[256,256]{1,0:T(8,128)(2,1)S(1)} %get-tuple-element.12), channel_id=2, replica_groups=mesh['yh'=2,'yl'=2,'xh'=2,'c'=2,'s'=2,'zr'=8,'z0'=2] {'z0','s'}, dimensions={0}, use_global_device_ids=true | all-gather | bytes 655360 | tf_op jit(solution)/shard_map/all_gather | solution.py:249
  97.2 3.2 %shard_map.104 = (bf16[16,256,256]{2,1,0:T(8,128)(2,1)S(1)}, bf16[16,256,256]{2,1,0:T(8,128)(2,1)}) custom-call(s32[5]{0:T(128)S(1)} %stack.23.me, bf16[8,256,256]{2,1,0:T(8,128)(2,1)S(1)} %copy-done.9, bf16[4,256,256]{2,1,0:T(8,128)(2,1)S(1)} %bitcast.14), custom_call_target="tpu_custom_call" | custom-call | flops 1073741824 | bytes 5242880 | tf_op jit(solution)/shard_map/pallas_call | solution.py:262
  100.4 1.9 %collective-permute-start.11 = (bf16[16,256,256]{2,1,0:T(8,128)(2,1)}, bf16[16,256,256]{2,1,0:T(8,128)(2,1)}, u32[]{:S(2)}, u32[]{:S(2)}) collective-permute-start(bf16[16,256,256]{2,1,0:T(8,128)(2,1)} %get-tuple-element.14), channel_id=1, source_target_pairs={{0,32},{32,0},{1,33},{33,1},{2,34},{34,2},{3,35},{35,3},{4,36},{36... | collective-permute-start | bytes 6291464 | tf_op jit(solution)/shard_map/ppermute | solution.py:132
  102.4 3.6 %shard_map.103 = bf16[8,256,256]{2,1,0:T(8,128)(2,1)} custom-call(s32[5]{0:T(128)S(1)} %stack.23.me, bf16[4,256,256]{2,1,0:T(8,128)(2,1)S(1)} %bitcast.15, bf16[256,1024]{1,0:T(8,128)(2,1)S(1)} %pad_maximum_fusion.refs_0_, bf16[256,1024]{1,0:T(8,128)(2,1)S(1)} %copy-done.5, bf16[256,1024]{1,0:T(8,128)(2,1)S(1)} %copy-done.3, ...), custom_call_target="tpu_custom_call" | custom-call | flops 1073741824 | bytes 5242880 | tf_op jit(solution)/shard_map/pallas_call | solution.py:251
  106.0 0.8 collective-permute-done.11
  106.8 2.2 %add_convert_fusion = bf16[16,256,256]{2,1,0:T(8,128)(2,1)S(1)} fusion(bf16[16,256,256]{2,1,0:T(8,128)(2,1)} %collective-permute-done.11, bf16[16,256,256]{2,1,0:T(8,128)(2,1)S(1)} %get-tuple-element.13), kind=kLoop, calls=%fused_computation | loop fusion | flops 4194304 | bytes 6291456 | tf_op jit(solution)/shard_map/convert_element_type | solution.py:265
  109.0 0.1 fusion.1
  109.1 2.9 %collective-permute-start.12 = (bf16[4,256,256]{2,1,0:T(8,128)(2,1)S(1)}, bf16[4,256,256]{2,1,0:T(8,128)(2,1)S(1)}, u32[]{:S(2)}, u32[]{:S(2)}) collective-permute-start(bf16[4,256,256]{2,1,0:T(8,128)(2,1)S(1)} %get-tuple-element.15), channel_id=1, source_target_pairs={{0,128},{128,0},{256,384},{384,256},{1,129},{129,1},{257,385},{385... | collective-permute-start | bytes 1572872 | tf_op jit(solution)/shard_map/ppermute | solution.py:176
  112.1 3.7 %collective-permute-start.14 = (bf16[4,256,256]{2,1,0:T(8,128)(2,1)S(1)}, bf16[4,256,256]{2,1,0:T(8,128)(2,1)S(1)}, u32[]{:S(2)}, u32[]{:S(2)}) collective-permute-start(bf16[4,256,256]{2,1,0:T(8,128)(2,1)S(1)} %get-tuple-element.16), channel_id=1, source_target_pairs={{0,384},{128,256},{256,128},{384,0},{1,385},{129,257},{257,129},{3... | collective-permute-start | bytes 1572872 | tf_op jit(solution)/shard_map/ppermute | solution.py:176
  115.8 3.2 %collective-permute-start.13 = (bf16[4,256,256]{2,1,0:T(8,128)(2,1)S(1)}, bf16[4,256,256]{2,1,0:T(8,128)(2,1)S(1)}, u32[]{:S(2)}, u32[]{:S(2)}) collective-permute-start(bf16[4,256,256]{2,1,0:T(8,128)(2,1)S(1)} %get-tuple-element.17), channel_id=1, source_target_pairs={{0,256},{128,384},{256,0},{384,128},{1,257},{129,385},{257,1},{385... | collective-permute-start | bytes 1572872 | tf_op jit(solution)/shard_map/ppermute | solution.py:176
  119.0 6.8 %collective-permute-done.12 = bf16[4,256,256]{2,1,0:T(8,128)(2,1)S(1)} collective-permute-done((bf16[4,256,256]{2,1,0:T(8,128)(2,1)S(1)}, bf16[4,256,256]{2,1,0:T(8,128)(2,1)S(1)}, u32[]{:S(2)}, u32[]{:S(2)}) %collective-permute-start.12) | collective-permute-done | bytes 524320 | tf_op jit(solution)/shard_map/ppermute | solution.py:176
  125.8 14.3 %collective-permute-done.14 = bf16[4,256,256]{2,1,0:T(8,128)(2,1)S(1)} collective-permute-done((bf16[4,256,256]{2,1,0:T(8,128)(2,1)S(1)}, bf16[4,256,256]{2,1,0:T(8,128)(2,1)S(1)}, u32[]{:S(2)}, u32[]{:S(2)}) %collective-permute-start.14) | collective-permute-done | bytes 524320 | tf_op jit(solution)/shard_map/ppermute | solution.py:176
  140.1 0.3 add_convert_fusion.1
  140.4 4.6 %collective-permute-start.15 = (bf16[2,256,256]{2,1,0:T(8,128)(2,1)S(1)}, bf16[2,256,256]{2,1,0:T(8,128)(2,1)S(1)}, u32[]{:S(2)}, u32[]{:S(2)}) collective-permute-start(bf16[2,256,256]{2,1,0:T(8,128)(2,1)S(1)} %slice.65), channel_id=1, source_target_pairs={{0,64},{64,0},{1,65},{65,1},{2,66},{66,2},{3,67},{67,3},{4,68},{68... | collective-permute-start | bytes 786440 | tf_op jit(solution)/shard_map/ppermute | solution.py:132
  145.0 6.0 %collective-permute-done.15 = bf16[2,256,256]{2,1,0:T(8,128)(2,1)S(1)} collective-permute-done((bf16[2,256,256]{2,1,0:T(8,128)(2,1)S(1)}, bf16[2,256,256]{2,1,0:T(8,128)(2,1)S(1)}, u32[]{:S(2)}, u32[]{:S(2)}) %collective-permute-start.15) | collective-permute-done | bytes 262176 | tf_op jit(solution)/shard_map/ppermute | solution.py:132
  151.0 0.1 add_convert_fusion.2
  151.1 4.7 %collective-permute-start.17 = (bf16[256,256]{1,0:T(8,128)(2,1)S(1)}, bf16[256,256]{1,0:T(8,128)(2,1)S(1)}, u32[]{:S(2)}, u32[]{:S(2)}) collective-permute-start(bf16[256,256]{1,0:T(8,128)(2,1)S(1)} %get-tuple-element.22), channel_id=1, source_target_pairs={{1,0},{0,1},{385,16},{384,17},{129,128},{128,129},{257,144},{256,1... | collective-permute-start | bytes 393224 | tf_op jit(solution)/shard_map/ppermute | solution.py:193
  155.8 4.0 %collective-permute-start.16 = (bf16[256,256]{1,0:T(8,128)(2,1)S(1)}, bf16[256,256]{1,0:T(8,128)(2,1)S(1)}, u32[]{:S(2)}, u32[]{:S(2)}) collective-permute-start(bf16[256,256]{1,0:T(8,128)(2,1)S(1)} %get-tuple-element.23), channel_id=1, source_target_pairs={{0,0},{1,1},{384,16},{385,17},{128,128},{129,129},{256,144},{257,1... | collective-permute-start | bytes 393224 | tf_op jit(solution)/shard_map/ppermute | solution.py:193
  159.8 2.4 %collective-permute-done.17 = bf16[256,256]{1,0:T(8,128)(2,1)S(1)} collective-permute-done((bf16[256,256]{1,0:T(8,128)(2,1)S(1)}, bf16[256,256]{1,0:T(8,128)(2,1)S(1)}, u32[]{:S(2)}, u32[]{:S(2)}) %collective-permute-start.17) | collective-permute-done | bytes 131104 | tf_op jit(solution)/shard_map/ppermute | solution.py:193
  162.2 2.6 %collective-permute-done.16 = bf16[256,256]{1,0:T(8,128)(2,1)S(1)} collective-permute-done((bf16[256,256]{1,0:T(8,128)(2,1)S(1)}, bf16[256,256]{1,0:T(8,128)(2,1)S(1)}, u32[]{:S(2)}, u32[]{:S(2)}) %collective-permute-start.16) | collective-permute-done | bytes 131104 | tf_op jit(solution)/shard_map/ppermute | solution.py:193
  164.8 0.7 pad_maximum_fusion.1
  (40 shorter events, 0.3 us)
Async XLA Ops:
  7.2 60.1 %all-gather.3.cloned.1.call-start = ((), (), s32[]{:S(2)}) async-start(), calls=%async_computation.2 | async-start | bytes 1179648 | tf_op jit(solution)/shard_map/all_gather | solution.py:197
  7.9 157.6 %reduce-scatter.2.cloned.1.call-start = ((), (), s32[]{:S(2)}) async-start(), calls=%async_computation.3 | async-start | bytes 1179648 | tf_op jit(solution)/shard_map/reduce_scatter | solution.py:259
  9.0 13.6 %collective-permute-start.3 = (bf16[256,256]{1,0:T(8,128)(2,1)S(1)}, bf16[256,256]{1,0:T(8,128)(2,1)S(1)}, u32[]{:S(2)}, u32[]{:S(2)}) collective-permute-start(bf16[256,256]{1,0:T(8,128)(2,1)S(1)} %get-tuple-element.25), channel_id=1, source_target_pairs={{0,385},{16,1},{1,384},{17,0},{128,257},{144,129},{129,256},{145,1... | collective-permute-start | bytes 393224 | tf_op jit(solution)/shard_map/ppermute | solution.py:172
  13.1 9.9 %collective-permute-start.2 = (bf16[256,256]{1,0:T(8,128)(2,1)S(1)}, bf16[256,256]{1,0:T(8,128)(2,1)S(1)}, u32[]{:S(2)}, u32[]{:S(2)}) collective-permute-start(bf16[256,256]{1,0:T(8,128)(2,1)S(1)} %get-tuple-element.25), channel_id=1, source_target_pairs={{0,1},{16,385},{1,0},{17,384},{128,129},{144,257},{129,128},{145,2... | collective-permute-start | bytes 393224 | tf_op jit(solution)/shard_map/ppermute | solution.py:172
  18.2 10.1 %collective-permute-start.1 = (bf16[256,256]{1,0:T(8,128)(2,1)S(1)}, bf16[256,256]{1,0:T(8,128)(2,1)S(1)}, u32[]{:S(2)}, u32[]{:S(2)}) collective-permute-start(bf16[256,256]{1,0:T(8,128)(2,1)S(1)} %get-tuple-element.24), channel_id=1, source_target_pairs={{16,384},{17,385},{144,256},{145,257},{256,144},{257,145},{384,16}... | collective-permute-start | bytes 393224 | tf_op jit(solution)/shard_map/ppermute | solution.py:172
  20.6 9.2 %collective-permute-start = (bf16[256,256]{1,0:T(8,128)(2,1)S(1)}, bf16[256,256]{1,0:T(8,128)(2,1)S(1)}, u32[]{:S(2)}, u32[]{:S(2)}) collective-permute-start(bf16[256,256]{1,0:T(8,128)(2,1)S(1)} %get-tuple-element.24), channel_id=1, source_target_pairs={{0,384},{16,0},{1,385},{17,1},{128,256},{144,128},{129,257},{145,1... | collective-permute-start | bytes 393224 | tf_op jit(solution)/shard_map/ppermute | solution.py:172
  29.9 19.2 %collective-permute-start.9 = (bf16[256,1024]{1,0:T(8,128)(2,1)S(1)}, bf16[256,1024]{1,0:T(8,128)(2,1)S(1)}, u32[]{:S(2)}, u32[]{:S(2)}) collective-permute-start(bf16[256,1024]{1,0:T(8,128)(2,1)S(1)} %pad_maximum_fusion.refs_0_), channel_id=1, source_target_pairs={{0,192},{64,128},{128,64},{192,0},{1,193},{65,129},{129,65},{193,1... | collective-permute-start | bytes 1572872 | tf_op jit(solution)/shard_map/ppermute | solution.py:136
  31.8 26.2 %collective-permute-start.7 = (bf16[256,1024]{1,0:T(8,128)(2,1)S(1)}, bf16[256,1024]{1,0:T(8,128)(2,1)S(1)}, u32[]{:S(2)}, u32[]{:S(2)}) collective-permute-start(bf16[256,1024]{1,0:T(8,128)(2,1)S(1)} %pad_maximum_fusion.refs_0_), channel_id=1, source_target_pairs={{0,128},{128,0},{1,129},{129,1},{2,130},{130,2},{3,131},{131,3},{4... | collective-permute-start | bytes 1572872 | tf_op jit(solution)/shard_map/ppermute | solution.py:132
  40.5 19.3 %collective-permute-start.5 = (bf16[256,1024]{1,0:T(8,128)(2,1)S(1)}, bf16[256,1024]{1,0:T(8,128)(2,1)S(1)}, u32[]{:S(2)}, u32[]{:S(2)}) collective-permute-start(bf16[256,1024]{1,0:T(8,128)(2,1)S(1)} %pad_maximum_fusion.refs_0_), channel_id=1, source_target_pairs={{0,64},{64,0},{1,65},{65,1},{2,66},{66,2},{3,67},{67,3},{4,68},{68... | collective-permute-start | bytes 1572872 | tf_op jit(solution)/shard_map/ppermute | solution.py:132
  42.5 20.0 %collective-permute-start.4 = (bf16[256,1024]{1,0:T(8,128)(2,1)S(1)}, bf16[256,1024]{1,0:T(8,128)(2,1)S(1)}, u32[]{:S(2)}, u32[]{:S(2)}) collective-permute-start(bf16[256,1024]{1,0:T(8,128)(2,1)S(1)} %pad_maximum_fusion.refs_0_), channel_id=1, source_target_pairs={{0,32},{32,0},{1,33},{33,1},{2,34},{34,2},{3,35},{35,3},{4,36},{36... | collective-permute-start | bytes 1572872 | tf_op jit(solution)/shard_map/ppermute | solution.py:132
  49.1 13.4 %collective-permute-start.10 = (bf16[256,1024]{1,0:T(8,128)(2,1)S(1)}, bf16[256,1024]{1,0:T(8,128)(2,1)S(1)}, u32[]{:S(2)}, u32[]{:S(2)}) collective-permute-start(bf16[256,1024]{1,0:T(8,128)(2,1)S(1)} %collective-permute-done.9.refs_6_), channel_id=1, source_target_pairs={{0,32},{32,0},{1,33},{33,1},{2,34},{34,2},{3,35},{35,3},{4,36},{36... | collective-permute-start | bytes 1572872 | tf_op jit(solution)/shard_map/ppermute | solution.py:132
  57.9 13.1 %copy-start = (bf16[256,1024]{1,0:T(8,128)(2,1)}, bf16[256,1024]{1,0:T(8,128)(2,1)S(1)}, u32[]{:S(2)}) copy-start(bf16[256,1024]{1,0:T(8,128)(2,1)S(1)} %collective-permute-done.7.refs_4_) | copy-start | bytes 1572868
  57.9 4.5 %collective-permute-start.8 = (bf16[256,1024]{1,0:T(8,128)(2,1)S(1)}, bf16[256,1024]{1,0:T(8,128)(2,1)}, u32[]{:S(2)}, u32[]{:S(2)}) collective-permute-start(bf16[256,1024]{1,0:T(8,128)(2,1)S(1)} %collective-permute-done.7.refs_4_), channel_id=1, source_target_pairs={{0,32},{32,0},{1,33},{33,1},{2,34},{34,2},{3,35},{35,3},{4,36},{36... | collective-permute-start | bytes 1572872 | tf_op jit(solution)/shard_map/ppermute | solution.py:132
  59.9 11.2 %copy-start.2 = (bf16[256,1024]{1,0:T(8,128)(2,1)}, bf16[256,1024]{1,0:T(8,128)(2,1)S(1)}, u32[]{:S(2)}) copy-start(bf16[256,1024]{1,0:T(8,128)(2,1)S(1)} %collective-permute-done.5.refs_2_) | copy-start | bytes 1572868
  59.9 4.1 %collective-permute-start.6 = (bf16[256,1024]{1,0:T(8,128)(2,1)S(1)}, bf16[256,1024]{1,0:T(8,128)(2,1)}, u32[]{:S(2)}, u32[]{:S(2)}) collective-permute-start(bf16[256,1024]{1,0:T(8,128)(2,1)S(1)} %collective-permute-done.5.refs_2_), channel_id=1, source_target_pairs={{0,32},{32,0},{1,33},{33,1},{2,34},{34,2},{3,35},{35,3},{4,36},{36... | collective-permute-start | bytes 1572872 | tf_op jit(solution)/shard_map/ppermute | solution.py:132
  62.3 18.3 %copy-start.12 = (s32[1,8]{1,0:T(1,128)S(1)}, s32[1,8]{1,0:T(1,128)}, u32[]{:S(2)}) copy-start(s32[1,8]{1,0:T(1,128)} %ids.1) | copy-start | bytes 100
  62.4 8.7 %copy-start.4 = (bf16[256,1024]{1,0:T(8,128)(2,1)}, bf16[256,1024]{1,0:T(8,128)(2,1)S(1)}, u32[]{:S(2)}) copy-start(bf16[256,1024]{1,0:T(8,128)(2,1)S(1)} %collective-permute-done.4.refs_1_) | copy-start | bytes 1572868
  62.4 8.7 %copy-start.6 = (bf16[256,1024]{1,0:T(8,128)(2,1)}, bf16[256,1024]{1,0:T(8,128)(2,1)S(1)}, u32[]{:S(2)}) copy-start(bf16[256,1024]{1,0:T(8,128)(2,1)S(1)} %collective-permute-done.10.refs_7_) | copy-start | bytes 1572868
  67.3 1.2 copy-start.8
  68.5 12.1 %copy-start.10 = (bf16[1,256,128]{2,1,0:T(8,128)(2,1)S(1)}, bf16[1,256,128]{2,1,0:T(8,128)(2,1)}, u32[]{:S(2)}) copy-start(bf16[1,256,128]{2,1,0:T(8,128)(2,1)} %param.6) | copy-start | bytes 196612
  68.5 12.1 %copy-start.11 = (bf16[1,256,128]{2,1,0:T(8,128)(2,1)S(1)}, bf16[1,256,128]{2,1,0:T(8,128)(2,1)}, u32[]{:S(2)}) copy-start(bf16[1,256,128]{2,1,0:T(8,128)(2,1)} %param.11) | copy-start | bytes 196612
  71.1 26.1 %copy-start.9 = (bf16[8,256,256]{2,1,0:T(8,128)(2,1)S(1)}, bf16[8,256,256]{2,1,0:T(8,128)(2,1)}, u32[]{:S(2)}) copy-start(bf16[8,256,256]{2,1,0:T(8,128)(2,1)} %all-gather.3.cloned.1.call-done.enc) | copy-start | bytes 3145732
  97.2 5.1 %copy-start.1 = (bf16[256,1024]{1,0:T(8,128)(2,1)S(1)}, bf16[256,1024]{1,0:T(8,128)(2,1)}, u32[]{:S(2)}) copy-start(bf16[256,1024]{1,0:T(8,128)(2,1)} %copy-done) | copy-start | bytes 1572868
  97.2 5.1 %copy-start.3 = (bf16[256,1024]{1,0:T(8,128)(2,1)S(1)}, bf16[256,1024]{1,0:T(8,128)(2,1)}, u32[]{:S(2)}) copy-start(bf16[256,1024]{1,0:T(8,128)(2,1)} %copy-done.2) | copy-start | bytes 1572868
  97.2 5.2 %copy-start.5 = (bf16[256,1024]{1,0:T(8,128)(2,1)S(1)}, bf16[256,1024]{1,0:T(8,128)(2,1)}, u32[]{:S(2)}) copy-start(bf16[256,1024]{1,0:T(8,128)(2,1)} %copy-done.4) | copy-start | bytes 1572868
  97.2 5.2 %copy-start.7 = (bf16[256,1024]{1,0:T(8,128)(2,1)S(1)}, bf16[256,1024]{1,0:T(8,128)(2,1)}, u32[]{:S(2)}) copy-start(bf16[256,1024]{1,0:T(8,128)(2,1)} %copy-done.6) | copy-start | bytes 1572868
  100.4 6.4 %collective-permute-start.11 = (bf16[16,256,256]{2,1,0:T(8,128)(2,1)}, bf16[16,256,256]{2,1,0:T(8,128)(2,1)}, u32[]{:S(2)}, u32[]{:S(2)}) collective-permute-start(bf16[16,256,256]{2,1,0:T(8,128)(2,1)} %get-tuple-element.14), channel_id=1, source_target_pairs={{0,32},{32,0},{1,33},{33,1},{2,34},{34,2},{3,35},{35,3},{4,36},{36... | collective-permute-start | bytes 6291464 | tf_op jit(solution)/shard_map/ppermute | solution.py:132
  109.1 16.7 %collective-permute-start.12 = (bf16[4,256,256]{2,1,0:T(8,128)(2,1)S(1)}, bf16[4,256,256]{2,1,0:T(8,128)(2,1)S(1)}, u32[]{:S(2)}, u32[]{:S(2)}) collective-permute-start(bf16[4,256,256]{2,1,0:T(8,128)(2,1)S(1)} %get-tuple-element.15), channel_id=1, source_target_pairs={{0,128},{128,0},{256,384},{384,256},{1,129},{129,1},{257,385},{385... | collective-permute-start | bytes 1572872 | tf_op jit(solution)/shard_map/ppermute | solution.py:176
  112.1 28.0 %collective-permute-start.14 = (bf16[4,256,256]{2,1,0:T(8,128)(2,1)S(1)}, bf16[4,256,256]{2,1,0:T(8,128)(2,1)S(1)}, u32[]{:S(2)}, u32[]{:S(2)}) collective-permute-start(bf16[4,256,256]{2,1,0:T(8,128)(2,1)S(1)} %get-tuple-element.16), channel_id=1, source_target_pairs={{0,384},{128,256},{256,128},{384,0},{1,385},{129,257},{257,129},{3... | collective-permute-start | bytes 1572872 | tf_op jit(solution)/shard_map/ppermute | solution.py:176
  115.8 24.3 %collective-permute-start.13 = (bf16[4,256,256]{2,1,0:T(8,128)(2,1)S(1)}, bf16[4,256,256]{2,1,0:T(8,128)(2,1)S(1)}, u32[]{:S(2)}, u32[]{:S(2)}) collective-permute-start(bf16[4,256,256]{2,1,0:T(8,128)(2,1)S(1)} %get-tuple-element.17), channel_id=1, source_target_pairs={{0,256},{128,384},{256,0},{384,128},{1,257},{129,385},{257,1},{385... | collective-permute-start | bytes 1572872 | tf_op jit(solution)/shard_map/ppermute | solution.py:176
  140.4 10.6 %collective-permute-start.15 = (bf16[2,256,256]{2,1,0:T(8,128)(2,1)S(1)}, bf16[2,256,256]{2,1,0:T(8,128)(2,1)S(1)}, u32[]{:S(2)}, u32[]{:S(2)}) collective-permute-start(bf16[2,256,256]{2,1,0:T(8,128)(2,1)S(1)} %slice.65), channel_id=1, source_target_pairs={{0,64},{64,0},{1,65},{65,1},{2,66},{66,2},{3,67},{67,3},{4,68},{68... | collective-permute-start | bytes 786440 | tf_op jit(solution)/shard_map/ppermute | solution.py:132
  151.1 11.1 %collective-permute-start.17 = (bf16[256,256]{1,0:T(8,128)(2,1)S(1)}, bf16[256,256]{1,0:T(8,128)(2,1)S(1)}, u32[]{:S(2)}, u32[]{:S(2)}) collective-permute-start(bf16[256,256]{1,0:T(8,128)(2,1)S(1)} %get-tuple-element.22), channel_id=1, source_target_pairs={{1,0},{0,1},{385,16},{384,17},{129,128},{128,129},{257,144},{256,1... | collective-permute-start | bytes 393224 | tf_op jit(solution)/shard_map/ppermute | solution.py:193
  155.8 9.0 %collective-permute-start.16 = (bf16[256,256]{1,0:T(8,128)(2,1)S(1)}, bf16[256,256]{1,0:T(8,128)(2,1)S(1)}, u32[]{:S(2)}, u32[]{:S(2)}) collective-permute-start(bf16[256,256]{1,0:T(8,128)(2,1)S(1)} %get-tuple-element.23), channel_id=1, source_target_pairs={{0,0},{1,1},{384,16},{385,17},{128,128},{129,129},{256,144},{257,1... | collective-permute-start | bytes 393224 | tf_op jit(solution)/shard_map/ppermute | solution.py:193
Sparse Core Ops, SparseCore 0:
  10.1 57.1 all-gather.2
  106.1 53.9 reduce-scatter.1

commit v4 on v3

--- a/solution.py
+++ b/solution.py
@@ -91,7 +91,9 @@
         grad_rows = jnp.concatenate([dot(scaled, q, (0, 0)), dot(attn, g, (0, 0))], axis=1)
         grad_rows = grad_rows.astype(BF16)
         for j in range(2):
-            grad_kv[pl.ds(starts[j], NTOK), :] = grad_rows[j * NTOK : (j + 1) * NTOK, :]
+            grad_kv[0, pl.ds(starts[j], NTOK), :] = grad_rows[j * NTOK : (j + 1) * NTOK, :]
+    for copy in range(1, GROUP):
+        grad_kv[copy] = grad_kv[0]
     context[...] = from_blocks(forward[...])
     grad_queries[...] = from_blocks(back[...])
 
@@ -233,9 +235,9 @@
     arrived = lax.all_to_all(terms, ("z0", "s"), 0, 0, tiled=True)
 
     head = jax.ShapeDtypeStruct((ROWS, HD), BF16)
-    context, grad_queries, grad_own = kernel_call(
+    context, grad_queries, copies = kernel_call(
         attention_body,
-        (head, head, jax.ShapeDtypeStruct((ROWS, WIDE), BF16)),
+        (head, head, group),
         1,
         3,
         scratch=(
@@ -246,7 +248,7 @@
         flops=2 * ROWS * CLEN * HD * 6,
         bytes_accessed=1 << 20,
     )(neighbour_ids, arrived, queries[0], grad_context[0])
-    grads = lax.all_gather(grad_own, ("z0", "s"), axis=0, tiled=False)
+    grads = lax.all_to_all(copies, ("z0", "s"), 0, 0, tiled=True)
 
     enc_terms = kernel_call(
         encoder_grad_body,

time: 174 us -> 170 us (0.977)
  blocking collectives: 23.3 us -> 19 us
    all_gather x1 -> x0, blocking collectives: 13.8 us -> none  [per_device(): grads = lax.all_gather(grad_own, ('z0', 's'), axis=0, tiled=False)]
    all_to_all x0 -> x1, blocking collectives: none -> 9.51 us  [per_device(): grads = lax.all_to_all(copies, ('z0', 's'), 0, 0, tiled=True)]
where the time goes in v4:
time: 170 us; the launch traced here: 169 us
  starting transfers between devices  58.7 us (35%)
  waiting for transfers between devices  58.6 us (34%)
  blocking collectives  19 us (11%)
  between operations  14.4 us (8%)
  Pallas kernels  12.1 us (7%)
  other arithmetic  3.45 us (2%)
  local copies, waits for them, and re-layouts  2.46 us (1%)
    ppermute x8, starting transfers between devices, swap(): return lax.ppermute(x, axis, [(0, 1), (1, 0)])  25.4 us
    ppermute x3, waiting for transfers between devices, hop(): return lax.ppermute(x, ('yh', 'yl'), [(i, i ^ by) for i in range(4)])  21.6 us
    ppermute x8, waiting for transfers between devices, swap(): return lax.ppermute(x, axis, [(0, 1), (1, 0)])  15.2 us
    ppermute x4, starting transfers between devices, send(): return lax.ppermute(x, Y_AXES, pairs)  13.5 us
    ppermute x3, starting transfers between devices, hop(): return lax.ppermute(x, ('yh', 'yl'), [(i, i ^ by) for i in range(4)])  9.82 us
    all_to_all x1, blocking collectives, per_device(): arrived = lax.all_to_all(terms, ('z0', 's'), 0, 0, tiled=True)  9.52 us
    all_to_all x1, blocking collectives, per_device(): grads = lax.all_to_all(copies, ('z0', 's'), 0, 0, tiled=True)  9.51 us
    ppermute x2, starting transfers between devices, turn_back(): return lax.ppermute(x, Y_AXES, pairs)  7.95 us
  transfers between devices with their start and end apart: 20, of which 13 were waited for; matrix products, arithmetic and copies ran while one was open for 3% of the time, Pallas kernels for 2%

profile of v4, /device:TPU:6, one launch (start us, length us, event | category | flops | bytes accessed | tf_op | source)
XLA Modules:
  0.0 168.7 jit_solution(15549895893344567823)
XLA Ops:
  7.2 0.7 all-gather.2.cloned.1.call-update
  8.0 1.0 fusion.2
  8.9 0.1 broadcast_select_fusion.3
  9.0 4.1 %collective-permute-start.3 = (bf16[256,256]{1,0:T(8,128)(2,1)S(1)}, bf16[256,256]{1,0:T(8,128)(2,1)S(1)}, u32[]{:S(2)}, u32[]{:S(2)}) collective-permute-start(bf16[256,256]{1,0:T(8,128)(2,1)S(1)} %get-tuple-element.25), channel_id=1, source_target_pairs={{0,385},{16,1},{1,384},{17,0},{128,257},{144,129},{129,256},{145,1... | collective-permute-start | bytes 393224 | tf_op jit(solution)/shard_map/ppermute | solution.py:174
  13.1 5.1 %collective-permute-start.2 = (bf16[256,256]{1,0:T(8,128)(2,1)S(1)}, bf16[256,256]{1,0:T(8,128)(2,1)S(1)}, u32[]{:S(2)}, u32[]{:S(2)}) collective-permute-start(bf16[256,256]{1,0:T(8,128)(2,1)S(1)} %get-tuple-element.25), channel_id=1, source_target_pairs={{0,1},{16,385},{1,0},{17,384},{128,129},{144,257},{129,128},{145,2... | collective-permute-start | bytes 393224 | tf_op jit(solution)/shard_map/ppermute | solution.py:174
  18.2 2.4 %collective-permute-start.1 = (bf16[256,256]{1,0:T(8,128)(2,1)S(1)}, bf16[256,256]{1,0:T(8,128)(2,1)S(1)}, u32[]{:S(2)}, u32[]{:S(2)}) collective-permute-start(bf16[256,256]{1,0:T(8,128)(2,1)S(1)} %get-tuple-element.24), channel_id=1, source_target_pairs={{16,384},{17,385},{144,256},{145,257},{256,144},{257,145},{384,16}... | collective-permute-start | bytes 393224 | tf_op jit(solution)/shard_map/ppermute | solution.py:174
  20.6 1.9 %collective-permute-start = (bf16[256,256]{1,0:T(8,128)(2,1)S(1)}, bf16[256,256]{1,0:T(8,128)(2,1)S(1)}, u32[]{:S(2)}, u32[]{:S(2)}) collective-permute-start(bf16[256,256]{1,0:T(8,128)(2,1)S(1)} %get-tuple-element.24), channel_id=1, source_target_pairs={{0,384},{16,0},{1,385},{17,1},{128,256},{144,128},{129,257},{145,1... | collective-permute-start | bytes 393224 | tf_op jit(solution)/shard_map/ppermute | solution.py:174
  22.5 0.4 collective-permute-done.2
  23.0 5.4 %collective-permute-done.1 = bf16[256,256]{1,0:T(8,128)(2,1)S(1)} collective-permute-done((bf16[256,256]{1,0:T(8,128)(2,1)S(1)}, bf16[256,256]{1,0:T(8,128)(2,1)S(1)}, u32[]{:S(2)}, u32[]{:S(2)}) %collective-permute-start.1) | collective-permute-done | bytes 131104 | tf_op jit(solution)/shard_map/ppermute | solution.py:174
  28.3 1.4 collective-permute-done
  29.8 0.1 pad_maximum_fusion.refs_0_
  29.9 1.9 %collective-permute-start.9 = (bf16[256,1024]{1,0:T(8,128)(2,1)S(1)}, bf16[256,1024]{1,0:T(8,128)(2,1)S(1)}, u32[]{:S(2)}, u32[]{:S(2)}) collective-permute-start(bf16[256,1024]{1,0:T(8,128)(2,1)S(1)} %pad_maximum_fusion.refs_0_), channel_id=1, source_target_pairs={{0,192},{64,128},{128,64},{192,0},{1,193},{65,129},{129,65},{193,1... | collective-permute-start | bytes 1572872 | tf_op jit(solution)/shard_map/ppermute | solution.py:138
  31.8 8.8 %collective-permute-start.7 = (bf16[256,1024]{1,0:T(8,128)(2,1)S(1)}, bf16[256,1024]{1,0:T(8,128)(2,1)S(1)}, u32[]{:S(2)}, u32[]{:S(2)}) collective-permute-start(bf16[256,1024]{1,0:T(8,128)(2,1)S(1)} %pad_maximum_fusion.refs_0_), channel_id=1, source_target_pairs={{0,128},{128,0},{1,129},{129,1},{2,130},{130,2},{3,131},{131,3},{4... | collective-permute-start | bytes 1572872 | tf_op jit(solution)/shard_map/ppermute | solution.py:134
  40.5 1.9 %collective-permute-start.5 = (bf16[256,1024]{1,0:T(8,128)(2,1)S(1)}, bf16[256,1024]{1,0:T(8,128)(2,1)S(1)}, u32[]{:S(2)}, u32[]{:S(2)}) collective-permute-start(bf16[256,1024]{1,0:T(8,128)(2,1)S(1)} %pad_maximum_fusion.refs_0_), channel_id=1, source_target_pairs={{0,64},{64,0},{1,65},{65,1},{2,66},{66,2},{3,67},{67,3},{4,68},{68... | collective-permute-start | bytes 1572872 | tf_op jit(solution)/shard_map/ppermute | solution.py:134
  42.5 1.9 %collective-permute-start.4 = (bf16[256,1024]{1,0:T(8,128)(2,1)S(1)}, bf16[256,1024]{1,0:T(8,128)(2,1)S(1)}, u32[]{:S(2)}, u32[]{:S(2)}) collective-permute-start(bf16[256,1024]{1,0:T(8,128)(2,1)S(1)} %pad_maximum_fusion.refs_0_), channel_id=1, source_target_pairs={{0,32},{32,0},{1,33},{33,1},{2,34},{34,2},{3,35},{35,3},{4,36},{36... | collective-permute-start | bytes 1572872 | tf_op jit(solution)/shard_map/ppermute | solution.py:134
  44.4 4.7 %collective-permute-done.9.refs_6_ = bf16[256,1024]{1,0:T(8,128)(2,1)S(1)} collective-permute-done((bf16[256,1024]{1,0:T(8,128)(2,1)S(1)}, bf16[256,1024]{1,0:T(8,128)(2,1)S(1)}, u32[]{:S(2)}, u32[]{:S(2)}) %collective-permute-start.9) | collective-permute-done | bytes 524320 | tf_op jit(solution)/shard_map/ppermute | solution.py:138
  49.1 1.9 %collective-permute-start.10 = (bf16[256,1024]{1,0:T(8,128)(2,1)S(1)}, bf16[256,1024]{1,0:T(8,128)(2,1)S(1)}, u32[]{:S(2)}, u32[]{:S(2)}) collective-permute-start(bf16[256,1024]{1,0:T(8,128)(2,1)S(1)} %collective-permute-done.9.refs_6_), channel_id=1, source_target_pairs={{0,32},{32,0},{1,33},{33,1},{2,34},{34,2},{3,35},{35,3},{4,36},{36... | collective-permute-start | bytes 1572872 | tf_op jit(solution)/shard_map/ppermute | solution.py:134
  51.0 7.0 %collective-permute-done.7.refs_4_ = bf16[256,1024]{1,0:T(8,128)(2,1)S(1)} collective-permute-done((bf16[256,1024]{1,0:T(8,128)(2,1)S(1)}, bf16[256,1024]{1,0:T(8,128)(2,1)S(1)}, u32[]{:S(2)}, u32[]{:S(2)}) %collective-permute-start.7) | collective-permute-done | bytes 524320 | tf_op jit(solution)/shard_map/ppermute | solution.py:134
  57.9 1.9 %collective-permute-start.8 = (bf16[256,1024]{1,0:T(8,128)(2,1)S(1)}, bf16[256,1024]{1,0:T(8,128)(2,1)}, u32[]{:S(2)}, u32[]{:S(2)}) collective-permute-start(bf16[256,1024]{1,0:T(8,128)(2,1)S(1)} %collective-permute-done.7.refs_4_), channel_id=1, source_target_pairs={{0,32},{32,0},{1,33},{33,1},{2,34},{34,2},{3,35},{35,3},{4,36},{36... | collective-permute-start | bytes 1572872 | tf_op jit(solution)/shard_map/ppermute | solution.py:134
  59.9 2.4 %collective-permute-start.6 = (bf16[256,1024]{1,0:T(8,128)(2,1)S(1)}, bf16[256,1024]{1,0:T(8,128)(2,1)}, u32[]{:S(2)}, u32[]{:S(2)}) collective-permute-start(bf16[256,1024]{1,0:T(8,128)(2,1)S(1)} %collective-permute-done.5.refs_2_), channel_id=1, source_target_pairs={{0,32},{32,0},{1,33},{33,1},{2,34},{34,2},{3,35},{35,3},{4,36},{36... | collective-permute-start | bytes 1572872 | tf_op jit(solution)/shard_map/ppermute | solution.py:134
  62.3 0.1 stack.23.me
  62.4 1.5 collective-permute-done.6.refs_3_
  63.9 3.3 %all-gather.2.cloned.1.call-done.enc = bf16[8,256,256]{2,1,0:T(8,128)(2,1)} async-done(((bf16[1,256,256]{2,1,0:T(8,128)(2,1)}), bf16[8,256,256]{2,1,0:T(8,128)(2,1)}) %all-gather.2.cloned.1.call-update) | async-done | bytes 1048592 | tf_op jit(solution)/shard_map/all_gather | solution.py:199
  67.3 1.2 copy-done.8
  68.5 2.5 %shard_map.101 = bf16[4,256,256]{2,1,0:T(8,128)(2,1)S(1)} custom-call(s32[5]{0:T(128)S(1)} %stack.23.me, bf16[8,256,256]{2,1,0:T(8,128)(2,1)S(1)} %copy-done.8, bf16[256,1024]{1,0:T(8,128)(2,1)S(1)} %pad_maximum_fusion.refs_0_, bf16[256,1024]{1,0:T(8,128)(2,1)S(1)} %collective-permute-done.4.refs_1_, bf16[256,1024]{1,0:T(8,128)(2,1)S(1)} %collective-permute-done.5.refs_2_, ...), custom_call_target="tpu_custom_call" | custom-call | flops 1073741824 | bytes 5242880 | tf_op jit(solution)/shard_map/pallas_call | solution.py:232
  71.1 9.5 %all_to_all.10.arrived = bf16[4,256,256]{2,1,0:T(8,128)(2,1)S(1)} all-to-all(bf16[4,256,256]{2,1,0:T(8,128)(2,1)S(1)} %shard_map.101), channel_id=1, replica_groups=mesh['yh'=2,'yl'=2,'xh'=2,'c'=2,'s'=2,'zr'=8,'z0'=2] {'z0','s'}, dimensions={0} | all-to-all | bytes 1048576 | tf_op jit(solution)/shard_map/all_to_all | solution.py:235
  80.6 2.8 %shard_map.102 = (bf16[256,128]{1,0:T(8,128)(2,1)}, bf16[256,128]{1,0:T(8,128)(2,1)}, bf16[4,256,256]{2,1,0:T(8,128)(2,1)S(1)}) custom-call(s32[1,8]{1,0:T(1,128)S(1)} %copy-done.12, bf16[4,256,256]{2,1,0:T(8,128)(2,1)S(1)} %all_to_all.10.arrived, bf16[256,128]{1,0:T(8,128)(2,1)S(1)} %bitcast.13, bf16[256,128]{1,0:T(8,128)(2,1)S(1)} %bitcast.14), custom_call_target="tpu_custom_call" | custom-call | flops 25165824 | bytes 1048576 | tf_op jit(solution)/shard_map/pallas_call | solution.py:238
  83.4 9.5 %all_to_all.11.grads = bf16[4,256,256]{2,1,0:T(8,128)(2,1)S(1)} all-to-all(bf16[4,256,256]{2,1,0:T(8,128)(2,1)S(1)} %get-tuple-element.12), channel_id=1, replica_groups=mesh['yh'=2,'yl'=2,'xh'=2,'c'=2,'s'=2,'zr'=8,'z0'=2] {'z0','s'}, dimensions={0} | all-to-all | bytes 1048576 | tf_op jit(solution)/shard_map/all_to_all | solution.py:251
  92.9 3.2 %shard_map.104 = (bf16[16,256,256]{2,1,0:T(8,128)(2,1)S(1)}, bf16[16,256,256]{2,1,0:T(8,128)(2,1)}) custom-call(s32[5]{0:T(128)S(1)} %stack.23.me, bf16[8,256,256]{2,1,0:T(8,128)(2,1)S(1)} %copy-done.9, bf16[4,256,256]{2,1,0:T(8,128)(2,1)S(1)} %all_to_all.11.grads), custom_call_target="tpu_custom_call" | custom-call | flops 1073741824 | bytes 5242880 | tf_op jit(solution)/shard_map/pallas_call | solution.py:264
  96.1 1.9 %collective-permute-start.11 = (bf16[16,256,256]{2,1,0:T(8,128)(2,1)}, bf16[16,256,256]{2,1,0:T(8,128)(2,1)}, u32[]{:S(2)}, u32[]{:S(2)}) collective-permute-start(bf16[16,256,256]{2,1,0:T(8,128)(2,1)} %get-tuple-element.14), channel_id=1, source_target_pairs={{0,32},{32,0},{1,33},{33,1},{2,34},{34,2},{3,35},{35,3},{4,36},{36... | collective-permute-start | bytes 6291464 | tf_op jit(solution)/shard_map/ppermute | solution.py:134
  98.1 3.6 %shard_map.103 = bf16[8,256,256]{2,1,0:T(8,128)(2,1)} custom-call(s32[5]{0:T(128)S(1)} %stack.23.me, bf16[4,256,256]{2,1,0:T(8,128)(2,1)S(1)} %all_to_all.11.grads, bf16[256,1024]{1,0:T(8,128)(2,1)S(1)} %pad_maximum_fusion.refs_0_, bf16[256,1024]{1,0:T(8,128)(2,1)S(1)} %copy-done.5, bf16[256,1024]{1,0:T(8,128)(2,1)S(1)} %copy-done.3, ...), custom_call_target="tpu_custom_call" | custom-call | flops 1073741824 | bytes 5242880 | tf_op jit(solution)/shard_map/pallas_call | solution.py:253
  101.7 0.8 collective-permute-done.11
  102.5 2.2 %add_convert_fusion = bf16[16,256,256]{2,1,0:T(8,128)(2,1)S(1)} fusion(bf16[16,256,256]{2,1,0:T(8,128)(2,1)} %collective-permute-done.11, bf16[16,256,256]{2,1,0:T(8,128)(2,1)S(1)} %get-tuple-element.13), kind=kLoop, calls=%fused_computation | loop fusion | flops 4194304 | bytes 6291456 | tf_op jit(solution)/shard_map/convert_element_type | solution.py:267
  104.8 0.1 fusion.1
  104.9 3.4 %collective-permute-start.12 = (bf16[4,256,256]{2,1,0:T(8,128)(2,1)S(1)}, bf16[4,256,256]{2,1,0:T(8,128)(2,1)S(1)}, u32[]{:S(2)}, u32[]{:S(2)}) collective-permute-start(bf16[4,256,256]{2,1,0:T(8,128)(2,1)S(1)} %get-tuple-element.15), channel_id=1, source_target_pairs={{0,128},{128,0},{256,384},{384,256},{1,129},{129,1},{257,385},{385... | collective-permute-start | bytes 1572872 | tf_op jit(solution)/shard_map/ppermute | solution.py:178
  108.2 4.0 %collective-permute-start.14 = (bf16[4,256,256]{2,1,0:T(8,128)(2,1)S(1)}, bf16[4,256,256]{2,1,0:T(8,128)(2,1)S(1)}, u32[]{:S(2)}, u32[]{:S(2)}) collective-permute-start(bf16[4,256,256]{2,1,0:T(8,128)(2,1)S(1)} %get-tuple-element.16), channel_id=1, source_target_pairs={{0,384},{128,256},{256,128},{384,0},{1,385},{129,257},{257,129},{3... | collective-permute-start | bytes 1572872 | tf_op jit(solution)/shard_map/ppermute | solution.py:178
  112.3 2.4 %collective-permute-start.13 = (bf16[4,256,256]{2,1,0:T(8,128)(2,1)S(1)}, bf16[4,256,256]{2,1,0:T(8,128)(2,1)S(1)}, u32[]{:S(2)}, u32[]{:S(2)}) collective-permute-start(bf16[4,256,256]{2,1,0:T(8,128)(2,1)S(1)} %get-tuple-element.17), channel_id=1, source_target_pairs={{0,256},{128,384},{256,0},{384,128},{1,257},{129,385},{257,1},{385... | collective-permute-start | bytes 1572872 | tf_op jit(solution)/shard_map/ppermute | solution.py:178
  114.7 6.8 %collective-permute-done.12 = bf16[4,256,256]{2,1,0:T(8,128)(2,1)S(1)} collective-permute-done((bf16[4,256,256]{2,1,0:T(8,128)(2,1)S(1)}, bf16[4,256,256]{2,1,0:T(8,128)(2,1)S(1)}, u32[]{:S(2)}, u32[]{:S(2)}) %collective-permute-start.12) | collective-permute-done | bytes 524320 | tf_op jit(solution)/shard_map/ppermute | solution.py:178
  121.5 14.7 %collective-permute-done.14 = bf16[4,256,256]{2,1,0:T(8,128)(2,1)S(1)} collective-permute-done((bf16[4,256,256]{2,1,0:T(8,128)(2,1)S(1)}, bf16[4,256,256]{2,1,0:T(8,128)(2,1)S(1)}, u32[]{:S(2)}, u32[]{:S(2)}) %collective-permute-start.14) | collective-permute-done | bytes 524320 | tf_op jit(solution)/shard_map/ppermute | solution.py:178
  136.3 0.3 add_convert_fusion.1
  136.6 4.7 %collective-permute-start.15 = (bf16[2,256,256]{2,1,0:T(8,128)(2,1)S(1)}, bf16[2,256,256]{2,1,0:T(8,128)(2,1)S(1)}, u32[]{:S(2)}, u32[]{:S(2)}) collective-permute-start(bf16[2,256,256]{2,1,0:T(8,128)(2,1)S(1)} %slice.65), channel_id=1, source_target_pairs={{0,64},{64,0},{1,65},{65,1},{2,66},{66,2},{3,67},{67,3},{4,68},{68... | collective-permute-start | bytes 786440 | tf_op jit(solution)/shard_map/ppermute | solution.py:134
  141.2 5.9 %collective-permute-done.15 = bf16[2,256,256]{2,1,0:T(8,128)(2,1)S(1)} collective-permute-done((bf16[2,256,256]{2,1,0:T(8,128)(2,1)S(1)}, bf16[2,256,256]{2,1,0:T(8,128)(2,1)S(1)}, u32[]{:S(2)}, u32[]{:S(2)}) %collective-permute-start.15) | collective-permute-done | bytes 262176 | tf_op jit(solution)/shard_map/ppermute | solution.py:134
  147.1 0.1 add_convert_fusion.2
  147.2 4.9 %collective-permute-start.17 = (bf16[256,256]{1,0:T(8,128)(2,1)S(1)}, bf16[256,256]{1,0:T(8,128)(2,1)S(1)}, u32[]{:S(2)}, u32[]{:S(2)}) collective-permute-start(bf16[256,256]{1,0:T(8,128)(2,1)S(1)} %get-tuple-element.22), channel_id=1, source_target_pairs={{1,0},{0,1},{385,16},{384,17},{129,128},{128,129},{257,144},{256,1... | collective-permute-start | bytes 393224 | tf_op jit(solution)/shard_map/ppermute | solution.py:195
  152.2 3.0 %collective-permute-start.16 = (bf16[256,256]{1,0:T(8,128)(2,1)S(1)}, bf16[256,256]{1,0:T(8,128)(2,1)S(1)}, u32[]{:S(2)}, u32[]{:S(2)}) collective-permute-start(bf16[256,256]{1,0:T(8,128)(2,1)S(1)} %get-tuple-element.23), channel_id=1, source_target_pairs={{0,0},{1,1},{384,16},{385,17},{128,128},{129,129},{256,144},{257,1... | collective-permute-start | bytes 393224 | tf_op jit(solution)/shard_map/ppermute | solution.py:195
  155.2 3.2 %collective-permute-done.17 = bf16[256,256]{1,0:T(8,128)(2,1)S(1)} collective-permute-done((bf16[256,256]{1,0:T(8,128)(2,1)S(1)}, bf16[256,256]{1,0:T(8,128)(2,1)S(1)}, u32[]{:S(2)}, u32[]{:S(2)}) %collective-permute-start.17) | collective-permute-done | bytes 131104 | tf_op jit(solution)/shard_map/ppermute | solution.py:195
  158.4 2.7 %collective-permute-done.16 = bf16[256,256]{1,0:T(8,128)(2,1)S(1)} collective-permute-done((bf16[256,256]{1,0:T(8,128)(2,1)S(1)}, bf16[256,256]{1,0:T(8,128)(2,1)S(1)}, u32[]{:S(2)}, u32[]{:S(2)}) %collective-permute-start.16) | collective-permute-done | bytes 131104 | tf_op jit(solution)/shard_map/ppermute | solution.py:195
  161.2 0.7 pad_maximum_fusion.1
  (40 shorter events, 0.3 us)
Async XLA Ops:
  7.2 60.1 %all-gather.2.cloned.1.call-start = ((), (), s32[]{:S(2)}) async-start(), calls=%async_computation.3 | async-start | bytes 1179648 | tf_op jit(solution)/shard_map/all_gather | solution.py:199
  7.9 154.0 %reduce-scatter.2.cloned.1.call-start = ((), (), s32[]{:S(2)}) async-start(), calls=%async_computation.4 | async-start | bytes 1179648 | tf_op jit(solution)/shard_map/reduce_scatter | solution.py:261
  9.0 13.6 %collective-permute-start.3 = (bf16[256,256]{1,0:T(8,128)(2,1)S(1)}, bf16[256,256]{1,0:T(8,128)(2,1)S(1)}, u32[]{:S(2)}, u32[]{:S(2)}) collective-permute-start(bf16[256,256]{1,0:T(8,128)(2,1)S(1)} %get-tuple-element.25), channel_id=1, source_target_pairs={{0,385},{16,1},{1,384},{17,0},{128,257},{144,129},{129,256},{145,1... | collective-permute-start | bytes 393224 | tf_op jit(solution)/shard_map/ppermute | solution.py:174
  13.1 9.9 %collective-permute-start.2 = (bf16[256,256]{1,0:T(8,128)(2,1)S(1)}, bf16[256,256]{1,0:T(8,128)(2,1)S(1)}, u32[]{:S(2)}, u32[]{:S(2)}) collective-permute-start(bf16[256,256]{1,0:T(8,128)(2,1)S(1)} %get-tuple-element.25), channel_id=1, source_target_pairs={{0,1},{16,385},{1,0},{17,384},{128,129},{144,257},{129,128},{145,2... | collective-permute-start | bytes 393224 | tf_op jit(solution)/shard_map/ppermute | solution.py:174
  18.2 10.1 %collective-permute-start.1 = (bf16[256,256]{1,0:T(8,128)(2,1)S(1)}, bf16[256,256]{1,0:T(8,128)(2,1)S(1)}, u32[]{:S(2)}, u32[]{:S(2)}) collective-permute-start(bf16[256,256]{1,0:T(8,128)(2,1)S(1)} %get-tuple-element.24), channel_id=1, source_target_pairs={{16,384},{17,385},{144,256},{145,257},{256,144},{257,145},{384,16}... | collective-permute-start | bytes 393224 | tf_op jit(solution)/shard_map/ppermute | solution.py:174
  20.6 9.2 %collective-permute-start = (bf16[256,256]{1,0:T(8,128)(2,1)S(1)}, bf16[256,256]{1,0:T(8,128)(2,1)S(1)}, u32[]{:S(2)}, u32[]{:S(2)}) collective-permute-start(bf16[256,256]{1,0:T(8,128)(2,1)S(1)} %get-tuple-element.24), channel_id=1, source_target_pairs={{0,384},{16,0},{1,385},{17,1},{128,256},{144,128},{129,257},{145,1... | collective-permute-start | bytes 393224 | tf_op jit(solution)/shard_map/ppermute | solution.py:174
  29.9 19.2 %collective-permute-start.9 = (bf16[256,1024]{1,0:T(8,128)(2,1)S(1)}, bf16[256,1024]{1,0:T(8,128)(2,1)S(1)}, u32[]{:S(2)}, u32[]{:S(2)}) collective-permute-start(bf16[256,1024]{1,0:T(8,128)(2,1)S(1)} %pad_maximum_fusion.refs_0_), channel_id=1, source_target_pairs={{0,192},{64,128},{128,64},{192,0},{1,193},{65,129},{129,65},{193,1... | collective-permute-start | bytes 1572872 | tf_op jit(solution)/shard_map/ppermute | solution.py:138
  31.8 26.2 %collective-permute-start.7 = (bf16[256,1024]{1,0:T(8,128)(2,1)S(1)}, bf16[256,1024]{1,0:T(8,128)(2,1)S(1)}, u32[]{:S(2)}, u32[]{:S(2)}) collective-permute-start(bf16[256,1024]{1,0:T(8,128)(2,1)S(1)} %pad_maximum_fusion.refs_0_), channel_id=1, source_target_pairs={{0,128},{128,0},{1,129},{129,1},{2,130},{130,2},{3,131},{131,3},{4... | collective-permute-start | bytes 1572872 | tf_op jit(solution)/shard_map/ppermute | solution.py:134
  40.5 19.3 %collective-permute-start.5 = (bf16[256,1024]{1,0:T(8,128)(2,1)S(1)}, bf16[256,1024]{1,0:T(8,128)(2,1)S(1)}, u32[]{:S(2)}, u32[]{:S(2)}) collective-permute-start(bf16[256,1024]{1,0:T(8,128)(2,1)S(1)} %pad_maximum_fusion.refs_0_), channel_id=1, source_target_pairs={{0,64},{64,0},{1,65},{65,1},{2,66},{66,2},{3,67},{67,3},{4,68},{68... | collective-permute-start | bytes 1572872 | tf_op jit(solution)/shard_map/ppermute | solution.py:134
  42.5 20.0 %collective-permute-start.4 = (bf16[256,1024]{1,0:T(8,128)(2,1)S(1)}, bf16[256,1024]{1,0:T(8,128)(2,1)S(1)}, u32[]{:S(2)}, u32[]{:S(2)}) collective-permute-start(bf16[256,1024]{1,0:T(8,128)(2,1)S(1)} %pad_maximum_fusion.refs_0_), channel_id=1, source_target_pairs={{0,32},{32,0},{1,33},{33,1},{2,34},{34,2},{3,35},{35,3},{4,36},{36... | collective-permute-start | bytes 1572872 | tf_op jit(solution)/shard_map/ppermute | solution.py:134
  49.1 13.4 %collective-permute-start.10 = (bf16[256,1024]{1,0:T(8,128)(2,1)S(1)}, bf16[256,1024]{1,0:T(8,128)(2,1)S(1)}, u32[]{:S(2)}, u32[]{:S(2)}) collective-permute-start(bf16[256,1024]{1,0:T(8,128)(2,1)S(1)} %collective-permute-done.9.refs_6_), channel_id=1, source_target_pairs={{0,32},{32,0},{1,33},{33,1},{2,34},{34,2},{3,35},{35,3},{4,36},{36... | collective-permute-start | bytes 1572872 | tf_op jit(solution)/shard_map/ppermute | solution.py:134
  57.9 13.1 %copy-start = (bf16[256,1024]{1,0:T(8,128)(2,1)}, bf16[256,1024]{1,0:T(8,128)(2,1)S(1)}, u32[]{:S(2)}) copy-start(bf16[256,1024]{1,0:T(8,128)(2,1)S(1)} %collective-permute-done.7.refs_4_) | copy-start | bytes 1572868
  57.9 4.5 %collective-permute-start.8 = (bf16[256,1024]{1,0:T(8,128)(2,1)S(1)}, bf16[256,1024]{1,0:T(8,128)(2,1)}, u32[]{:S(2)}, u32[]{:S(2)}) collective-permute-start(bf16[256,1024]{1,0:T(8,128)(2,1)S(1)} %collective-permute-done.7.refs_4_), channel_id=1, source_target_pairs={{0,32},{32,0},{1,33},{33,1},{2,34},{34,2},{3,35},{35,3},{4,36},{36... | collective-permute-start | bytes 1572872 | tf_op jit(solution)/shard_map/ppermute | solution.py:134
  59.9 11.2 %copy-start.2 = (bf16[256,1024]{1,0:T(8,128)(2,1)}, bf16[256,1024]{1,0:T(8,128)(2,1)S(1)}, u32[]{:S(2)}) copy-start(bf16[256,1024]{1,0:T(8,128)(2,1)S(1)} %collective-permute-done.5.refs_2_) | copy-start | bytes 1572868
  59.9 4.1 %collective-permute-start.6 = (bf16[256,1024]{1,0:T(8,128)(2,1)S(1)}, bf16[256,1024]{1,0:T(8,128)(2,1)}, u32[]{:S(2)}, u32[]{:S(2)}) collective-permute-start(bf16[256,1024]{1,0:T(8,128)(2,1)S(1)} %collective-permute-done.5.refs_2_), channel_id=1, source_target_pairs={{0,32},{32,0},{1,33},{33,1},{2,34},{34,2},{3,35},{35,3},{4,36},{36... | collective-permute-start | bytes 1572872 | tf_op jit(solution)/shard_map/ppermute | solution.py:134
  62.3 18.3 %copy-start.12 = (s32[1,8]{1,0:T(1,128)S(1)}, s32[1,8]{1,0:T(1,128)}, u32[]{:S(2)}) copy-start(s32[1,8]{1,0:T(1,128)} %ids.1) | copy-start | bytes 100
  62.4 8.7 %copy-start.4 = (bf16[256,1024]{1,0:T(8,128)(2,1)}, bf16[256,1024]{1,0:T(8,128)(2,1)S(1)}, u32[]{:S(2)}) copy-start(bf16[256,1024]{1,0:T(8,128)(2,1)S(1)} %collective-permute-done.4.refs_1_) | copy-start | bytes 1572868
  62.4 8.7 %copy-start.6 = (bf16[256,1024]{1,0:T(8,128)(2,1)}, bf16[256,1024]{1,0:T(8,128)(2,1)S(1)}, u32[]{:S(2)}) copy-start(bf16[256,1024]{1,0:T(8,128)(2,1)S(1)} %collective-permute-done.10.refs_7_) | copy-start | bytes 1572868
  67.3 1.2 copy-start.8
  68.5 12.1 %copy-start.10 = (bf16[1,256,128]{2,1,0:T(8,128)(2,1)S(1)}, bf16[1,256,128]{2,1,0:T(8,128)(2,1)}, u32[]{:S(2)}) copy-start(bf16[1,256,128]{2,1,0:T(8,128)(2,1)} %param.6) | copy-start | bytes 196612
  68.5 12.1 %copy-start.11 = (bf16[1,256,128]{2,1,0:T(8,128)(2,1)S(1)}, bf16[1,256,128]{2,1,0:T(8,128)(2,1)}, u32[]{:S(2)}) copy-start(bf16[1,256,128]{2,1,0:T(8,128)(2,1)} %param.11) | copy-start | bytes 196612
  71.1 21.8 %copy-start.9 = (bf16[8,256,256]{2,1,0:T(8,128)(2,1)S(1)}, bf16[8,256,256]{2,1,0:T(8,128)(2,1)}, u32[]{:S(2)}) copy-start(bf16[8,256,256]{2,1,0:T(8,128)(2,1)} %all-gather.2.cloned.1.call-done.enc) | copy-start | bytes 3145732
  92.9 5.1 %copy-start.1 = (bf16[256,1024]{1,0:T(8,128)(2,1)S(1)}, bf16[256,1024]{1,0:T(8,128)(2,1)}, u32[]{:S(2)}) copy-start(bf16[256,1024]{1,0:T(8,128)(2,1)} %copy-done) | copy-start | bytes 1572868
  92.9 5.1 %copy-start.3 = (bf16[256,1024]{1,0:T(8,128)(2,1)S(1)}, bf16[256,1024]{1,0:T(8,128)(2,1)}, u32[]{:S(2)}) copy-start(bf16[256,1024]{1,0:T(8,128)(2,1)} %copy-done.2) | copy-start | bytes 1572868
  92.9 5.2 %copy-start.5 = (bf16[256,1024]{1,0:T(8,128)(2,1)S(1)}, bf16[256,1024]{1,0:T(8,128)(2,1)}, u32[]{:S(2)}) copy-start(bf16[256,1024]{1,0:T(8,128)(2,1)} %copy-done.4) | copy-start | bytes 1572868
  92.9 5.2 %copy-start.7 = (bf16[256,1024]{1,0:T(8,128)(2,1)S(1)}, bf16[256,1024]{1,0:T(8,128)(2,1)}, u32[]{:S(2)}) copy-start(bf16[256,1024]{1,0:T(8,128)(2,1)} %copy-done.6) | copy-start | bytes 1572868
  96.1 6.4 %collective-permute-start.11 = (bf16[16,256,256]{2,1,0:T(8,128)(2,1)}, bf16[16,256,256]{2,1,0:T(8,128)(2,1)}, u32[]{:S(2)}, u32[]{:S(2)}) collective-permute-start(bf16[16,256,256]{2,1,0:T(8,128)(2,1)} %get-tuple-element.14), channel_id=1, source_target_pairs={{0,32},{32,0},{1,33},{33,1},{2,34},{34,2},{3,35},{35,3},{4,36},{36... | collective-permute-start | bytes 6291464 | tf_op jit(solution)/shard_map/ppermute | solution.py:134
  104.9 16.7 %collective-permute-start.12 = (bf16[4,256,256]{2,1,0:T(8,128)(2,1)S(1)}, bf16[4,256,256]{2,1,0:T(8,128)(2,1)S(1)}, u32[]{:S(2)}, u32[]{:S(2)}) collective-permute-start(bf16[4,256,256]{2,1,0:T(8,128)(2,1)S(1)} %get-tuple-element.15), channel_id=1, source_target_pairs={{0,128},{128,0},{256,384},{384,256},{1,129},{129,1},{257,385},{385... | collective-permute-start | bytes 1572872 | tf_op jit(solution)/shard_map/ppermute | solution.py:178
  108.2 28.0 %collective-permute-start.14 = (bf16[4,256,256]{2,1,0:T(8,128)(2,1)S(1)}, bf16[4,256,256]{2,1,0:T(8,128)(2,1)S(1)}, u32[]{:S(2)}, u32[]{:S(2)}) collective-permute-start(bf16[4,256,256]{2,1,0:T(8,128)(2,1)S(1)} %get-tuple-element.16), channel_id=1, source_target_pairs={{0,384},{128,256},{256,128},{384,0},{1,385},{129,257},{257,129},{3... | collective-permute-start | bytes 1572872 | tf_op jit(solution)/shard_map/ppermute | solution.py:178
  112.3 24.0 %collective-permute-start.13 = (bf16[4,256,256]{2,1,0:T(8,128)(2,1)S(1)}, bf16[4,256,256]{2,1,0:T(8,128)(2,1)S(1)}, u32[]{:S(2)}, u32[]{:S(2)}) collective-permute-start(bf16[4,256,256]{2,1,0:T(8,128)(2,1)S(1)} %get-tuple-element.17), channel_id=1, source_target_pairs={{0,256},{128,384},{256,0},{384,128},{1,257},{129,385},{257,1},{385... | collective-permute-start | bytes 1572872 | tf_op jit(solution)/shard_map/ppermute | solution.py:178
  136.6 10.6 %collective-permute-start.15 = (bf16[2,256,256]{2,1,0:T(8,128)(2,1)S(1)}, bf16[2,256,256]{2,1,0:T(8,128)(2,1)S(1)}, u32[]{:S(2)}, u32[]{:S(2)}) collective-permute-start(bf16[2,256,256]{2,1,0:T(8,128)(2,1)S(1)} %slice.65), channel_id=1, source_target_pairs={{0,64},{64,0},{1,65},{65,1},{2,66},{66,2},{3,67},{67,3},{4,68},{68... | collective-permute-start | bytes 786440 | tf_op jit(solution)/shard_map/ppermute | solution.py:134
  147.2 11.2 %collective-permute-start.17 = (bf16[256,256]{1,0:T(8,128)(2,1)S(1)}, bf16[256,256]{1,0:T(8,128)(2,1)S(1)}, u32[]{:S(2)}, u32[]{:S(2)}) collective-permute-start(bf16[256,256]{1,0:T(8,128)(2,1)S(1)} %get-tuple-element.22), channel_id=1, source_target_pairs={{1,0},{0,1},{385,16},{384,17},{129,128},{128,129},{257,144},{256,1... | collective-permute-start | bytes 393224 | tf_op jit(solution)/shard_map/ppermute | solution.py:195
  152.2 9.0 %collective-permute-start.16 = (bf16[256,256]{1,0:T(8,128)(2,1)S(1)}, bf16[256,256]{1,0:T(8,128)(2,1)S(1)}, u32[]{:S(2)}, u32[]{:S(2)}) collective-permute-start(bf16[256,256]{1,0:T(8,128)(2,1)S(1)} %get-tuple-element.23), channel_id=1, source_target_pairs={{0,0},{1,1},{384,16},{385,17},{128,128},{129,129},{256,144},{257,1... | collective-permute-start | bytes 393224 | tf_op jit(solution)/shard_map/ppermute | solution.py:195
Sparse Core Ops, SparseCore 0:
  10.1 57.1 all-gather.1
  101.8 55.1 reduce-scatter.1

commit v5 on v4

--- a/solution.py
+++ b/solution.py
@@ -178,21 +178,14 @@
     return lax.ppermute(x, ("yh", "yl"), [(i, i ^ by) for i in range(4)])
 
 
-def turned(flip):
+def turn_back(x, across, flip):
+    place = lambda at: (((at[0] * 2 + at[1]) * 2 + at[2]) * 2 + at[3]) * 2 + at[4]
     pairs = []
-    for yh in range(2):
-        for yl in range(2):
-            for s in range(2):
-                for z in range(2):
-                    target = (s, yl if yh == s else 1 - yl, yh, z ^ flip)
-                    pairs.append(((yh, yl, s, z), target))
-    place = lambda at: ((at[0] * 2 + at[1]) * 2 + at[2]) * 2 + at[3]
-    return [(place(source), place(target)) for source, target in pairs]
-
-
-def turn_back(x, flip):
-    pairs = [(target, source) for source, target in turned(flip)]
-    return lax.ppermute(x, Y_AXES, pairs)
+    for at in range(32):
+        yh, yl, xh, s, z = [at >> bit & 1 for bit in (4, 3, 2, 1, 0)]
+        holder = (s, yl if yh == s else 1 - yl, xh ^ across, yh, z ^ flip)
+        pairs.append((place(holder), at))
+    return lax.ppermute(x, ("yh", "yl", "xh", "s", "z0"), pairs)
 
 
 def per_device(queries, encoded, neighbour_ids, key_weight, value_weight, grad_context):
@@ -267,8 +260,8 @@
     near = (near.astype(F32) + swap(far, "c").astype(F32)).astype(BF16)
     near = near.reshape(4, 4, BLOCK, WIDE)
     near = add(near[0], hop(near[1], 1), hop(near[2], 2), hop(near[3], 3))
-    total = add(near[:2], swap(near[2:], "xh"))
-    kept, given = turn_back(total[0], 0), turn_back(total[1], 1)
+    kept = add(turn_back(near[2], 1, 0), turn_back(near[0], 0, 0))
+    given = add(turn_back(near[3], 1, 1), turn_back(near[1], 0, 1))
     upper, lower = jnp.where(even, kept, given), jnp.where(even, given, kept)
     weight_grad = jnp.concatenate([upper, lower], axis=0)
     return (

time: 170 us -> 169 us (level)
  waiting for transfers between devices: 58.6 us -> 52.4 us
  starting transfers between devices: 58.7 us -> 64.1 us
    ppermute x2 -> x4, starting transfers between devices: 7.95 us -> 18 us  [turn_back(): return lax.ppermute(x, ('yh', 'yl', 'xh', 's', 'z0'), pairs)]
    ppermute x8 -> x7, waiting for transfers between devices: 15.2 us -> 9.3 us  [swap(): return lax.ppermute(x, axis, [(0, 1), (1, 0)])]
    ppermute x8 -> x7, starting transfers between devices: 25.4 us -> 20.7 us  [swap(): return lax.ppermute(x, axis, [(0, 1), (1, 0)])]
    ppermute x2 -> x4, waiting for transfers between devices: 5.95 us -> 5.68 us  [turn_back(): return lax.ppermute(x, ('yh', 'yl', 'xh', 's', 'z0'), pairs)]
  transfers between devices with their start and end apart: 20 -> 21, of which waited for: 13 -> 14; matrix products, arithmetic and copies ran while one was open for 3% -> 3% of each run, Pallas kernels for 2% -> 2%
where the time goes in v5:
time: 169 us; the launch traced here: 168 us
  starting transfers between devices  64.1 us (38%)
  waiting for transfers between devices  52.4 us (31%)
  blocking collectives  19 us (11%)
  between operations  14.4 us (9%)
  Pallas kernels  12.1 us (7%)
  other arithmetic  3.44 us (2%)
  local copies, waits for them, and re-layouts  2.46 us (1%)
    ppermute x3, waiting for transfers between devices, hop(): return lax.ppermute(x, ('yh', 'yl'), [(i, i ^ by) for i in range(4)])  21.6 us
    ppermute x7, starting transfers between devices, swap(): return lax.ppermute(x, axis, [(0, 1), (1, 0)])  20.7 us
    ppermute x4, starting transfers between devices, turn_back(): return lax.ppermute(x, ('yh', 'yl', 'xh', 's', 'z0'), pairs)  18 us
    ppermute x4, starting transfers between devices, send(): return lax.ppermute(x, Y_AXES, pairs)  13.5 us
    ppermute x3, starting transfers between devices, hop(): return lax.ppermute(x, ('yh', 'yl'), [(i, i ^ by) for i in range(4)])  9.82 us
    all_to_all x1, blocking collectives, per_device(): arrived = lax.all_to_all(terms, ('z0', 's'), 0, 0, tiled=True)  9.52 us
    all_to_all x1, blocking collectives, per_device(): grads = lax.all_to_all(copies, ('z0', 's'), 0, 0, tiled=True)  9.51 us
    ppermute x7, waiting for transfers between devices, swap(): return lax.ppermute(x, axis, [(0, 1), (1, 0)])  9.3 us
  transfers between devices with their start and end apart: 21, of which 14 were waited for; matrix products, arithmetic and copies ran while one was open for 3% of the time, Pallas kernels for 2%

profile of v5, /device:TPU:6, one launch (start us, length us, event | category | flops | bytes accessed | tf_op | source)
XLA Modules:
  0.0 167.9 jit_solution(279747987255028812)
XLA Ops:
  7.2 0.7 all-gather.2.cloned.1.call-update
  8.0 1.0 fusion.2
  9.0 4.1 %collective-permute-start.3 = (bf16[256,256]{1,0:T(8,128)(2,1)S(1)}, bf16[256,256]{1,0:T(8,128)(2,1)S(1)}, u32[]{:S(2)}, u32[]{:S(2)}) collective-permute-start(bf16[256,256]{1,0:T(8,128)(2,1)S(1)} %get-tuple-element.27), channel_id=1, source_target_pairs={{0,385},{16,1},{1,384},{17,0},{128,257},{144,129},{129,256},{145,1... | collective-permute-start | bytes 393224 | tf_op jit(solution)/shard_map/ppermute | solution.py:174
  13.1 5.1 %collective-permute-start.2 = (bf16[256,256]{1,0:T(8,128)(2,1)S(1)}, bf16[256,256]{1,0:T(8,128)(2,1)S(1)}, u32[]{:S(2)}, u32[]{:S(2)}) collective-permute-start(bf16[256,256]{1,0:T(8,128)(2,1)S(1)} %get-tuple-element.27), channel_id=1, source_target_pairs={{0,1},{16,385},{1,0},{17,384},{128,129},{144,257},{129,128},{145,2... | collective-permute-start | bytes 393224 | tf_op jit(solution)/shard_map/ppermute | solution.py:174
  18.2 2.4 %collective-permute-start.1 = (bf16[256,256]{1,0:T(8,128)(2,1)S(1)}, bf16[256,256]{1,0:T(8,128)(2,1)S(1)}, u32[]{:S(2)}, u32[]{:S(2)}) collective-permute-start(bf16[256,256]{1,0:T(8,128)(2,1)S(1)} %get-tuple-element.26), channel_id=1, source_target_pairs={{16,384},{17,385},{144,256},{145,257},{256,144},{257,145},{384,16}... | collective-permute-start | bytes 393224 | tf_op jit(solution)/shard_map/ppermute | solution.py:174
  20.6 1.9 %collective-permute-start = (bf16[256,256]{1,0:T(8,128)(2,1)S(1)}, bf16[256,256]{1,0:T(8,128)(2,1)S(1)}, u32[]{:S(2)}, u32[]{:S(2)}) collective-permute-start(bf16[256,256]{1,0:T(8,128)(2,1)S(1)} %get-tuple-element.26), channel_id=1, source_target_pairs={{0,384},{16,0},{1,385},{17,1},{128,256},{144,128},{129,257},{145,1... | collective-permute-start | bytes 393224 | tf_op jit(solution)/shard_map/ppermute | solution.py:174
  22.5 0.4 collective-permute-done.2
  23.0 5.4 %collective-permute-done.1 = bf16[256,256]{1,0:T(8,128)(2,1)S(1)} collective-permute-done((bf16[256,256]{1,0:T(8,128)(2,1)S(1)}, bf16[256,256]{1,0:T(8,128)(2,1)S(1)}, u32[]{:S(2)}, u32[]{:S(2)}) %collective-permute-start.1) | collective-permute-done | bytes 131104 | tf_op jit(solution)/shard_map/ppermute | solution.py:174
  28.3 1.4 collective-permute-done
  29.9 1.9 %collective-permute-start.9 = (bf16[256,1024]{1,0:T(8,128)(2,1)S(1)}, bf16[256,1024]{1,0:T(8,128)(2,1)S(1)}, u32[]{:S(2)}, u32[]{:S(2)}) collective-permute-start(bf16[256,1024]{1,0:T(8,128)(2,1)S(1)} %pad_maximum_fusion.refs_0_), channel_id=1, source_target_pairs={{0,192},{64,128},{128,64},{192,0},{1,193},{65,129},{129,65},{193,1... | collective-permute-start | bytes 1572872 | tf_op jit(solution)/shard_map/ppermute | solution.py:138
  31.8 8.8 %collective-permute-start.7 = (bf16[256,1024]{1,0:T(8,128)(2,1)S(1)}, bf16[256,1024]{1,0:T(8,128)(2,1)S(1)}, u32[]{:S(2)}, u32[]{:S(2)}) collective-permute-start(bf16[256,1024]{1,0:T(8,128)(2,1)S(1)} %pad_maximum_fusion.refs_0_), channel_id=1, source_target_pairs={{0,128},{128,0},{1,129},{129,1},{2,130},{130,2},{3,131},{131,3},{4... | collective-permute-start | bytes 1572872 | tf_op jit(solution)/shard_map/ppermute | solution.py:134
  40.5 1.9 %collective-permute-start.5 = (bf16[256,1024]{1,0:T(8,128)(2,1)S(1)}, bf16[256,1024]{1,0:T(8,128)(2,1)S(1)}, u32[]{:S(2)}, u32[]{:S(2)}) collective-permute-start(bf16[256,1024]{1,0:T(8,128)(2,1)S(1)} %pad_maximum_fusion.refs_0_), channel_id=1, source_target_pairs={{0,64},{64,0},{1,65},{65,1},{2,66},{66,2},{3,67},{67,3},{4,68},{68... | collective-permute-start | bytes 1572872 | tf_op jit(solution)/shard_map/ppermute | solution.py:134
  42.5 1.9 %collective-permute-start.4 = (bf16[256,1024]{1,0:T(8,128)(2,1)S(1)}, bf16[256,1024]{1,0:T(8,128)(2,1)S(1)}, u32[]{:S(2)}, u32[]{:S(2)}) collective-permute-start(bf16[256,1024]{1,0:T(8,128)(2,1)S(1)} %pad_maximum_fusion.refs_0_), channel_id=1, source_target_pairs={{0,32},{32,0},{1,33},{33,1},{2,34},{34,2},{3,35},{35,3},{4,36},{36... | collective-permute-start | bytes 1572872 | tf_op jit(solution)/shard_map/ppermute | solution.py:134
  44.4 4.7 %collective-permute-done.9.refs_6_ = bf16[256,1024]{1,0:T(8,128)(2,1)S(1)} collective-permute-done((bf16[256,1024]{1,0:T(8,128)(2,1)S(1)}, bf16[256,1024]{1,0:T(8,128)(2,1)S(1)}, u32[]{:S(2)}, u32[]{:S(2)}) %collective-permute-start.9) | collective-permute-done | bytes 524320 | tf_op jit(solution)/shard_map/ppermute | solution.py:138
  49.1 1.9 %collective-permute-start.10 = (bf16[256,1024]{1,0:T(8,128)(2,1)S(1)}, bf16[256,1024]{1,0:T(8,128)(2,1)S(1)}, u32[]{:S(2)}, u32[]{:S(2)}) collective-permute-start(bf16[256,1024]{1,0:T(8,128)(2,1)S(1)} %collective-permute-done.9.refs_6_), channel_id=1, source_target_pairs={{0,32},{32,0},{1,33},{33,1},{2,34},{34,2},{3,35},{35,3},{4,36},{36... | collective-permute-start | bytes 1572872 | tf_op jit(solution)/shard_map/ppermute | solution.py:134
  51.0 7.0 %collective-permute-done.7.refs_4_ = bf16[256,1024]{1,0:T(8,128)(2,1)S(1)} collective-permute-done((bf16[256,1024]{1,0:T(8,128)(2,1)S(1)}, bf16[256,1024]{1,0:T(8,128)(2,1)S(1)}, u32[]{:S(2)}, u32[]{:S(2)}) %collective-permute-start.7) | collective-permute-done | bytes 524320 | tf_op jit(solution)/shard_map/ppermute | solution.py:134
  57.9 1.9 %collective-permute-start.8 = (bf16[256,1024]{1,0:T(8,128)(2,1)S(1)}, bf16[256,1024]{1,0:T(8,128)(2,1)}, u32[]{:S(2)}, u32[]{:S(2)}) collective-permute-start(bf16[256,1024]{1,0:T(8,128)(2,1)S(1)} %collective-permute-done.7.refs_4_), channel_id=1, source_target_pairs={{0,32},{32,0},{1,33},{33,1},{2,34},{34,2},{3,35},{35,3},{4,36},{36... | collective-permute-start | bytes 1572872 | tf_op jit(solution)/shard_map/ppermute | solution.py:134
  59.9 2.4 %collective-permute-start.6 = (bf16[256,1024]{1,0:T(8,128)(2,1)S(1)}, bf16[256,1024]{1,0:T(8,128)(2,1)}, u32[]{:S(2)}, u32[]{:S(2)}) collective-permute-start(bf16[256,1024]{1,0:T(8,128)(2,1)S(1)} %collective-permute-done.5.refs_2_), channel_id=1, source_target_pairs={{0,32},{32,0},{1,33},{33,1},{2,34},{34,2},{3,35},{35,3},{4,36},{36... | collective-permute-start | bytes 1572872 | tf_op jit(solution)/shard_map/ppermute | solution.py:134
  62.3 0.1 stack.23.me
  62.4 1.5 collective-permute-done.6.refs_3_
  63.9 3.3 %all-gather.2.cloned.1.call-done.enc = bf16[8,256,256]{2,1,0:T(8,128)(2,1)} async-done(((bf16[1,256,256]{2,1,0:T(8,128)(2,1)}), bf16[8,256,256]{2,1,0:T(8,128)(2,1)}) %all-gather.2.cloned.1.call-update) | async-done | bytes 1048592 | tf_op jit(solution)/shard_map/all_gather | solution.py:192
  67.3 1.2 copy-done.8
  68.5 2.5 %shard_map.101 = bf16[4,256,256]{2,1,0:T(8,128)(2,1)S(1)} custom-call(s32[5]{0:T(128)S(1)} %stack.23.me, bf16[8,256,256]{2,1,0:T(8,128)(2,1)S(1)} %copy-done.8, bf16[256,1024]{1,0:T(8,128)(2,1)S(1)} %pad_maximum_fusion.refs_0_, bf16[256,1024]{1,0:T(8,128)(2,1)S(1)} %collective-permute-done.4.refs_1_, bf16[256,1024]{1,0:T(8,128)(2,1)S(1)} %collective-permute-done.5.refs_2_, ...), custom_call_target="tpu_custom_call" | custom-call | flops 1073741824 | bytes 5242880 | tf_op jit(solution)/shard_map/pallas_call | solution.py:225
  71.1 9.5 %all_to_all.10.arrived = bf16[4,256,256]{2,1,0:T(8,128)(2,1)S(1)} all-to-all(bf16[4,256,256]{2,1,0:T(8,128)(2,1)S(1)} %shard_map.101), channel_id=1, replica_groups=mesh['yh'=2,'yl'=2,'xh'=2,'c'=2,'s'=2,'zr'=8,'z0'=2] {'z0','s'}, dimensions={0} | all-to-all | bytes 1048576 | tf_op jit(solution)/shard_map/all_to_all | solution.py:228
  80.6 2.8 %shard_map.102 = (bf16[256,128]{1,0:T(8,128)(2,1)}, bf16[256,128]{1,0:T(8,128)(2,1)}, bf16[4,256,256]{2,1,0:T(8,128)(2,1)S(1)}) custom-call(s32[1,8]{1,0:T(1,128)S(1)} %copy-done.12, bf16[4,256,256]{2,1,0:T(8,128)(2,1)S(1)} %all_to_all.10.arrived, bf16[256,128]{1,0:T(8,128)(2,1)S(1)} %bitcast.17, bf16[256,128]{1,0:T(8,128)(2,1)S(1)} %bitcast.18), custom_call_target="tpu_custom_call" | custom-call | flops 25165824 | bytes 1048576 | tf_op jit(solution)/shard_map/pallas_call | solution.py:231
  83.4 9.5 %all_to_all.11.grads = bf16[4,256,256]{2,1,0:T(8,128)(2,1)S(1)} all-to-all(bf16[4,256,256]{2,1,0:T(8,128)(2,1)S(1)} %get-tuple-element.12), channel_id=1, replica_groups=mesh['yh'=2,'yl'=2,'xh'=2,'c'=2,'s'=2,'zr'=8,'z0'=2] {'z0','s'}, dimensions={0} | all-to-all | bytes 1048576 | tf_op jit(solution)/shard_map/all_to_all | solution.py:244
  92.9 3.2 %shard_map.104 = (bf16[16,256,256]{2,1,0:T(8,128)(2,1)S(1)}, bf16[16,256,256]{2,1,0:T(8,128)(2,1)}) custom-call(s32[5]{0:T(128)S(1)} %stack.23.me, bf16[8,256,256]{2,1,0:T(8,128)(2,1)S(1)} %copy-done.9, bf16[4,256,256]{2,1,0:T(8,128)(2,1)S(1)} %all_to_all.11.grads), custom_call_target="tpu_custom_call" | custom-call | flops 1073741824 | bytes 5242880 | tf_op jit(solution)/shard_map/pallas_call | solution.py:257
  96.1 1.9 %collective-permute-start.11 = (bf16[16,256,256]{2,1,0:T(8,128)(2,1)}, bf16[16,256,256]{2,1,0:T(8,128)(2,1)}, u32[]{:S(2)}, u32[]{:S(2)}) collective-permute-start(bf16[16,256,256]{2,1,0:T(8,128)(2,1)} %get-tuple-element.14), channel_id=1, source_target_pairs={{0,32},{32,0},{1,33},{33,1},{2,34},{34,2},{3,35},{35,3},{4,36},{36... | collective-permute-start | bytes 6291464 | tf_op jit(solution)/shard_map/ppermute | solution.py:134
  98.1 3.6 %shard_map.103 = bf16[8,256,256]{2,1,0:T(8,128)(2,1)} custom-call(s32[5]{0:T(128)S(1)} %stack.23.me, bf16[4,256,256]{2,1,0:T(8,128)(2,1)S(1)} %all_to_all.11.grads, bf16[256,1024]{1,0:T(8,128)(2,1)S(1)} %pad_maximum_fusion.refs_0_, bf16[256,1024]{1,0:T(8,128)(2,1)S(1)} %copy-done.5, bf16[256,1024]{1,0:T(8,128)(2,1)S(1)} %copy-done.3, ...), custom_call_target="tpu_custom_call" | custom-call | flops 1073741824 | bytes 5242880 | tf_op jit(solution)/shard_map/pallas_call | solution.py:246
  101.7 0.8 collective-permute-done.11
  102.5 2.2 %add_convert_fusion = bf16[16,256,256]{2,1,0:T(8,128)(2,1)S(1)} fusion(bf16[16,256,256]{2,1,0:T(8,128)(2,1)} %collective-permute-done.11, bf16[16,256,256]{2,1,0:T(8,128)(2,1)S(1)} %get-tuple-element.13), kind=kLoop, calls=%fused_computation | loop fusion | flops 4194304 | bytes 6291456 | tf_op jit(solution)/shard_map/convert_element_type | solution.py:260
  104.7 0.1 fusion.1
  104.9 3.4 %collective-permute-start.12 = (bf16[4,256,256]{2,1,0:T(8,128)(2,1)S(1)}, bf16[4,256,256]{2,1,0:T(8,128)(2,1)S(1)}, u32[]{:S(2)}, u32[]{:S(2)}) collective-permute-start(bf16[4,256,256]{2,1,0:T(8,128)(2,1)S(1)} %get-tuple-element.15), channel_id=1, source_target_pairs={{0,128},{128,0},{256,384},{384,256},{1,129},{129,1},{257,385},{385... | collective-permute-start | bytes 1572872 | tf_op jit(solution)/shard_map/ppermute | solution.py:178
  108.2 4.0 %collective-permute-start.14 = (bf16[4,256,256]{2,1,0:T(8,128)(2,1)S(1)}, bf16[4,256,256]{2,1,0:T(8,128)(2,1)S(1)}, u32[]{:S(2)}, u32[]{:S(2)}) collective-permute-start(bf16[4,256,256]{2,1,0:T(8,128)(2,1)S(1)} %get-tuple-element.16), channel_id=1, source_target_pairs={{0,384},{128,256},{256,128},{384,0},{1,385},{129,257},{257,129},{3... | collective-permute-start | bytes 1572872 | tf_op jit(solution)/shard_map/ppermute | solution.py:178
  112.3 2.4 %collective-permute-start.13 = (bf16[4,256,256]{2,1,0:T(8,128)(2,1)S(1)}, bf16[4,256,256]{2,1,0:T(8,128)(2,1)S(1)}, u32[]{:S(2)}, u32[]{:S(2)}) collective-permute-start(bf16[4,256,256]{2,1,0:T(8,128)(2,1)S(1)} %get-tuple-element.17), channel_id=1, source_target_pairs={{0,256},{128,384},{256,0},{384,128},{1,257},{129,385},{257,1},{385... | collective-permute-start | bytes 1572872 | tf_op jit(solution)/shard_map/ppermute | solution.py:178
  114.7 6.8 %collective-permute-done.12 = bf16[4,256,256]{2,1,0:T(8,128)(2,1)S(1)} collective-permute-done((bf16[4,256,256]{2,1,0:T(8,128)(2,1)S(1)}, bf16[4,256,256]{2,1,0:T(8,128)(2,1)S(1)}, u32[]{:S(2)}, u32[]{:S(2)}) %collective-permute-start.12) | collective-permute-done | bytes 524320 | tf_op jit(solution)/shard_map/ppermute | solution.py:178
  121.5 14.7 %collective-permute-done.14 = bf16[4,256,256]{2,1,0:T(8,128)(2,1)S(1)} collective-permute-done((bf16[4,256,256]{2,1,0:T(8,128)(2,1)S(1)}, bf16[4,256,256]{2,1,0:T(8,128)(2,1)S(1)}, u32[]{:S(2)}, u32[]{:S(2)}) %collective-permute-start.14) | collective-permute-done | bytes 524320 | tf_op jit(solution)/shard_map/ppermute | solution.py:178
  136.3 0.3 add_convert_fusion.1
  136.6 4.6 %collective-permute-start.17 = (bf16[256,256]{1,0:T(8,128)(2,1)S(1)}, bf16[256,256]{1,0:T(8,128)(2,1)S(1)}, u32[]{:S(2)}, u32[]{:S(2)}) collective-permute-start(bf16[256,256]{1,0:T(8,128)(2,1)S(1)} %get-tuple-element.20), channel_id=1, source_target_pairs={{65,0},{64,1},{449,16},{448,17},{1,64},{0,65},{385,80},{384,81},{1... | collective-permute-start | bytes 393224 | tf_op jit(solution)/shard_map/ppermute | solution.py:188
  141.1 5.0 %collective-permute-start.18 = (bf16[256,256]{1,0:T(8,128)(2,1)S(1)}, bf16[256,256]{1,0:T(8,128)(2,1)S(1)}, u32[]{:S(2)}, u32[]{:S(2)}) collective-permute-start(bf16[256,256]{1,0:T(8,128)(2,1)S(1)} %get-tuple-element.21), channel_id=1, source_target_pairs={{1,0},{0,1},{385,16},{384,17},{65,64},{64,65},{449,80},{448,81},{1... | collective-permute-start | bytes 393224 | tf_op jit(solution)/shard_map/ppermute | solution.py:188
  146.1 3.5 %collective-permute-start.16 = (bf16[256,256]{1,0:T(8,128)(2,1)S(1)}, bf16[256,256]{1,0:T(8,128)(2,1)S(1)}, u32[]{:S(2)}, u32[]{:S(2)}) collective-permute-start(bf16[256,256]{1,0:T(8,128)(2,1)S(1)} %get-tuple-element.22), channel_id=1, source_target_pairs={{0,0},{1,1},{384,16},{385,17},{64,64},{65,65},{448,80},{449,81},{1... | collective-permute-start | bytes 393224 | tf_op jit(solution)/shard_map/ppermute | solution.py:188
  149.7 4.9 %collective-permute-start.15 = (bf16[256,256]{1,0:T(8,128)(2,1)S(1)}, bf16[256,256]{1,0:T(8,128)(2,1)S(1)}, u32[]{:S(2)}, u32[]{:S(2)}) collective-permute-start(bf16[256,256]{1,0:T(8,128)(2,1)S(1)} %get-tuple-element.23), channel_id=1, source_target_pairs={{64,0},{65,1},{448,16},{449,17},{0,64},{1,65},{384,80},{385,81},{1... | collective-permute-start | bytes 393224 | tf_op jit(solution)/shard_map/ppermute | solution.py:188
  154.6 0.1 collective-permute-done.17
  154.7 4.2 %collective-permute-done.18 = bf16[256,256]{1,0:T(8,128)(2,1)S(1)} collective-permute-done((bf16[256,256]{1,0:T(8,128)(2,1)S(1)}, bf16[256,256]{1,0:T(8,128)(2,1)S(1)}, u32[]{:S(2)}, u32[]{:S(2)}) %collective-permute-start.18) | collective-permute-done | bytes 131104 | tf_op jit(solution)/shard_map/ppermute | solution.py:188
  158.9 0.4 collective-permute-done.16
  159.3 1.0 collective-permute-done.15
  160.3 0.1 broadcast_select_fusion
  160.4 0.7 pad_maximum_fusion.1
  (40 shorter events, 0.4 us)
Async XLA Ops:
  7.2 60.1 %all-gather.2.cloned.1.call-start = ((), (), s32[]{:S(2)}) async-start(), calls=%async_computation.3 | async-start | bytes 1179648 | tf_op jit(solution)/shard_map/all_gather | solution.py:192
  7.9 153.2 %reduce-scatter.2.cloned.1.call-start = ((), (), s32[]{:S(2)}) async-start(), calls=%async_computation.4 | async-start | bytes 1179648 | tf_op jit(solution)/shard_map/reduce_scatter | solution.py:254
  9.0 13.6 %collective-permute-start.3 = (bf16[256,256]{1,0:T(8,128)(2,1)S(1)}, bf16[256,256]{1,0:T(8,128)(2,1)S(1)}, u32[]{:S(2)}, u32[]{:S(2)}) collective-permute-start(bf16[256,256]{1,0:T(8,128)(2,1)S(1)} %get-tuple-element.27), channel_id=1, source_target_pairs={{0,385},{16,1},{1,384},{17,0},{128,257},{144,129},{129,256},{145,1... | collective-permute-start | bytes 393224 | tf_op jit(solution)/shard_map/ppermute | solution.py:174
  13.1 9.9 %collective-permute-start.2 = (bf16[256,256]{1,0:T(8,128)(2,1)S(1)}, bf16[256,256]{1,0:T(8,128)(2,1)S(1)}, u32[]{:S(2)}, u32[]{:S(2)}) collective-permute-start(bf16[256,256]{1,0:T(8,128)(2,1)S(1)} %get-tuple-element.27), channel_id=1, source_target_pairs={{0,1},{16,385},{1,0},{17,384},{128,129},{144,257},{129,128},{145,2... | collective-permute-start | bytes 393224 | tf_op jit(solution)/shard_map/ppermute | solution.py:174
  18.2 10.1 %collective-permute-start.1 = (bf16[256,256]{1,0:T(8,128)(2,1)S(1)}, bf16[256,256]{1,0:T(8,128)(2,1)S(1)}, u32[]{:S(2)}, u32[]{:S(2)}) collective-permute-start(bf16[256,256]{1,0:T(8,128)(2,1)S(1)} %get-tuple-element.26), channel_id=1, source_target_pairs={{16,384},{17,385},{144,256},{145,257},{256,144},{257,145},{384,16}... | collective-permute-start | bytes 393224 | tf_op jit(solution)/shard_map/ppermute | solution.py:174
  20.6 9.2 %collective-permute-start = (bf16[256,256]{1,0:T(8,128)(2,1)S(1)}, bf16[256,256]{1,0:T(8,128)(2,1)S(1)}, u32[]{:S(2)}, u32[]{:S(2)}) collective-permute-start(bf16[256,256]{1,0:T(8,128)(2,1)S(1)} %get-tuple-element.26), channel_id=1, source_target_pairs={{0,384},{16,0},{1,385},{17,1},{128,256},{144,128},{129,257},{145,1... | collective-permute-start | bytes 393224 | tf_op jit(solution)/shard_map/ppermute | solution.py:174
  29.9 19.2 %collective-permute-start.9 = (bf16[256,1024]{1,0:T(8,128)(2,1)S(1)}, bf16[256,1024]{1,0:T(8,128)(2,1)S(1)}, u32[]{:S(2)}, u32[]{:S(2)}) collective-permute-start(bf16[256,1024]{1,0:T(8,128)(2,1)S(1)} %pad_maximum_fusion.refs_0_), channel_id=1, source_target_pairs={{0,192},{64,128},{128,64},{192,0},{1,193},{65,129},{129,65},{193,1... | collective-permute-start | bytes 1572872 | tf_op jit(solution)/shard_map/ppermute | solution.py:138
  31.8 26.2 %collective-permute-start.7 = (bf16[256,1024]{1,0:T(8,128)(2,1)S(1)}, bf16[256,1024]{1,0:T(8,128)(2,1)S(1)}, u32[]{:S(2)}, u32[]{:S(2)}) collective-permute-start(bf16[256,1024]{1,0:T(8,128)(2,1)S(1)} %pad_maximum_fusion.refs_0_), channel_id=1, source_target_pairs={{0,128},{128,0},{1,129},{129,1},{2,130},{130,2},{3,131},{131,3},{4... | collective-permute-start | bytes 1572872 | tf_op jit(solution)/shard_map/ppermute | solution.py:134
  40.5 19.3 %collective-permute-start.5 = (bf16[256,1024]{1,0:T(8,128)(2,1)S(1)}, bf16[256,1024]{1,0:T(8,128)(2,1)S(1)}, u32[]{:S(2)}, u32[]{:S(2)}) collective-permute-start(bf16[256,1024]{1,0:T(8,128)(2,1)S(1)} %pad_maximum_fusion.refs_0_), channel_id=1, source_target_pairs={{0,64},{64,0},{1,65},{65,1},{2,66},{66,2},{3,67},{67,3},{4,68},{68... | collective-permute-start | bytes 1572872 | tf_op jit(solution)/shard_map/ppermute | solution.py:134
  42.5 20.0 %collective-permute-start.4 = (bf16[256,1024]{1,0:T(8,128)(2,1)S(1)}, bf16[256,1024]{1,0:T(8,128)(2,1)S(1)}, u32[]{:S(2)}, u32[]{:S(2)}) collective-permute-start(bf16[256,1024]{1,0:T(8,128)(2,1)S(1)} %pad_maximum_fusion.refs_0_), channel_id=1, source_target_pairs={{0,32},{32,0},{1,33},{33,1},{2,34},{34,2},{3,35},{35,3},{4,36},{36... | collective-permute-start | bytes 1572872 | tf_op jit(solution)/shard_map/ppermute | solution.py:134
  49.1 13.4 %collective-permute-start.10 = (bf16[256,1024]{1,0:T(8,128)(2,1)S(1)}, bf16[256,1024]{1,0:T(8,128)(2,1)S(1)}, u32[]{:S(2)}, u32[]{:S(2)}) collective-permute-start(bf16[256,1024]{1,0:T(8,128)(2,1)S(1)} %collective-permute-done.9.refs_6_), channel_id=1, source_target_pairs={{0,32},{32,0},{1,33},{33,1},{2,34},{34,2},{3,35},{35,3},{4,36},{36... | collective-permute-start | bytes 1572872 | tf_op jit(solution)/shard_map/ppermute | solution.py:134
  57.9 13.1 %copy-start = (bf16[256,1024]{1,0:T(8,128)(2,1)}, bf16[256,1024]{1,0:T(8,128)(2,1)S(1)}, u32[]{:S(2)}) copy-start(bf16[256,1024]{1,0:T(8,128)(2,1)S(1)} %collective-permute-done.7.refs_4_) | copy-start | bytes 1572868
  57.9 4.5 %collective-permute-start.8 = (bf16[256,1024]{1,0:T(8,128)(2,1)S(1)}, bf16[256,1024]{1,0:T(8,128)(2,1)}, u32[]{:S(2)}, u32[]{:S(2)}) collective-permute-start(bf16[256,1024]{1,0:T(8,128)(2,1)S(1)} %collective-permute-done.7.refs_4_), channel_id=1, source_target_pairs={{0,32},{32,0},{1,33},{33,1},{2,34},{34,2},{3,35},{35,3},{4,36},{36... | collective-permute-start | bytes 1572872 | tf_op jit(solution)/shard_map/ppermute | solution.py:134
  59.9 11.2 %copy-start.2 = (bf16[256,1024]{1,0:T(8,128)(2,1)}, bf16[256,1024]{1,0:T(8,128)(2,1)S(1)}, u32[]{:S(2)}) copy-start(bf16[256,1024]{1,0:T(8,128)(2,1)S(1)} %collective-permute-done.5.refs_2_) | copy-start | bytes 1572868
  59.9 4.1 %collective-permute-start.6 = (bf16[256,1024]{1,0:T(8,128)(2,1)S(1)}, bf16[256,1024]{1,0:T(8,128)(2,1)}, u32[]{:S(2)}, u32[]{:S(2)}) collective-permute-start(bf16[256,1024]{1,0:T(8,128)(2,1)S(1)} %collective-permute-done.5.refs_2_), channel_id=1, source_target_pairs={{0,32},{32,0},{1,33},{33,1},{2,34},{34,2},{3,35},{35,3},{4,36},{36... | collective-permute-start | bytes 1572872 | tf_op jit(solution)/shard_map/ppermute | solution.py:134
  62.3 18.3 %copy-start.12 = (s32[1,8]{1,0:T(1,128)S(1)}, s32[1,8]{1,0:T(1,128)}, u32[]{:S(2)}) copy-start(s32[1,8]{1,0:T(1,128)} %ids.1) | copy-start | bytes 100
  62.4 8.7 %copy-start.4 = (bf16[256,1024]{1,0:T(8,128)(2,1)}, bf16[256,1024]{1,0:T(8,128)(2,1)S(1)}, u32[]{:S(2)}) copy-start(bf16[256,1024]{1,0:T(8,128)(2,1)S(1)} %collective-permute-done.4.refs_1_) | copy-start | bytes 1572868
  62.4 8.7 %copy-start.6 = (bf16[256,1024]{1,0:T(8,128)(2,1)}, bf16[256,1024]{1,0:T(8,128)(2,1)S(1)}, u32[]{:S(2)}) copy-start(bf16[256,1024]{1,0:T(8,128)(2,1)S(1)} %collective-permute-done.10.refs_7_) | copy-start | bytes 1572868
  67.3 1.2 copy-start.8
  68.5 12.1 %copy-start.10 = (bf16[1,256,128]{2,1,0:T(8,128)(2,1)S(1)}, bf16[1,256,128]{2,1,0:T(8,128)(2,1)}, u32[]{:S(2)}) copy-start(bf16[1,256,128]{2,1,0:T(8,128)(2,1)} %param.6) | copy-start | bytes 196612
  68.5 12.1 %copy-start.11 = (bf16[1,256,128]{2,1,0:T(8,128)(2,1)S(1)}, bf16[1,256,128]{2,1,0:T(8,128)(2,1)}, u32[]{:S(2)}) copy-start(bf16[1,256,128]{2,1,0:T(8,128)(2,1)} %param.11) | copy-start | bytes 196612
  71.1 21.8 %copy-start.9 = (bf16[8,256,256]{2,1,0:T(8,128)(2,1)S(1)}, bf16[8,256,256]{2,1,0:T(8,128)(2,1)}, u32[]{:S(2)}) copy-start(bf16[8,256,256]{2,1,0:T(8,128)(2,1)} %all-gather.2.cloned.1.call-done.enc) | copy-start | bytes 3145732
  92.9 5.1 %copy-start.1 = (bf16[256,1024]{1,0:T(8,128)(2,1)S(1)}, bf16[256,1024]{1,0:T(8,128)(2,1)}, u32[]{:S(2)}) copy-start(bf16[256,1024]{1,0:T(8,128)(2,1)} %copy-done) | copy-start | bytes 1572868
  92.9 5.1 %copy-start.3 = (bf16[256,1024]{1,0:T(8,128)(2,1)S(1)}, bf16[256,1024]{1,0:T(8,128)(2,1)}, u32[]{:S(2)}) copy-start(bf16[256,1024]{1,0:T(8,128)(2,1)} %copy-done.2) | copy-start | bytes 1572868
  92.9 5.1 %copy-start.5 = (bf16[256,1024]{1,0:T(8,128)(2,1)S(1)}, bf16[256,1024]{1,0:T(8,128)(2,1)}, u32[]{:S(2)}) copy-start(bf16[256,1024]{1,0:T(8,128)(2,1)} %copy-done.4) | copy-start | bytes 1572868
  92.9 5.2 %copy-start.7 = (bf16[256,1024]{1,0:T(8,128)(2,1)S(1)}, bf16[256,1024]{1,0:T(8,128)(2,1)}, u32[]{:S(2)}) copy-start(bf16[256,1024]{1,0:T(8,128)(2,1)} %copy-done.6) | copy-start | bytes 1572868
  96.1 6.4 %collective-permute-start.11 = (bf16[16,256,256]{2,1,0:T(8,128)(2,1)}, bf16[16,256,256]{2,1,0:T(8,128)(2,1)}, u32[]{:S(2)}, u32[]{:S(2)}) collective-permute-start(bf16[16,256,256]{2,1,0:T(8,128)(2,1)} %get-tuple-element.14), channel_id=1, source_target_pairs={{0,32},{32,0},{1,33},{33,1},{2,34},{34,2},{3,35},{35,3},{4,36},{36... | collective-permute-start | bytes 6291464 | tf_op jit(solution)/shard_map/ppermute | solution.py:134
  104.9 16.7 %collective-permute-start.12 = (bf16[4,256,256]{2,1,0:T(8,128)(2,1)S(1)}, bf16[4,256,256]{2,1,0:T(8,128)(2,1)S(1)}, u32[]{:S(2)}, u32[]{:S(2)}) collective-permute-start(bf16[4,256,256]{2,1,0:T(8,128)(2,1)S(1)} %get-tuple-element.15), channel_id=1, source_target_pairs={{0,128},{128,0},{256,384},{384,256},{1,129},{129,1},{257,385},{385... | collective-permute-start | bytes 1572872 | tf_op jit(solution)/shard_map/ppermute | solution.py:178
  108.2 28.0 %collective-permute-start.14 = (bf16[4,256,256]{2,1,0:T(8,128)(2,1)S(1)}, bf16[4,256,256]{2,1,0:T(8,128)(2,1)S(1)}, u32[]{:S(2)}, u32[]{:S(2)}) collective-permute-start(bf16[4,256,256]{2,1,0:T(8,128)(2,1)S(1)} %get-tuple-element.16), channel_id=1, source_target_pairs={{0,384},{128,256},{256,128},{384,0},{1,385},{129,257},{257,129},{3... | collective-permute-start | bytes 1572872 | tf_op jit(solution)/shard_map/ppermute | solution.py:178
  112.3 24.0 %collective-permute-start.13 = (bf16[4,256,256]{2,1,0:T(8,128)(2,1)S(1)}, bf16[4,256,256]{2,1,0:T(8,128)(2,1)S(1)}, u32[]{:S(2)}, u32[]{:S(2)}) collective-permute-start(bf16[4,256,256]{2,1,0:T(8,128)(2,1)S(1)} %get-tuple-element.17), channel_id=1, source_target_pairs={{0,256},{128,384},{256,0},{384,128},{1,257},{129,385},{257,1},{385... | collective-permute-start | bytes 1572872 | tf_op jit(solution)/shard_map/ppermute | solution.py:178
  136.6 18.1 %collective-permute-start.17 = (bf16[256,256]{1,0:T(8,128)(2,1)S(1)}, bf16[256,256]{1,0:T(8,128)(2,1)S(1)}, u32[]{:S(2)}, u32[]{:S(2)}) collective-permute-start(bf16[256,256]{1,0:T(8,128)(2,1)S(1)} %get-tuple-element.20), channel_id=1, source_target_pairs={{65,0},{64,1},{449,16},{448,17},{1,64},{0,65},{385,80},{384,81},{1... | collective-permute-start | bytes 393224 | tf_op jit(solution)/shard_map/ppermute | solution.py:188
  141.1 17.7 %collective-permute-start.18 = (bf16[256,256]{1,0:T(8,128)(2,1)S(1)}, bf16[256,256]{1,0:T(8,128)(2,1)S(1)}, u32[]{:S(2)}, u32[]{:S(2)}) collective-permute-start(bf16[256,256]{1,0:T(8,128)(2,1)S(1)} %get-tuple-element.21), channel_id=1, source_target_pairs={{1,0},{0,1},{385,16},{384,17},{65,64},{64,65},{449,80},{448,81},{1... | collective-permute-start | bytes 393224 | tf_op jit(solution)/shard_map/ppermute | solution.py:188
  146.1 13.2 %collective-permute-start.16 = (bf16[256,256]{1,0:T(8,128)(2,1)S(1)}, bf16[256,256]{1,0:T(8,128)(2,1)S(1)}, u32[]{:S(2)}, u32[]{:S(2)}) collective-permute-start(bf16[256,256]{1,0:T(8,128)(2,1)S(1)} %get-tuple-element.22), channel_id=1, source_target_pairs={{0,0},{1,1},{384,16},{385,17},{64,64},{65,65},{448,80},{449,81},{1... | collective-permute-start | bytes 393224 | tf_op jit(solution)/shard_map/ppermute | solution.py:188
  149.7 10.6 %collective-permute-start.15 = (bf16[256,256]{1,0:T(8,128)(2,1)S(1)}, bf16[256,256]{1,0:T(8,128)(2,1)S(1)}, u32[]{:S(2)}, u32[]{:S(2)}) collective-permute-start(bf16[256,256]{1,0:T(8,128)(2,1)S(1)} %get-tuple-element.23), channel_id=1, source_target_pairs={{64,0},{65,1},{448,16},{449,17},{0,64},{1,65},{384,80},{385,81},{1... | collective-permute-start | bytes 393224 | tf_op jit(solution)/shard_map/ppermute | solution.py:188
Sparse Core Ops, SparseCore 0:
  10.1 57.1 all-gather.1
  101.8 56.0 reduce-scatter.1

commit v6 on v5

--- a/solution.py
+++ b/solution.py
@@ -47,12 +47,12 @@
 
 def project_body(me, enc, *refs):
     weights, out = refs[:PIECES], refs[PIECES]
+    blocks = [enc[jnp.bitwise_xor(me[0], piece)] for piece in range(PIECES)]
+    wide = jnp.concatenate(blocks, axis=1)
     for head in range(GROUP):
         columns = slice(head * WIDE, (head + 1) * WIDE)
-        total = jnp.zeros((ROWS, WIDE), F32)
-        for piece in range(PIECES):
-            block = enc[jnp.bitwise_xor(me[0], piece)]
-            total = total + dot(block, weights[piece][:, columns], (1, 0))
+        rows = jnp.concatenate([piece[:, columns] for piece in weights], axis=0)
+        total = dot(wide, rows, (1, 0))
         out[jnp.bitwise_xor(me[1], head)] = total.astype(BF16)
 
 
@@ -73,25 +73,32 @@
 
     query_blocks = to_blocks(queries[...])
     grad_blocks = to_blocks(grads[...])
-    for span in range(SPANS):
-        starts = [pl.multiple_of(ids[0, span * 2 + j] * NTOK, NTOK) for j in range(2)]
-        taken = jnp.concatenate([kv[pl.ds(start, NTOK), :] for start in starts], axis=0)
-        span_keys, span_values = taken[:, :HD], taken[:, HD:]
-        q = query_blocks[span * CLEN : (span + 1) * CLEN, :]
-        g = grad_blocks[span * CLEN : (span + 1) * CLEN, :]
-        exponent = jnp.exp(dot(q, span_keys, (1, 1)) * inverse_root)
-        probs = exponent / jnp.sum(exponent, -1, keepdims=True)
-        attn = probs.astype(BF16)
-        dprob = dot(g, span_values, (1, 1))
-        scaled = (
-            probs * (dprob - jnp.sum(probs * dprob, -1, keepdims=True)) * inverse_root
-        ).astype(BF16)
-        forward[span * CLEN : (span + 1) * CLEN, :] = dot(attn, span_values, (1, 0))
-        back[span * CLEN : (span + 1) * CLEN, :] = dot(scaled, span_keys, (1, 0))
-        grad_rows = jnp.concatenate([dot(scaled, q, (0, 0)), dot(attn, g, (0, 0))], axis=1)
-        grad_rows = grad_rows.astype(BF16)
-        for j in range(2):
-            grad_kv[0, pl.ds(starts[j], NTOK), :] = grad_rows[j * NTOK : (j + 1) * NTOK, :]
+    spans = range(SPANS)
+    rows = [slice(span * CLEN, (span + 1) * CLEN) for span in spans]
+    starts = [pl.multiple_of(ids[0, entry] * NTOK, NTOK) for entry in range(2 * SPANS)]
+    pool = [kv[pl.ds(start, NTOK), :] for start in starts]
+    taken = [jnp.concatenate(pool[2 * span : 2 * span + 2], axis=0) for span in spans]
+    keys, values = [x[:, :HD] for x in taken], [x[:, HD:] for x in taken]
+    qs, gs = [query_blocks[r, :] for r in rows], [grad_blocks[r, :] for r in rows]
+    exponents = [jnp.exp(dot(q, k, (1, 1)) * inverse_root) for q, k in zip(qs, keys, strict=True)]
+    dprobs = [dot(g, v, (1, 1)) for g, v in zip(gs, values, strict=True)]
+    probs = [x / jnp.sum(x, -1, keepdims=True) for x in exponents]
+    attns = [p.astype(BF16) for p in probs]
+    scaled = [
+        (p * (d - jnp.sum(p * d, -1, keepdims=True)) * inverse_root).astype(BF16)
+        for p, d in zip(probs, dprobs, strict=True)
+    ]
+    for span in spans:
+        forward[rows[span], :] = dot(attns[span], values[span], (1, 0))
+    for span in spans:
+        back[rows[span], :] = dot(scaled[span], keys[span], (1, 0))
+    grad_rows = [
+        jnp.concatenate([dot(sg, q, (0, 0)), dot(attn, g, (0, 0))], axis=1).astype(BF16)
+        for sg, q, attn, g in zip(scaled, qs, attns, gs, strict=True)
+    ]
+    for entry in range(2 * SPANS):
+        part = (entry % 2) * NTOK
+        grad_kv[0, pl.ds(starts[entry], NTOK), :] = grad_rows[entry // 2][part : part + NTOK, :]
     for copy in range(1, GROUP):
         grad_kv[copy] = grad_kv[0]
     context[...] = from_blocks(forward[...])

time: 169 us -> 168 us (level)
  no operation moved by 1% of the time
where the time goes in v6:
time: 168 us; the launch traced here: 167 us
  starting transfers between devices  64.1 us (38%)
  waiting for transfers between devices  52.5 us (31%)
  blocking collectives  19 us (11%)
  between operations  14.4 us (9%)
  Pallas kernels  11 us (7%)
  other arithmetic  3.44 us (2%)
  local copies, waits for them, and re-layouts  2.46 us (1%)
    ppermute x3, waiting for transfers between devices, hop(): return lax.ppermute(x, ('yh', 'yl'), [(i, i ^ by) for i in range(4)])  21.6 us
    ppermute x7, starting transfers between devices, swap(): return lax.ppermute(x, axis, [(0, 1), (1, 0)])  20.7 us
    ppermute x4, starting transfers between devices, turn_back(): return lax.ppermute(x, ('yh', 'yl', 'xh', 's', 'z0'), pairs)  18 us
    ppermute x4, starting transfers between devices, send(): return lax.ppermute(x, Y_AXES, pairs)  13.5 us
    ppermute x3, starting transfers between devices, hop(): return lax.ppermute(x, ('yh', 'yl'), [(i, i ^ by) for i in range(4)])  9.82 us
    all_to_all x1, blocking collectives, per_device(): arrived = lax.all_to_all(terms, ('z0', 's'), 0, 0, tiled=True)  9.52 us
    all_to_all x1, blocking collectives, per_device(): grads = lax.all_to_all(copies, ('z0', 's'), 0, 0, tiled=True)  9.51 us
    ppermute x7, waiting for transfers between devices, swap(): return lax.ppermute(x, axis, [(0, 1), (1, 0)])  9.3 us
  transfers between devices with their start and end apart: 21, of which 14 were waited for; matrix products, arithmetic and copies ran while one was open for 3% of the time, Pallas kernels for 2%

profile of v6, /device:TPU:6, one launch (start us, length us, event | category | flops | bytes accessed | tf_op | source)
XLA Modules:
  0.0 167.0 jit_solution(14876582240197872614)
XLA Ops:
  7.2 0.7 all-gather.2.cloned.1.call-update
  8.0 1.0 fusion.2
  9.0 4.1 %collective-permute-start.3 = (bf16[256,256]{1,0:T(8,128)(2,1)S(1)}, bf16[256,256]{1,0:T(8,128)(2,1)S(1)}, u32[]{:S(2)}, u32[]{:S(2)}) collective-permute-start(bf16[256,256]{1,0:T(8,128)(2,1)S(1)} %get-tuple-element.27), channel_id=1, source_target_pairs={{0,385},{16,1},{1,384},{17,0},{128,257},{144,129},{129,256},{145,1... | collective-permute-start | bytes 393224 | tf_op jit(solution)/shard_map/ppermute | solution.py:181
  13.1 5.1 %collective-permute-start.2 = (bf16[256,256]{1,0:T(8,128)(2,1)S(1)}, bf16[256,256]{1,0:T(8,128)(2,1)S(1)}, u32[]{:S(2)}, u32[]{:S(2)}) collective-permute-start(bf16[256,256]{1,0:T(8,128)(2,1)S(1)} %get-tuple-element.27), channel_id=1, source_target_pairs={{0,1},{16,385},{1,0},{17,384},{128,129},{144,257},{129,128},{145,2... | collective-permute-start | bytes 393224 | tf_op jit(solution)/shard_map/ppermute | solution.py:181
  18.2 2.4 %collective-permute-start.1 = (bf16[256,256]{1,0:T(8,128)(2,1)S(1)}, bf16[256,256]{1,0:T(8,128)(2,1)S(1)}, u32[]{:S(2)}, u32[]{:S(2)}) collective-permute-start(bf16[256,256]{1,0:T(8,128)(2,1)S(1)} %get-tuple-element.26), channel_id=1, source_target_pairs={{16,384},{17,385},{144,256},{145,257},{256,144},{257,145},{384,16}... | collective-permute-start | bytes 393224 | tf_op jit(solution)/shard_map/ppermute | solution.py:181
  20.6 1.9 %collective-permute-start = (bf16[256,256]{1,0:T(8,128)(2,1)S(1)}, bf16[256,256]{1,0:T(8,128)(2,1)S(1)}, u32[]{:S(2)}, u32[]{:S(2)}) collective-permute-start(bf16[256,256]{1,0:T(8,128)(2,1)S(1)} %get-tuple-element.26), channel_id=1, source_target_pairs={{0,384},{16,0},{1,385},{17,1},{128,256},{144,128},{129,257},{145,1... | collective-permute-start | bytes 393224 | tf_op jit(solution)/shard_map/ppermute | solution.py:181
  22.5 0.4 collective-permute-done.2
  23.0 5.4 %collective-permute-done.1 = bf16[256,256]{1,0:T(8,128)(2,1)S(1)} collective-permute-done((bf16[256,256]{1,0:T(8,128)(2,1)S(1)}, bf16[256,256]{1,0:T(8,128)(2,1)S(1)}, u32[]{:S(2)}, u32[]{:S(2)}) %collective-permute-start.1) | collective-permute-done | bytes 131104 | tf_op jit(solution)/shard_map/ppermute | solution.py:181
  28.3 1.4 collective-permute-done
  29.9 1.9 %collective-permute-start.9 = (bf16[256,1024]{1,0:T(8,128)(2,1)S(1)}, bf16[256,1024]{1,0:T(8,128)(2,1)S(1)}, u32[]{:S(2)}, u32[]{:S(2)}) collective-permute-start(bf16[256,1024]{1,0:T(8,128)(2,1)S(1)} %pad_maximum_fusion.refs_0_), channel_id=1, source_target_pairs={{0,192},{64,128},{128,64},{192,0},{1,193},{65,129},{129,65},{193,1... | collective-permute-start | bytes 1572872 | tf_op jit(solution)/shard_map/ppermute | solution.py:145
  31.8 8.8 %collective-permute-start.7 = (bf16[256,1024]{1,0:T(8,128)(2,1)S(1)}, bf16[256,1024]{1,0:T(8,128)(2,1)S(1)}, u32[]{:S(2)}, u32[]{:S(2)}) collective-permute-start(bf16[256,1024]{1,0:T(8,128)(2,1)S(1)} %pad_maximum_fusion.refs_0_), channel_id=1, source_target_pairs={{0,128},{128,0},{1,129},{129,1},{2,130},{130,2},{3,131},{131,3},{4... | collective-permute-start | bytes 1572872 | tf_op jit(solution)/shard_map/ppermute | solution.py:141
  40.5 1.9 %collective-permute-start.5 = (bf16[256,1024]{1,0:T(8,128)(2,1)S(1)}, bf16[256,1024]{1,0:T(8,128)(2,1)S(1)}, u32[]{:S(2)}, u32[]{:S(2)}) collective-permute-start(bf16[256,1024]{1,0:T(8,128)(2,1)S(1)} %pad_maximum_fusion.refs_0_), channel_id=1, source_target_pairs={{0,64},{64,0},{1,65},{65,1},{2,66},{66,2},{3,67},{67,3},{4,68},{68... | collective-permute-start | bytes 1572872 | tf_op jit(solution)/shard_map/ppermute | solution.py:141
  42.5 1.9 %collective-permute-start.4 = (bf16[256,1024]{1,0:T(8,128)(2,1)S(1)}, bf16[256,1024]{1,0:T(8,128)(2,1)S(1)}, u32[]{:S(2)}, u32[]{:S(2)}) collective-permute-start(bf16[256,1024]{1,0:T(8,128)(2,1)S(1)} %pad_maximum_fusion.refs_0_), channel_id=1, source_target_pairs={{0,32},{32,0},{1,33},{33,1},{2,34},{34,2},{3,35},{35,3},{4,36},{36... | collective-permute-start | bytes 1572872 | tf_op jit(solution)/shard_map/ppermute | solution.py:141
  44.4 4.7 %collective-permute-done.9.refs_6_ = bf16[256,1024]{1,0:T(8,128)(2,1)S(1)} collective-permute-done((bf16[256,1024]{1,0:T(8,128)(2,1)S(1)}, bf16[256,1024]{1,0:T(8,128)(2,1)S(1)}, u32[]{:S(2)}, u32[]{:S(2)}) %collective-permute-start.9) | collective-permute-done | bytes 524320 | tf_op jit(solution)/shard_map/ppermute | solution.py:145
  49.1 1.9 %collective-permute-start.10 = (bf16[256,1024]{1,0:T(8,128)(2,1)S(1)}, bf16[256,1024]{1,0:T(8,128)(2,1)S(1)}, u32[]{:S(2)}, u32[]{:S(2)}) collective-permute-start(bf16[256,1024]{1,0:T(8,128)(2,1)S(1)} %collective-permute-done.9.refs_6_), channel_id=1, source_target_pairs={{0,32},{32,0},{1,33},{33,1},{2,34},{34,2},{3,35},{35,3},{4,36},{36... | collective-permute-start | bytes 1572872 | tf_op jit(solution)/shard_map/ppermute | solution.py:141
  51.0 7.0 %collective-permute-done.7.refs_4_ = bf16[256,1024]{1,0:T(8,128)(2,1)S(1)} collective-permute-done((bf16[256,1024]{1,0:T(8,128)(2,1)S(1)}, bf16[256,1024]{1,0:T(8,128)(2,1)S(1)}, u32[]{:S(2)}, u32[]{:S(2)}) %collective-permute-start.7) | collective-permute-done | bytes 524320 | tf_op jit(solution)/shard_map/ppermute | solution.py:141
  57.9 1.9 %collective-permute-start.8 = (bf16[256,1024]{1,0:T(8,128)(2,1)S(1)}, bf16[256,1024]{1,0:T(8,128)(2,1)}, u32[]{:S(2)}, u32[]{:S(2)}) collective-permute-start(bf16[256,1024]{1,0:T(8,128)(2,1)S(1)} %collective-permute-done.7.refs_4_), channel_id=1, source_target_pairs={{0,32},{32,0},{1,33},{33,1},{2,34},{34,2},{3,35},{35,3},{4,36},{36... | collective-permute-start | bytes 1572872 | tf_op jit(solution)/shard_map/ppermute | solution.py:141
  59.9 2.4 %collective-permute-start.6 = (bf16[256,1024]{1,0:T(8,128)(2,1)S(1)}, bf16[256,1024]{1,0:T(8,128)(2,1)}, u32[]{:S(2)}, u32[]{:S(2)}) collective-permute-start(bf16[256,1024]{1,0:T(8,128)(2,1)S(1)} %collective-permute-done.5.refs_2_), channel_id=1, source_target_pairs={{0,32},{32,0},{1,33},{33,1},{2,34},{34,2},{3,35},{35,3},{4,36},{36... | collective-permute-start | bytes 1572872 | tf_op jit(solution)/shard_map/ppermute | solution.py:141
  62.3 0.1 stack.23.me
  62.4 1.5 collective-permute-done.6.refs_3_
  63.9 3.3 %all-gather.2.cloned.1.call-done.enc = bf16[8,256,256]{2,1,0:T(8,128)(2,1)} async-done(((bf16[1,256,256]{2,1,0:T(8,128)(2,1)}), bf16[8,256,256]{2,1,0:T(8,128)(2,1)}) %all-gather.2.cloned.1.call-update) | async-done | bytes 1048592 | tf_op jit(solution)/shard_map/all_gather | solution.py:199
  67.3 1.2 copy-done.8
  68.5 2.5 %shard_map.101 = bf16[4,256,256]{2,1,0:T(8,128)(2,1)S(1)} custom-call(s32[5]{0:T(128)S(1)} %stack.23.me, bf16[8,256,256]{2,1,0:T(8,128)(2,1)S(1)} %copy-done.8, bf16[256,1024]{1,0:T(8,128)(2,1)S(1)} %pad_maximum_fusion.refs_0_, bf16[256,1024]{1,0:T(8,128)(2,1)S(1)} %collective-permute-done.4.refs_1_, bf16[256,1024]{1,0:T(8,128)(2,1)S(1)} %collective-permute-done.5.refs_2_, ...), custom_call_target="tpu_custom_call" | custom-call | flops 1073741824 | bytes 5242880 | tf_op jit(solution)/shard_map/pallas_call | solution.py:232
  71.1 9.5 %all_to_all.10.arrived = bf16[4,256,256]{2,1,0:T(8,128)(2,1)S(1)} all-to-all(bf16[4,256,256]{2,1,0:T(8,128)(2,1)S(1)} %shard_map.101), channel_id=1, replica_groups=mesh['yh'=2,'yl'=2,'xh'=2,'c'=2,'s'=2,'zr'=8,'z0'=2] {'z0','s'}, dimensions={0} | all-to-all | bytes 1048576 | tf_op jit(solution)/shard_map/all_to_all | solution.py:235
  80.6 1.8 %shard_map.102 = (bf16[256,128]{1,0:T(8,128)(2,1)}, bf16[256,128]{1,0:T(8,128)(2,1)}, bf16[4,256,256]{2,1,0:T(8,128)(2,1)S(1)}) custom-call(s32[1,8]{1,0:T(1,128)S(1)} %copy-done.12, bf16[4,256,256]{2,1,0:T(8,128)(2,1)S(1)} %all_to_all.10.arrived, bf16[256,128]{1,0:T(8,128)(2,1)S(1)} %bitcast.17, bf16[256,128]{1,0:T(8,128)(2,1)S(1)} %bitcast.18), custom_call_target="tpu_custom_call" | custom-call | flops 25165824 | bytes 1048576 | tf_op jit(solution)/shard_map/pallas_call | solution.py:238
  82.4 9.5 %all_to_all.11.grads = bf16[4,256,256]{2,1,0:T(8,128)(2,1)S(1)} all-to-all(bf16[4,256,256]{2,1,0:T(8,128)(2,1)S(1)} %get-tuple-element.12), channel_id=1, replica_groups=mesh['yh'=2,'yl'=2,'xh'=2,'c'=2,'s'=2,'zr'=8,'z0'=2] {'z0','s'}, dimensions={0} | all-to-all | bytes 1048576 | tf_op jit(solution)/shard_map/all_to_all | solution.py:251
  91.9 3.2 %shard_map.104 = (bf16[16,256,256]{2,1,0:T(8,128)(2,1)S(1)}, bf16[16,256,256]{2,1,0:T(8,128)(2,1)}) custom-call(s32[5]{0:T(128)S(1)} %stack.23.me, bf16[8,256,256]{2,1,0:T(8,128)(2,1)S(1)} %copy-done.9, bf16[4,256,256]{2,1,0:T(8,128)(2,1)S(1)} %all_to_all.11.grads), custom_call_target="tpu_custom_call" | custom-call | flops 1073741824 | bytes 5242880 | tf_op jit(solution)/shard_map/pallas_call | solution.py:264
  95.1 1.9 %collective-permute-start.11 = (bf16[16,256,256]{2,1,0:T(8,128)(2,1)}, bf16[16,256,256]{2,1,0:T(8,128)(2,1)}, u32[]{:S(2)}, u32[]{:S(2)}) collective-permute-start(bf16[16,256,256]{2,1,0:T(8,128)(2,1)} %get-tuple-element.14), channel_id=1, source_target_pairs={{0,32},{32,0},{1,33},{33,1},{2,34},{34,2},{3,35},{35,3},{4,36},{36... | collective-permute-start | bytes 6291464 | tf_op jit(solution)/shard_map/ppermute | solution.py:141
  97.0 3.6 %shard_map.103 = bf16[8,256,256]{2,1,0:T(8,128)(2,1)} custom-call(s32[5]{0:T(128)S(1)} %stack.23.me, bf16[4,256,256]{2,1,0:T(8,128)(2,1)S(1)} %all_to_all.11.grads, bf16[256,1024]{1,0:T(8,128)(2,1)S(1)} %pad_maximum_fusion.refs_0_, bf16[256,1024]{1,0:T(8,128)(2,1)S(1)} %copy-done.5, bf16[256,1024]{1,0:T(8,128)(2,1)S(1)} %copy-done.3, ...), custom_call_target="tpu_custom_call" | custom-call | flops 1073741824 | bytes 5242880 | tf_op jit(solution)/shard_map/pallas_call | solution.py:253
  100.6 0.8 collective-permute-done.11
  101.5 2.2 %add_convert_fusion = bf16[16,256,256]{2,1,0:T(8,128)(2,1)S(1)} fusion(bf16[16,256,256]{2,1,0:T(8,128)(2,1)} %collective-permute-done.11, bf16[16,256,256]{2,1,0:T(8,128)(2,1)S(1)} %get-tuple-element.13), kind=kLoop, calls=%fused_computation | loop fusion | flops 4194304 | bytes 6291456 | tf_op jit(solution)/shard_map/convert_element_type | solution.py:267
  103.7 0.1 fusion.1
  103.8 3.4 %collective-permute-start.12 = (bf16[4,256,256]{2,1,0:T(8,128)(2,1)S(1)}, bf16[4,256,256]{2,1,0:T(8,128)(2,1)S(1)}, u32[]{:S(2)}, u32[]{:S(2)}) collective-permute-start(bf16[4,256,256]{2,1,0:T(8,128)(2,1)S(1)} %get-tuple-element.15), channel_id=1, source_target_pairs={{0,128},{128,0},{256,384},{384,256},{1,129},{129,1},{257,385},{385... | collective-permute-start | bytes 1572872 | tf_op jit(solution)/shard_map/ppermute | solution.py:185
  107.2 4.0 %collective-permute-start.14 = (bf16[4,256,256]{2,1,0:T(8,128)(2,1)S(1)}, bf16[4,256,256]{2,1,0:T(8,128)(2,1)S(1)}, u32[]{:S(2)}, u32[]{:S(2)}) collective-permute-start(bf16[4,256,256]{2,1,0:T(8,128)(2,1)S(1)} %get-tuple-element.16), channel_id=1, source_target_pairs={{0,384},{128,256},{256,128},{384,0},{1,385},{129,257},{257,129},{3... | collective-permute-start | bytes 1572872 | tf_op jit(solution)/shard_map/ppermute | solution.py:185
  111.2 2.4 %collective-permute-start.13 = (bf16[4,256,256]{2,1,0:T(8,128)(2,1)S(1)}, bf16[4,256,256]{2,1,0:T(8,128)(2,1)S(1)}, u32[]{:S(2)}, u32[]{:S(2)}) collective-permute-start(bf16[4,256,256]{2,1,0:T(8,128)(2,1)S(1)} %get-tuple-element.17), channel_id=1, source_target_pairs={{0,256},{128,384},{256,0},{384,128},{1,257},{129,385},{257,1},{385... | collective-permute-start | bytes 1572872 | tf_op jit(solution)/shard_map/ppermute | solution.py:185
  113.7 6.8 %collective-permute-done.12 = bf16[4,256,256]{2,1,0:T(8,128)(2,1)S(1)} collective-permute-done((bf16[4,256,256]{2,1,0:T(8,128)(2,1)S(1)}, bf16[4,256,256]{2,1,0:T(8,128)(2,1)S(1)}, u32[]{:S(2)}, u32[]{:S(2)}) %collective-permute-start.12) | collective-permute-done | bytes 524320 | tf_op jit(solution)/shard_map/ppermute | solution.py:185
  120.5 14.7 %collective-permute-done.14 = bf16[4,256,256]{2,1,0:T(8,128)(2,1)S(1)} collective-permute-done((bf16[4,256,256]{2,1,0:T(8,128)(2,1)S(1)}, bf16[4,256,256]{2,1,0:T(8,128)(2,1)S(1)}, u32[]{:S(2)}, u32[]{:S(2)}) %collective-permute-start.14) | collective-permute-done | bytes 524320 | tf_op jit(solution)/shard_map/ppermute | solution.py:185
  135.2 0.3 add_convert_fusion.1
  135.5 4.6 %collective-permute-start.17 = (bf16[256,256]{1,0:T(8,128)(2,1)S(1)}, bf16[256,256]{1,0:T(8,128)(2,1)S(1)}, u32[]{:S(2)}, u32[]{:S(2)}) collective-permute-start(bf16[256,256]{1,0:T(8,128)(2,1)S(1)} %get-tuple-element.20), channel_id=1, source_target_pairs={{65,0},{64,1},{449,16},{448,17},{1,64},{0,65},{385,80},{384,81},{1... | collective-permute-start | bytes 393224 | tf_op jit(solution)/shard_map/ppermute | solution.py:195
  140.1 5.0 %collective-permute-start.18 = (bf16[256,256]{1,0:T(8,128)(2,1)S(1)}, bf16[256,256]{1,0:T(8,128)(2,1)S(1)}, u32[]{:S(2)}, u32[]{:S(2)}) collective-permute-start(bf16[256,256]{1,0:T(8,128)(2,1)S(1)} %get-tuple-element.21), channel_id=1, source_target_pairs={{1,0},{0,1},{385,16},{384,17},{65,64},{64,65},{449,80},{448,81},{1... | collective-permute-start | bytes 393224 | tf_op jit(solution)/shard_map/ppermute | solution.py:195
  145.1 3.5 %collective-permute-start.16 = (bf16[256,256]{1,0:T(8,128)(2,1)S(1)}, bf16[256,256]{1,0:T(8,128)(2,1)S(1)}, u32[]{:S(2)}, u32[]{:S(2)}) collective-permute-start(bf16[256,256]{1,0:T(8,128)(2,1)S(1)} %get-tuple-element.22), channel_id=1, source_target_pairs={{0,0},{1,1},{384,16},{385,17},{64,64},{65,65},{448,80},{449,81},{1... | collective-permute-start | bytes 393224 | tf_op jit(solution)/shard_map/ppermute | solution.py:195
  148.6 4.9 %collective-permute-start.15 = (bf16[256,256]{1,0:T(8,128)(2,1)S(1)}, bf16[256,256]{1,0:T(8,128)(2,1)S(1)}, u32[]{:S(2)}, u32[]{:S(2)}) collective-permute-start(bf16[256,256]{1,0:T(8,128)(2,1)S(1)} %get-tuple-element.23), channel_id=1, source_target_pairs={{64,0},{65,1},{448,16},{449,17},{0,64},{1,65},{384,80},{385,81},{1... | collective-permute-start | bytes 393224 | tf_op jit(solution)/shard_map/ppermute | solution.py:195
  153.6 0.4 collective-permute-done.17
  153.9 3.9 %collective-permute-done.18 = bf16[256,256]{1,0:T(8,128)(2,1)S(1)} collective-permute-done((bf16[256,256]{1,0:T(8,128)(2,1)S(1)}, bf16[256,256]{1,0:T(8,128)(2,1)S(1)}, u32[]{:S(2)}, u32[]{:S(2)}) %collective-permute-start.18) | collective-permute-done | bytes 131104 | tf_op jit(solution)/shard_map/ppermute | solution.py:195
  157.9 0.6 collective-permute-done.16
  158.4 0.9 collective-permute-done.15
  159.3 0.1 broadcast_select_fusion
  159.4 0.7 pad_maximum_fusion.1
  (40 shorter events, 0.4 us)
Async XLA Ops:
  7.2 60.1 %all-gather.2.cloned.1.call-start = ((), (), s32[]{:S(2)}) async-start(), calls=%async_computation.3 | async-start | bytes 1179648 | tf_op jit(solution)/shard_map/all_gather | solution.py:199
  7.9 152.2 %reduce-scatter.2.cloned.1.call-start = ((), (), s32[]{:S(2)}) async-start(), calls=%async_computation.4 | async-start | bytes 1179648 | tf_op jit(solution)/shard_map/reduce_scatter | solution.py:261
  9.0 13.6 %collective-permute-start.3 = (bf16[256,256]{1,0:T(8,128)(2,1)S(1)}, bf16[256,256]{1,0:T(8,128)(2,1)S(1)}, u32[]{:S(2)}, u32[]{:S(2)}) collective-permute-start(bf16[256,256]{1,0:T(8,128)(2,1)S(1)} %get-tuple-element.27), channel_id=1, source_target_pairs={{0,385},{16,1},{1,384},{17,0},{128,257},{144,129},{129,256},{145,1... | collective-permute-start | bytes 393224 | tf_op jit(solution)/shard_map/ppermute | solution.py:181
  13.1 9.9 %collective-permute-start.2 = (bf16[256,256]{1,0:T(8,128)(2,1)S(1)}, bf16[256,256]{1,0:T(8,128)(2,1)S(1)}, u32[]{:S(2)}, u32[]{:S(2)}) collective-permute-start(bf16[256,256]{1,0:T(8,128)(2,1)S(1)} %get-tuple-element.27), channel_id=1, source_target_pairs={{0,1},{16,385},{1,0},{17,384},{128,129},{144,257},{129,128},{145,2... | collective-permute-start | bytes 393224 | tf_op jit(solution)/shard_map/ppermute | solution.py:181
  18.2 10.1 %collective-permute-start.1 = (bf16[256,256]{1,0:T(8,128)(2,1)S(1)}, bf16[256,256]{1,0:T(8,128)(2,1)S(1)}, u32[]{:S(2)}, u32[]{:S(2)}) collective-permute-start(bf16[256,256]{1,0:T(8,128)(2,1)S(1)} %get-tuple-element.26), channel_id=1, source_target_pairs={{16,384},{17,385},{144,256},{145,257},{256,144},{257,145},{384,16}... | collective-permute-start | bytes 393224 | tf_op jit(solution)/shard_map/ppermute | solution.py:181
  20.6 9.2 %collective-permute-start = (bf16[256,256]{1,0:T(8,128)(2,1)S(1)}, bf16[256,256]{1,0:T(8,128)(2,1)S(1)}, u32[]{:S(2)}, u32[]{:S(2)}) collective-permute-start(bf16[256,256]{1,0:T(8,128)(2,1)S(1)} %get-tuple-element.26), channel_id=1, source_target_pairs={{0,384},{16,0},{1,385},{17,1},{128,256},{144,128},{129,257},{145,1... | collective-permute-start | bytes 393224 | tf_op jit(solution)/shard_map/ppermute | solution.py:181
  29.9 19.2 %collective-permute-start.9 = (bf16[256,1024]{1,0:T(8,128)(2,1)S(1)}, bf16[256,1024]{1,0:T(8,128)(2,1)S(1)}, u32[]{:S(2)}, u32[]{:S(2)}) collective-permute-start(bf16[256,1024]{1,0:T(8,128)(2,1)S(1)} %pad_maximum_fusion.refs_0_), channel_id=1, source_target_pairs={{0,192},{64,128},{128,64},{192,0},{1,193},{65,129},{129,65},{193,1... | collective-permute-start | bytes 1572872 | tf_op jit(solution)/shard_map/ppermute | solution.py:145
  31.8 26.2 %collective-permute-start.7 = (bf16[256,1024]{1,0:T(8,128)(2,1)S(1)}, bf16[256,1024]{1,0:T(8,128)(2,1)S(1)}, u32[]{:S(2)}, u32[]{:S(2)}) collective-permute-start(bf16[256,1024]{1,0:T(8,128)(2,1)S(1)} %pad_maximum_fusion.refs_0_), channel_id=1, source_target_pairs={{0,128},{128,0},{1,129},{129,1},{2,130},{130,2},{3,131},{131,3},{4... | collective-permute-start | bytes 1572872 | tf_op jit(solution)/shard_map/ppermute | solution.py:141
  40.5 19.3 %collective-permute-start.5 = (bf16[256,1024]{1,0:T(8,128)(2,1)S(1)}, bf16[256,1024]{1,0:T(8,128)(2,1)S(1)}, u32[]{:S(2)}, u32[]{:S(2)}) collective-permute-start(bf16[256,1024]{1,0:T(8,128)(2,1)S(1)} %pad_maximum_fusion.refs_0_), channel_id=1, source_target_pairs={{0,64},{64,0},{1,65},{65,1},{2,66},{66,2},{3,67},{67,3},{4,68},{68... | collective-permute-start | bytes 1572872 | tf_op jit(solution)/shard_map/ppermute | solution.py:141
  42.5 20.0 %collective-permute-start.4 = (bf16[256,1024]{1,0:T(8,128)(2,1)S(1)}, bf16[256,1024]{1,0:T(8,128)(2,1)S(1)}, u32[]{:S(2)}, u32[]{:S(2)}) collective-permute-start(bf16[256,1024]{1,0:T(8,128)(2,1)S(1)} %pad_maximum_fusion.refs_0_), channel_id=1, source_target_pairs={{0,32},{32,0},{1,33},{33,1},{2,34},{34,2},{3,35},{35,3},{4,36},{36... | collective-permute-start | bytes 1572872 | tf_op jit(solution)/shard_map/ppermute | solution.py:141
  49.1 13.4 %collective-permute-start.10 = (bf16[256,1024]{1,0:T(8,128)(2,1)S(1)}, bf16[256,1024]{1,0:T(8,128)(2,1)S(1)}, u32[]{:S(2)}, u32[]{:S(2)}) collective-permute-start(bf16[256,1024]{1,0:T(8,128)(2,1)S(1)} %collective-permute-done.9.refs_6_), channel_id=1, source_target_pairs={{0,32},{32,0},{1,33},{33,1},{2,34},{34,2},{3,35},{35,3},{4,36},{36... | collective-permute-start | bytes 1572872 | tf_op jit(solution)/shard_map/ppermute | solution.py:141
  57.9 13.1 %copy-start = (bf16[256,1024]{1,0:T(8,128)(2,1)}, bf16[256,1024]{1,0:T(8,128)(2,1)S(1)}, u32[]{:S(2)}) copy-start(bf16[256,1024]{1,0:T(8,128)(2,1)S(1)} %collective-permute-done.7.refs_4_) | copy-start | bytes 1572868
  57.9 4.5 %collective-permute-start.8 = (bf16[256,1024]{1,0:T(8,128)(2,1)S(1)}, bf16[256,1024]{1,0:T(8,128)(2,1)}, u32[]{:S(2)}, u32[]{:S(2)}) collective-permute-start(bf16[256,1024]{1,0:T(8,128)(2,1)S(1)} %collective-permute-done.7.refs_4_), channel_id=1, source_target_pairs={{0,32},{32,0},{1,33},{33,1},{2,34},{34,2},{3,35},{35,3},{4,36},{36... | collective-permute-start | bytes 1572872 | tf_op jit(solution)/shard_map/ppermute | solution.py:141
  59.9 11.2 %copy-start.2 = (bf16[256,1024]{1,0:T(8,128)(2,1)}, bf16[256,1024]{1,0:T(8,128)(2,1)S(1)}, u32[]{:S(2)}) copy-start(bf16[256,1024]{1,0:T(8,128)(2,1)S(1)} %collective-permute-done.5.refs_2_) | copy-start | bytes 1572868
  59.9 4.1 %collective-permute-start.6 = (bf16[256,1024]{1,0:T(8,128)(2,1)S(1)}, bf16[256,1024]{1,0:T(8,128)(2,1)}, u32[]{:S(2)}, u32[]{:S(2)}) collective-permute-start(bf16[256,1024]{1,0:T(8,128)(2,1)S(1)} %collective-permute-done.5.refs_2_), channel_id=1, source_target_pairs={{0,32},{32,0},{1,33},{33,1},{2,34},{34,2},{3,35},{35,3},{4,36},{36... | collective-permute-start | bytes 1572872 | tf_op jit(solution)/shard_map/ppermute | solution.py:141
  62.3 18.3 %copy-start.12 = (s32[1,8]{1,0:T(1,128)S(1)}, s32[1,8]{1,0:T(1,128)}, u32[]{:S(2)}) copy-start(s32[1,8]{1,0:T(1,128)} %ids.1) | copy-start | bytes 100
  62.4 8.6 %copy-start.4 = (bf16[256,1024]{1,0:T(8,128)(2,1)}, bf16[256,1024]{1,0:T(8,128)(2,1)S(1)}, u32[]{:S(2)}) copy-start(bf16[256,1024]{1,0:T(8,128)(2,1)S(1)} %collective-permute-done.4.refs_1_) | copy-start | bytes 1572868
  62.4 8.6 %copy-start.6 = (bf16[256,1024]{1,0:T(8,128)(2,1)}, bf16[256,1024]{1,0:T(8,128)(2,1)S(1)}, u32[]{:S(2)}) copy-start(bf16[256,1024]{1,0:T(8,128)(2,1)S(1)} %collective-permute-done.10.refs_7_) | copy-start | bytes 1572868
  67.3 1.2 copy-start.8
  68.5 12.1 %copy-start.10 = (bf16[1,256,128]{2,1,0:T(8,128)(2,1)S(1)}, bf16[1,256,128]{2,1,0:T(8,128)(2,1)}, u32[]{:S(2)}) copy-start(bf16[1,256,128]{2,1,0:T(8,128)(2,1)} %param.6) | copy-start | bytes 196612
  68.5 12.1 %copy-start.11 = (bf16[1,256,128]{2,1,0:T(8,128)(2,1)S(1)}, bf16[1,256,128]{2,1,0:T(8,128)(2,1)}, u32[]{:S(2)}) copy-start(bf16[1,256,128]{2,1,0:T(8,128)(2,1)} %param.11) | copy-start | bytes 196612
  71.1 20.8 %copy-start.9 = (bf16[8,256,256]{2,1,0:T(8,128)(2,1)S(1)}, bf16[8,256,256]{2,1,0:T(8,128)(2,1)}, u32[]{:S(2)}) copy-start(bf16[8,256,256]{2,1,0:T(8,128)(2,1)} %all-gather.2.cloned.1.call-done.enc) | copy-start | bytes 3145732
  91.9 5.1 %copy-start.1 = (bf16[256,1024]{1,0:T(8,128)(2,1)S(1)}, bf16[256,1024]{1,0:T(8,128)(2,1)}, u32[]{:S(2)}) copy-start(bf16[256,1024]{1,0:T(8,128)(2,1)} %copy-done) | copy-start | bytes 1572868
  91.9 5.1 %copy-start.3 = (bf16[256,1024]{1,0:T(8,128)(2,1)S(1)}, bf16[256,1024]{1,0:T(8,128)(2,1)}, u32[]{:S(2)}) copy-start(bf16[256,1024]{1,0:T(8,128)(2,1)} %copy-done.2) | copy-start | bytes 1572868
  91.9 5.1 %copy-start.5 = (bf16[256,1024]{1,0:T(8,128)(2,1)S(1)}, bf16[256,1024]{1,0:T(8,128)(2,1)}, u32[]{:S(2)}) copy-start(bf16[256,1024]{1,0:T(8,128)(2,1)} %copy-done.4) | copy-start | bytes 1572868
  91.9 5.2 %copy-start.7 = (bf16[256,1024]{1,0:T(8,128)(2,1)S(1)}, bf16[256,1024]{1,0:T(8,128)(2,1)}, u32[]{:S(2)}) copy-start(bf16[256,1024]{1,0:T(8,128)(2,1)} %copy-done.6) | copy-start | bytes 1572868
  95.1 6.4 %collective-permute-start.11 = (bf16[16,256,256]{2,1,0:T(8,128)(2,1)}, bf16[16,256,256]{2,1,0:T(8,128)(2,1)}, u32[]{:S(2)}, u32[]{:S(2)}) collective-permute-start(bf16[16,256,256]{2,1,0:T(8,128)(2,1)} %get-tuple-element.14), channel_id=1, source_target_pairs={{0,32},{32,0},{1,33},{33,1},{2,34},{34,2},{3,35},{35,3},{4,36},{36... | collective-permute-start | bytes 6291464 | tf_op jit(solution)/shard_map/ppermute | solution.py:141
  103.8 16.7 %collective-permute-start.12 = (bf16[4,256,256]{2,1,0:T(8,128)(2,1)S(1)}, bf16[4,256,256]{2,1,0:T(8,128)(2,1)S(1)}, u32[]{:S(2)}, u32[]{:S(2)}) collective-permute-start(bf16[4,256,256]{2,1,0:T(8,128)(2,1)S(1)} %get-tuple-element.15), channel_id=1, source_target_pairs={{0,128},{128,0},{256,384},{384,256},{1,129},{129,1},{257,385},{385... | collective-permute-start | bytes 1572872 | tf_op jit(solution)/shard_map/ppermute | solution.py:185
  107.2 28.0 %collective-permute-start.14 = (bf16[4,256,256]{2,1,0:T(8,128)(2,1)S(1)}, bf16[4,256,256]{2,1,0:T(8,128)(2,1)S(1)}, u32[]{:S(2)}, u32[]{:S(2)}) collective-permute-start(bf16[4,256,256]{2,1,0:T(8,128)(2,1)S(1)} %get-tuple-element.16), channel_id=1, source_target_pairs={{0,384},{128,256},{256,128},{384,0},{1,385},{129,257},{257,129},{3... | collective-permute-start | bytes 1572872 | tf_op jit(solution)/shard_map/ppermute | solution.py:185
  111.2 24.0 %collective-permute-start.13 = (bf16[4,256,256]{2,1,0:T(8,128)(2,1)S(1)}, bf16[4,256,256]{2,1,0:T(8,128)(2,1)S(1)}, u32[]{:S(2)}, u32[]{:S(2)}) collective-permute-start(bf16[4,256,256]{2,1,0:T(8,128)(2,1)S(1)} %get-tuple-element.17), channel_id=1, source_target_pairs={{0,256},{128,384},{256,0},{384,128},{1,257},{129,385},{257,1},{385... | collective-permute-start | bytes 1572872 | tf_op jit(solution)/shard_map/ppermute | solution.py:185
  135.5 18.4 %collective-permute-start.17 = (bf16[256,256]{1,0:T(8,128)(2,1)S(1)}, bf16[256,256]{1,0:T(8,128)(2,1)S(1)}, u32[]{:S(2)}, u32[]{:S(2)}) collective-permute-start(bf16[256,256]{1,0:T(8,128)(2,1)S(1)} %get-tuple-element.20), channel_id=1, source_target_pairs={{65,0},{64,1},{449,16},{448,17},{1,64},{0,65},{385,80},{384,81},{1... | collective-permute-start | bytes 393224 | tf_op jit(solution)/shard_map/ppermute | solution.py:195
  140.1 17.8 %collective-permute-start.18 = (bf16[256,256]{1,0:T(8,128)(2,1)S(1)}, bf16[256,256]{1,0:T(8,128)(2,1)S(1)}, u32[]{:S(2)}, u32[]{:S(2)}) collective-permute-start(bf16[256,256]{1,0:T(8,128)(2,1)S(1)} %get-tuple-element.21), channel_id=1, source_target_pairs={{1,0},{0,1},{385,16},{384,17},{65,64},{64,65},{449,80},{448,81},{1... | collective-permute-start | bytes 393224 | tf_op jit(solution)/shard_map/ppermute | solution.py:195
  145.1 13.3 %collective-permute-start.16 = (bf16[256,256]{1,0:T(8,128)(2,1)S(1)}, bf16[256,256]{1,0:T(8,128)(2,1)S(1)}, u32[]{:S(2)}, u32[]{:S(2)}) collective-permute-start(bf16[256,256]{1,0:T(8,128)(2,1)S(1)} %get-tuple-element.22), channel_id=1, source_target_pairs={{0,0},{1,1},{384,16},{385,17},{64,64},{65,65},{448,80},{449,81},{1... | collective-permute-start | bytes 393224 | tf_op jit(solution)/shard_map/ppermute | solution.py:195
  148.6 10.7 %collective-permute-start.15 = (bf16[256,256]{1,0:T(8,128)(2,1)S(1)}, bf16[256,256]{1,0:T(8,128)(2,1)S(1)}, u32[]{:S(2)}, u32[]{:S(2)}) collective-permute-start(bf16[256,256]{1,0:T(8,128)(2,1)S(1)} %get-tuple-element.23), channel_id=1, source_target_pairs={{64,0},{65,1},{448,16},{449,17},{0,64},{1,65},{384,80},{385,81},{1... | collective-permute-start | bytes 393224 | tf_op jit(solution)/shard_map/ppermute | solution.py:195
Sparse Core Ops, SparseCore 0:
  10.1 57.1 all-gather.1
  100.8 56.4 reduce-scatter.1

commit v7 on v6

--- a/solution.py
+++ b/solution.py
@@ -266,7 +266,7 @@
     )(me, enc, grads)
     near = (near.astype(F32) + swap(far, "c").astype(F32)).astype(BF16)
     near = near.reshape(4, 4, BLOCK, WIDE)
-    near = add(near[0], hop(near[1], 1), hop(near[2], 2), hop(near[3], 3))
+    near = add(near[0], hop(near[2], 2), hop(near[1], 1), hop(near[3], 3))
     kept = add(turn_back(near[2], 1, 0), turn_back(near[0], 0, 0))
     given = add(turn_back(near[3], 1, 1), turn_back(near[1], 0, 1))
     upper, lower = jnp.where(even, kept, given), jnp.where(even, given, kept)

time: 168 us -> 167 us (level)
    ppermute x3, waiting for transfers between devices: 21.6 us -> 18.7 us  [hop(): return lax.ppermute(x, ('yh', 'yl'), [(i, i ^ by) for i in range(4)])]
    ppermute x4, waiting for transfers between devices: 5.77 us -> 7.47 us  [turn_back(): return lax.ppermute(x, ('yh', 'yl', 'xh', 's', 'z0'), pairs)]
  transfers between devices with their start and end apart: 21 -> 21, of which waited for: 14 -> 12; matrix products, arithmetic and copies ran while one was open for 3% -> 3% of each run, Pallas kernels for 2% -> 2%
where the time goes in v7:
time: 167 us; the launch traced here: 166 us
  starting transfers between devices  64.1 us (38%)
  waiting for transfers between devices  51.4 us (31%)
  blocking collectives  19 us (11%)
  between operations  14.4 us (9%)
  Pallas kernels  11 us (7%)
  other arithmetic  3.44 us (2%)
  local copies, waits for them, and re-layouts  2.46 us (1%)
    ppermute x7, starting transfers between devices, swap(): return lax.ppermute(x, axis, [(0, 1), (1, 0)])  20.7 us
    ppermute x3, waiting for transfers between devices, hop(): return lax.ppermute(x, ('yh', 'yl'), [(i, i ^ by) for i in range(4)])  18.7 us
    ppermute x4, starting transfers between devices, turn_back(): return lax.ppermute(x, ('yh', 'yl', 'xh', 's', 'z0'), pairs)  18 us
    ppermute x4, starting transfers between devices, send(): return lax.ppermute(x, Y_AXES, pairs)  13.5 us
    ppermute x3, starting transfers between devices, hop(): return lax.ppermute(x, ('yh', 'yl'), [(i, i ^ by) for i in range(4)])  9.86 us
    all_to_all x1, blocking collectives, per_device(): arrived = lax.all_to_all(terms, ('z0', 's'), 0, 0, tiled=True)  9.52 us
    all_to_all x1, blocking collectives, per_device(): grads = lax.all_to_all(copies, ('z0', 's'), 0, 0, tiled=True)  9.52 us
    ppermute x7, waiting for transfers between devices, swap(): return lax.ppermute(x, axis, [(0, 1), (1, 0)])  9.3 us
  transfers between devices with their start and end apart: 21, of which 12 were waited for; matrix products, arithmetic and copies ran while one was open for 3% of the time, Pallas kernels for 2%

profile of v7, /device:TPU:6, one launch (start us, length us, event | category | flops | bytes accessed | tf_op | source)
XLA Modules:
  0.0 165.9 jit_solution(15629902877891261133)
XLA Ops:
  7.2 0.7 all-gather.2.cloned.1.call-update
  8.0 1.0 fusion.2
  8.9 0.1 broadcast_select_fusion.3
  9.0 4.1 %collective-permute-start.3 = (bf16[256,256]{1,0:T(8,128)(2,1)S(1)}, bf16[256,256]{1,0:T(8,128)(2,1)S(1)}, u32[]{:S(2)}, u32[]{:S(2)}) collective-permute-start(bf16[256,256]{1,0:T(8,128)(2,1)S(1)} %get-tuple-element.27), channel_id=1, source_target_pairs={{0,385},{16,1},{1,384},{17,0},{128,257},{144,129},{129,256},{145,1... | collective-permute-start | bytes 393224 | tf_op jit(solution)/shard_map/ppermute | solution.py:181
  13.1 5.1 %collective-permute-start.2 = (bf16[256,256]{1,0:T(8,128)(2,1)S(1)}, bf16[256,256]{1,0:T(8,128)(2,1)S(1)}, u32[]{:S(2)}, u32[]{:S(2)}) collective-permute-start(bf16[256,256]{1,0:T(8,128)(2,1)S(1)} %get-tuple-element.27), channel_id=1, source_target_pairs={{0,1},{16,385},{1,0},{17,384},{128,129},{144,257},{129,128},{145,2... | collective-permute-start | bytes 393224 | tf_op jit(solution)/shard_map/ppermute | solution.py:181
  18.2 2.4 %collective-permute-start.1 = (bf16[256,256]{1,0:T(8,128)(2,1)S(1)}, bf16[256,256]{1,0:T(8,128)(2,1)S(1)}, u32[]{:S(2)}, u32[]{:S(2)}) collective-permute-start(bf16[256,256]{1,0:T(8,128)(2,1)S(1)} %get-tuple-element.26), channel_id=1, source_target_pairs={{16,384},{17,385},{144,256},{145,257},{256,144},{257,145},{384,16}... | collective-permute-start | bytes 393224 | tf_op jit(solution)/shard_map/ppermute | solution.py:181
  20.6 1.9 %collective-permute-start = (bf16[256,256]{1,0:T(8,128)(2,1)S(1)}, bf16[256,256]{1,0:T(8,128)(2,1)S(1)}, u32[]{:S(2)}, u32[]{:S(2)}) collective-permute-start(bf16[256,256]{1,0:T(8,128)(2,1)S(1)} %get-tuple-element.26), channel_id=1, source_target_pairs={{0,384},{16,0},{1,385},{17,1},{128,256},{144,128},{129,257},{145,1... | collective-permute-start | bytes 393224 | tf_op jit(solution)/shard_map/ppermute | solution.py:181
  22.5 0.4 collective-permute-done.2
  23.0 5.4 %collective-permute-done.1 = bf16[256,256]{1,0:T(8,128)(2,1)S(1)} collective-permute-done((bf16[256,256]{1,0:T(8,128)(2,1)S(1)}, bf16[256,256]{1,0:T(8,128)(2,1)S(1)}, u32[]{:S(2)}, u32[]{:S(2)}) %collective-permute-start.1) | collective-permute-done | bytes 131104 | tf_op jit(solution)/shard_map/ppermute | solution.py:181
  28.3 1.4 collective-permute-done
  29.8 0.1 pad_maximum_fusion.refs_0_
  29.9 1.9 %collective-permute-start.9 = (bf16[256,1024]{1,0:T(8,128)(2,1)S(1)}, bf16[256,1024]{1,0:T(8,128)(2,1)S(1)}, u32[]{:S(2)}, u32[]{:S(2)}) collective-permute-start(bf16[256,1024]{1,0:T(8,128)(2,1)S(1)} %pad_maximum_fusion.refs_0_), channel_id=1, source_target_pairs={{0,192},{64,128},{128,64},{192,0},{1,193},{65,129},{129,65},{193,1... | collective-permute-start | bytes 1572872 | tf_op jit(solution)/shard_map/ppermute | solution.py:145
  31.8 8.8 %collective-permute-start.7 = (bf16[256,1024]{1,0:T(8,128)(2,1)S(1)}, bf16[256,1024]{1,0:T(8,128)(2,1)S(1)}, u32[]{:S(2)}, u32[]{:S(2)}) collective-permute-start(bf16[256,1024]{1,0:T(8,128)(2,1)S(1)} %pad_maximum_fusion.refs_0_), channel_id=1, source_target_pairs={{0,128},{128,0},{1,129},{129,1},{2,130},{130,2},{3,131},{131,3},{4... | collective-permute-start | bytes 1572872 | tf_op jit(solution)/shard_map/ppermute | solution.py:141
  40.5 1.9 %collective-permute-start.5 = (bf16[256,1024]{1,0:T(8,128)(2,1)S(1)}, bf16[256,1024]{1,0:T(8,128)(2,1)S(1)}, u32[]{:S(2)}, u32[]{:S(2)}) collective-permute-start(bf16[256,1024]{1,0:T(8,128)(2,1)S(1)} %pad_maximum_fusion.refs_0_), channel_id=1, source_target_pairs={{0,64},{64,0},{1,65},{65,1},{2,66},{66,2},{3,67},{67,3},{4,68},{68... | collective-permute-start | bytes 1572872 | tf_op jit(solution)/shard_map/ppermute | solution.py:141
  42.5 1.9 %collective-permute-start.4 = (bf16[256,1024]{1,0:T(8,128)(2,1)S(1)}, bf16[256,1024]{1,0:T(8,128)(2,1)S(1)}, u32[]{:S(2)}, u32[]{:S(2)}) collective-permute-start(bf16[256,1024]{1,0:T(8,128)(2,1)S(1)} %pad_maximum_fusion.refs_0_), channel_id=1, source_target_pairs={{0,32},{32,0},{1,33},{33,1},{2,34},{34,2},{3,35},{35,3},{4,36},{36... | collective-permute-start | bytes 1572872 | tf_op jit(solution)/shard_map/ppermute | solution.py:141
  44.4 4.7 %collective-permute-done.9.refs_6_ = bf16[256,1024]{1,0:T(8,128)(2,1)S(1)} collective-permute-done((bf16[256,1024]{1,0:T(8,128)(2,1)S(1)}, bf16[256,1024]{1,0:T(8,128)(2,1)S(1)}, u32[]{:S(2)}, u32[]{:S(2)}) %collective-permute-start.9) | collective-permute-done | bytes 524320 | tf_op jit(solution)/shard_map/ppermute | solution.py:145
  49.1 1.9 %collective-permute-start.10 = (bf16[256,1024]{1,0:T(8,128)(2,1)S(1)}, bf16[256,1024]{1,0:T(8,128)(2,1)S(1)}, u32[]{:S(2)}, u32[]{:S(2)}) collective-permute-start(bf16[256,1024]{1,0:T(8,128)(2,1)S(1)} %collective-permute-done.9.refs_6_), channel_id=1, source_target_pairs={{0,32},{32,0},{1,33},{33,1},{2,34},{34,2},{3,35},{35,3},{4,36},{36... | collective-permute-start | bytes 1572872 | tf_op jit(solution)/shard_map/ppermute | solution.py:141
  51.0 7.0 %collective-permute-done.7.refs_4_ = bf16[256,1024]{1,0:T(8,128)(2,1)S(1)} collective-permute-done((bf16[256,1024]{1,0:T(8,128)(2,1)S(1)}, bf16[256,1024]{1,0:T(8,128)(2,1)S(1)}, u32[]{:S(2)}, u32[]{:S(2)}) %collective-permute-start.7) | collective-permute-done | bytes 524320 | tf_op jit(solution)/shard_map/ppermute | solution.py:141
  57.9 1.9 %collective-permute-start.8 = (bf16[256,1024]{1,0:T(8,128)(2,1)S(1)}, bf16[256,1024]{1,0:T(8,128)(2,1)}, u32[]{:S(2)}, u32[]{:S(2)}) collective-permute-start(bf16[256,1024]{1,0:T(8,128)(2,1)S(1)} %collective-permute-done.7.refs_4_), channel_id=1, source_target_pairs={{0,32},{32,0},{1,33},{33,1},{2,34},{34,2},{3,35},{35,3},{4,36},{36... | collective-permute-start | bytes 1572872 | tf_op jit(solution)/shard_map/ppermute | solution.py:141
  59.9 2.4 %collective-permute-start.6 = (bf16[256,1024]{1,0:T(8,128)(2,1)S(1)}, bf16[256,1024]{1,0:T(8,128)(2,1)}, u32[]{:S(2)}, u32[]{:S(2)}) collective-permute-start(bf16[256,1024]{1,0:T(8,128)(2,1)S(1)} %collective-permute-done.5.refs_2_), channel_id=1, source_target_pairs={{0,32},{32,0},{1,33},{33,1},{2,34},{34,2},{3,35},{35,3},{4,36},{36... | collective-permute-start | bytes 1572872 | tf_op jit(solution)/shard_map/ppermute | solution.py:141
  62.3 0.1 stack.23.me
  62.4 1.5 collective-permute-done.6.refs_3_
  63.9 3.3 %all-gather.2.cloned.1.call-done.enc = bf16[8,256,256]{2,1,0:T(8,128)(2,1)} async-done(((bf16[1,256,256]{2,1,0:T(8,128)(2,1)}), bf16[8,256,256]{2,1,0:T(8,128)(2,1)}) %all-gather.2.cloned.1.call-update) | async-done | bytes 1048592 | tf_op jit(solution)/shard_map/all_gather | solution.py:199
  67.3 1.2 copy-done.8
  68.5 2.5 %shard_map.101 = bf16[4,256,256]{2,1,0:T(8,128)(2,1)S(1)} custom-call(s32[5]{0:T(128)S(1)} %stack.23.me, bf16[8,256,256]{2,1,0:T(8,128)(2,1)S(1)} %copy-done.8, bf16[256,1024]{1,0:T(8,128)(2,1)S(1)} %pad_maximum_fusion.refs_0_, bf16[256,1024]{1,0:T(8,128)(2,1)S(1)} %collective-permute-done.4.refs_1_, bf16[256,1024]{1,0:T(8,128)(2,1)S(1)} %collective-permute-done.5.refs_2_, ...), custom_call_target="tpu_custom_call" | custom-call | flops 1073741824 | bytes 5242880 | tf_op jit(solution)/shard_map/pallas_call | solution.py:232
  71.1 9.5 %all_to_all.10.arrived = bf16[4,256,256]{2,1,0:T(8,128)(2,1)S(1)} all-to-all(bf16[4,256,256]{2,1,0:T(8,128)(2,1)S(1)} %shard_map.101), channel_id=1, replica_groups=mesh['yh'=2,'yl'=2,'xh'=2,'c'=2,'s'=2,'zr'=8,'z0'=2] {'z0','s'}, dimensions={0} | all-to-all | bytes 1048576 | tf_op jit(solution)/shard_map/all_to_all | solution.py:235
  80.6 1.8 %shard_map.102 = (bf16[256,128]{1,0:T(8,128)(2,1)}, bf16[256,128]{1,0:T(8,128)(2,1)}, bf16[4,256,256]{2,1,0:T(8,128)(2,1)S(1)}) custom-call(s32[1,8]{1,0:T(1,128)S(1)} %copy-done.12, bf16[4,256,256]{2,1,0:T(8,128)(2,1)S(1)} %all_to_all.10.arrived, bf16[256,128]{1,0:T(8,128)(2,1)S(1)} %bitcast.17, bf16[256,128]{1,0:T(8,128)(2,1)S(1)} %bitcast.18), custom_call_target="tpu_custom_call" | custom-call | flops 25165824 | bytes 1048576 | tf_op jit(solution)/shard_map/pallas_call | solution.py:238
  82.4 9.5 %all_to_all.11.grads = bf16[4,256,256]{2,1,0:T(8,128)(2,1)S(1)} all-to-all(bf16[4,256,256]{2,1,0:T(8,128)(2,1)S(1)} %get-tuple-element.12), channel_id=1, replica_groups=mesh['yh'=2,'yl'=2,'xh'=2,'c'=2,'s'=2,'zr'=8,'z0'=2] {'z0','s'}, dimensions={0} | all-to-all | bytes 1048576 | tf_op jit(solution)/shard_map/all_to_all | solution.py:251
  91.9 3.2 %shard_map.104 = (bf16[16,256,256]{2,1,0:T(8,128)(2,1)S(1)}, bf16[16,256,256]{2,1,0:T(8,128)(2,1)}) custom-call(s32[5]{0:T(128)S(1)} %stack.23.me, bf16[8,256,256]{2,1,0:T(8,128)(2,1)S(1)} %copy-done.9, bf16[4,256,256]{2,1,0:T(8,128)(2,1)S(1)} %all_to_all.11.grads), custom_call_target="tpu_custom_call" | custom-call | flops 1073741824 | bytes 5242880 | tf_op jit(solution)/shard_map/pallas_call | solution.py:264
  95.1 1.9 %collective-permute-start.11 = (bf16[16,256,256]{2,1,0:T(8,128)(2,1)}, bf16[16,256,256]{2,1,0:T(8,128)(2,1)}, u32[]{:S(2)}, u32[]{:S(2)}) collective-permute-start(bf16[16,256,256]{2,1,0:T(8,128)(2,1)} %get-tuple-element.14), channel_id=1, source_target_pairs={{0,32},{32,0},{1,33},{33,1},{2,34},{34,2},{3,35},{35,3},{4,36},{36... | collective-permute-start | bytes 6291464 | tf_op jit(solution)/shard_map/ppermute | solution.py:141
  97.0 3.6 %shard_map.103 = bf16[8,256,256]{2,1,0:T(8,128)(2,1)} custom-call(s32[5]{0:T(128)S(1)} %stack.23.me, bf16[4,256,256]{2,1,0:T(8,128)(2,1)S(1)} %all_to_all.11.grads, bf16[256,1024]{1,0:T(8,128)(2,1)S(1)} %pad_maximum_fusion.refs_0_, bf16[256,1024]{1,0:T(8,128)(2,1)S(1)} %copy-done.5, bf16[256,1024]{1,0:T(8,128)(2,1)S(1)} %copy-done.3, ...), custom_call_target="tpu_custom_call" | custom-call | flops 1073741824 | bytes 5242880 | tf_op jit(solution)/shard_map/pallas_call | solution.py:253
  100.7 0.8 collective-permute-done.11
  101.5 2.2 %add_convert_fusion = bf16[16,256,256]{2,1,0:T(8,128)(2,1)S(1)} fusion(bf16[16,256,256]{2,1,0:T(8,128)(2,1)} %collective-permute-done.11, bf16[16,256,256]{2,1,0:T(8,128)(2,1)S(1)} %get-tuple-element.13), kind=kLoop, calls=%fused_computation | loop fusion | flops 4194304 | bytes 6291456 | tf_op jit(solution)/shard_map/convert_element_type | solution.py:267
  103.7 0.1 fusion.1
  103.8 4.9 %collective-permute-start.12 = (bf16[4,256,256]{2,1,0:T(8,128)(2,1)S(1)}, bf16[4,256,256]{2,1,0:T(8,128)(2,1)S(1)}, u32[]{:S(2)}, u32[]{:S(2)}) collective-permute-start(bf16[4,256,256]{2,1,0:T(8,128)(2,1)S(1)} %get-tuple-element.15), channel_id=1, source_target_pairs={{0,256},{128,384},{256,0},{384,128},{1,257},{129,385},{257,1},{385... | collective-permute-start | bytes 1572872 | tf_op jit(solution)/shard_map/ppermute | solution.py:185
  108.8 3.0 %collective-permute-start.14 = (bf16[4,256,256]{2,1,0:T(8,128)(2,1)S(1)}, bf16[4,256,256]{2,1,0:T(8,128)(2,1)S(1)}, u32[]{:S(2)}, u32[]{:S(2)}) collective-permute-start(bf16[4,256,256]{2,1,0:T(8,128)(2,1)S(1)} %get-tuple-element.16), channel_id=1, source_target_pairs={{0,384},{128,256},{256,128},{384,0},{1,385},{129,257},{257,129},{3... | collective-permute-start | bytes 1572872 | tf_op jit(solution)/shard_map/ppermute | solution.py:185
  111.8 1.9 %collective-permute-start.13 = (bf16[4,256,256]{2,1,0:T(8,128)(2,1)S(1)}, bf16[4,256,256]{2,1,0:T(8,128)(2,1)S(1)}, u32[]{:S(2)}, u32[]{:S(2)}) collective-permute-start(bf16[4,256,256]{2,1,0:T(8,128)(2,1)S(1)} %get-tuple-element.17), channel_id=1, source_target_pairs={{0,128},{128,0},{256,384},{384,256},{1,129},{129,1},{257,385},{385... | collective-permute-start | bytes 1572872 | tf_op jit(solution)/shard_map/ppermute | solution.py:185
  113.7 8.3 %collective-permute-done.12 = bf16[4,256,256]{2,1,0:T(8,128)(2,1)S(1)} collective-permute-done((bf16[4,256,256]{2,1,0:T(8,128)(2,1)S(1)}, bf16[4,256,256]{2,1,0:T(8,128)(2,1)S(1)}, u32[]{:S(2)}, u32[]{:S(2)}) %collective-permute-start.12) | collective-permute-done | bytes 524320 | tf_op jit(solution)/shard_map/ppermute | solution.py:185
  122.0 10.4 %collective-permute-done.14 = bf16[4,256,256]{2,1,0:T(8,128)(2,1)S(1)} collective-permute-done((bf16[4,256,256]{2,1,0:T(8,128)(2,1)S(1)}, bf16[4,256,256]{2,1,0:T(8,128)(2,1)S(1)}, u32[]{:S(2)}, u32[]{:S(2)}) %collective-permute-start.14) | collective-permute-done | bytes 524320 | tf_op jit(solution)/shard_map/ppermute | solution.py:185
  132.4 0.3 add_convert_fusion.1
  132.7 5.9 %collective-permute-start.17 = (bf16[256,256]{1,0:T(8,128)(2,1)S(1)}, bf16[256,256]{1,0:T(8,128)(2,1)S(1)}, u32[]{:S(2)}, u32[]{:S(2)}) collective-permute-start(bf16[256,256]{1,0:T(8,128)(2,1)S(1)} %get-tuple-element.20), channel_id=1, source_target_pairs={{65,0},{64,1},{449,16},{448,17},{1,64},{0,65},{385,80},{384,81},{1... | collective-permute-start | bytes 393224 | tf_op jit(solution)/shard_map/ppermute | solution.py:195
  138.6 4.8 %collective-permute-start.18 = (bf16[256,256]{1,0:T(8,128)(2,1)S(1)}, bf16[256,256]{1,0:T(8,128)(2,1)S(1)}, u32[]{:S(2)}, u32[]{:S(2)}) collective-permute-start(bf16[256,256]{1,0:T(8,128)(2,1)S(1)} %get-tuple-element.21), channel_id=1, source_target_pairs={{1,0},{0,1},{385,16},{384,17},{65,64},{64,65},{449,80},{448,81},{1... | collective-permute-start | bytes 393224 | tf_op jit(solution)/shard_map/ppermute | solution.py:195
  143.4 3.7 %collective-permute-start.16 = (bf16[256,256]{1,0:T(8,128)(2,1)S(1)}, bf16[256,256]{1,0:T(8,128)(2,1)S(1)}, u32[]{:S(2)}, u32[]{:S(2)}) collective-permute-start(bf16[256,256]{1,0:T(8,128)(2,1)S(1)} %get-tuple-element.22), channel_id=1, source_target_pairs={{0,0},{1,1},{384,16},{385,17},{64,64},{65,65},{448,80},{449,81},{1... | collective-permute-start | bytes 393224 | tf_op jit(solution)/shard_map/ppermute | solution.py:195
  147.1 3.6 %collective-permute-start.15 = (bf16[256,256]{1,0:T(8,128)(2,1)S(1)}, bf16[256,256]{1,0:T(8,128)(2,1)S(1)}, u32[]{:S(2)}, u32[]{:S(2)}) collective-permute-start(bf16[256,256]{1,0:T(8,128)(2,1)S(1)} %get-tuple-element.23), channel_id=1, source_target_pairs={{64,0},{65,1},{448,16},{449,17},{0,64},{1,65},{384,80},{385,81},{1... | collective-permute-start | bytes 393224 | tf_op jit(solution)/shard_map/ppermute | solution.py:195
  150.8 7.0 %collective-permute-done.18 = bf16[256,256]{1,0:T(8,128)(2,1)S(1)} collective-permute-done((bf16[256,256]{1,0:T(8,128)(2,1)S(1)}, bf16[256,256]{1,0:T(8,128)(2,1)S(1)}, u32[]{:S(2)}, u32[]{:S(2)}) %collective-permute-start.18) | collective-permute-done | bytes 131104 | tf_op jit(solution)/shard_map/ppermute | solution.py:195
  157.8 0.5 collective-permute-done.15
  158.2 0.1 broadcast_select_fusion
  158.3 0.7 pad_maximum_fusion.1
  (40 shorter events, 0.2 us)
Async XLA Ops:
  7.2 60.1 %all-gather.2.cloned.1.call-start = ((), (), s32[]{:S(2)}) async-start(), calls=%async_computation.3 | async-start | bytes 1179648 | tf_op jit(solution)/shard_map/all_gather | solution.py:199
  7.9 151.2 %reduce-scatter.2.cloned.1.call-start = ((), (), s32[]{:S(2)}) async-start(), calls=%async_computation.4 | async-start | bytes 1179648 | tf_op jit(solution)/shard_map/reduce_scatter | solution.py:261
  9.0 13.6 %collective-permute-start.3 = (bf16[256,256]{1,0:T(8,128)(2,1)S(1)}, bf16[256,256]{1,0:T(8,128)(2,1)S(1)}, u32[]{:S(2)}, u32[]{:S(2)}) collective-permute-start(bf16[256,256]{1,0:T(8,128)(2,1)S(1)} %get-tuple-element.27), channel_id=1, source_target_pairs={{0,385},{16,1},{1,384},{17,0},{128,257},{144,129},{129,256},{145,1... | collective-permute-start | bytes 393224 | tf_op jit(solution)/shard_map/ppermute | solution.py:181
  13.1 9.9 %collective-permute-start.2 = (bf16[256,256]{1,0:T(8,128)(2,1)S(1)}, bf16[256,256]{1,0:T(8,128)(2,1)S(1)}, u32[]{:S(2)}, u32[]{:S(2)}) collective-permute-start(bf16[256,256]{1,0:T(8,128)(2,1)S(1)} %get-tuple-element.27), channel_id=1, source_target_pairs={{0,1},{16,385},{1,0},{17,384},{128,129},{144,257},{129,128},{145,2... | collective-permute-start | bytes 393224 | tf_op jit(solution)/shard_map/ppermute | solution.py:181
  18.2 10.1 %collective-permute-start.1 = (bf16[256,256]{1,0:T(8,128)(2,1)S(1)}, bf16[256,256]{1,0:T(8,128)(2,1)S(1)}, u32[]{:S(2)}, u32[]{:S(2)}) collective-permute-start(bf16[256,256]{1,0:T(8,128)(2,1)S(1)} %get-tuple-element.26), channel_id=1, source_target_pairs={{16,384},{17,385},{144,256},{145,257},{256,144},{257,145},{384,16}... | collective-permute-start | bytes 393224 | tf_op jit(solution)/shard_map/ppermute | solution.py:181
  20.6 9.2 %collective-permute-start = (bf16[256,256]{1,0:T(8,128)(2,1)S(1)}, bf16[256,256]{1,0:T(8,128)(2,1)S(1)}, u32[]{:S(2)}, u32[]{:S(2)}) collective-permute-start(bf16[256,256]{1,0:T(8,128)(2,1)S(1)} %get-tuple-element.26), channel_id=1, source_target_pairs={{0,384},{16,0},{1,385},{17,1},{128,256},{144,128},{129,257},{145,1... | collective-permute-start | bytes 393224 | tf_op jit(solution)/shard_map/ppermute | solution.py:181
  29.9 19.2 %collective-permute-start.9 = (bf16[256,1024]{1,0:T(8,128)(2,1)S(1)}, bf16[256,1024]{1,0:T(8,128)(2,1)S(1)}, u32[]{:S(2)}, u32[]{:S(2)}) collective-permute-start(bf16[256,1024]{1,0:T(8,128)(2,1)S(1)} %pad_maximum_fusion.refs_0_), channel_id=1, source_target_pairs={{0,192},{64,128},{128,64},{192,0},{1,193},{65,129},{129,65},{193,1... | collective-permute-start | bytes 1572872 | tf_op jit(solution)/shard_map/ppermute | solution.py:145
  31.8 26.2 %collective-permute-start.7 = (bf16[256,1024]{1,0:T(8,128)(2,1)S(1)}, bf16[256,1024]{1,0:T(8,128)(2,1)S(1)}, u32[]{:S(2)}, u32[]{:S(2)}) collective-permute-start(bf16[256,1024]{1,0:T(8,128)(2,1)S(1)} %pad_maximum_fusion.refs_0_), channel_id=1, source_target_pairs={{0,128},{128,0},{1,129},{129,1},{2,130},{130,2},{3,131},{131,3},{4... | collective-permute-start | bytes 1572872 | tf_op jit(solution)/shard_map/ppermute | solution.py:141
  40.5 19.3 %collective-permute-start.5 = (bf16[256,1024]{1,0:T(8,128)(2,1)S(1)}, bf16[256,1024]{1,0:T(8,128)(2,1)S(1)}, u32[]{:S(2)}, u32[]{:S(2)}) collective-permute-start(bf16[256,1024]{1,0:T(8,128)(2,1)S(1)} %pad_maximum_fusion.refs_0_), channel_id=1, source_target_pairs={{0,64},{64,0},{1,65},{65,1},{2,66},{66,2},{3,67},{67,3},{4,68},{68... | collective-permute-start | bytes 1572872 | tf_op jit(solution)/shard_map/ppermute | solution.py:141
  42.5 20.0 %collective-permute-start.4 = (bf16[256,1024]{1,0:T(8,128)(2,1)S(1)}, bf16[256,1024]{1,0:T(8,128)(2,1)S(1)}, u32[]{:S(2)}, u32[]{:S(2)}) collective-permute-start(bf16[256,1024]{1,0:T(8,128)(2,1)S(1)} %pad_maximum_fusion.refs_0_), channel_id=1, source_target_pairs={{0,32},{32,0},{1,33},{33,1},{2,34},{34,2},{3,35},{35,3},{4,36},{36... | collective-permute-start | bytes 1572872 | tf_op jit(solution)/shard_map/ppermute | solution.py:141
  49.1 13.4 %collective-permute-start.10 = (bf16[256,1024]{1,0:T(8,128)(2,1)S(1)}, bf16[256,1024]{1,0:T(8,128)(2,1)S(1)}, u32[]{:S(2)}, u32[]{:S(2)}) collective-permute-start(bf16[256,1024]{1,0:T(8,128)(2,1)S(1)} %collective-permute-done.9.refs_6_), channel_id=1, source_target_pairs={{0,32},{32,0},{1,33},{33,1},{2,34},{34,2},{3,35},{35,3},{4,36},{36... | collective-permute-start | bytes 1572872 | tf_op jit(solution)/shard_map/ppermute | solution.py:141
  57.9 13.1 %copy-start = (bf16[256,1024]{1,0:T(8,128)(2,1)}, bf16[256,1024]{1,0:T(8,128)(2,1)S(1)}, u32[]{:S(2)}) copy-start(bf16[256,1024]{1,0:T(8,128)(2,1)S(1)} %collective-permute-done.7.refs_4_) | copy-start | bytes 1572868
  57.9 4.5 %collective-permute-start.8 = (bf16[256,1024]{1,0:T(8,128)(2,1)S(1)}, bf16[256,1024]{1,0:T(8,128)(2,1)}, u32[]{:S(2)}, u32[]{:S(2)}) collective-permute-start(bf16[256,1024]{1,0:T(8,128)(2,1)S(1)} %collective-permute-done.7.refs_4_), channel_id=1, source_target_pairs={{0,32},{32,0},{1,33},{33,1},{2,34},{34,2},{3,35},{35,3},{4,36},{36... | collective-permute-start | bytes 1572872 | tf_op jit(solution)/shard_map/ppermute | solution.py:141
  59.9 11.2 %copy-start.2 = (bf16[256,1024]{1,0:T(8,128)(2,1)}, bf16[256,1024]{1,0:T(8,128)(2,1)S(1)}, u32[]{:S(2)}) copy-start(bf16[256,1024]{1,0:T(8,128)(2,1)S(1)} %collective-permute-done.5.refs_2_) | copy-start | bytes 1572868
  59.9 4.1 %collective-permute-start.6 = (bf16[256,1024]{1,0:T(8,128)(2,1)S(1)}, bf16[256,1024]{1,0:T(8,128)(2,1)}, u32[]{:S(2)}, u32[]{:S(2)}) collective-permute-start(bf16[256,1024]{1,0:T(8,128)(2,1)S(1)} %collective-permute-done.5.refs_2_), channel_id=1, source_target_pairs={{0,32},{32,0},{1,33},{33,1},{2,34},{34,2},{3,35},{35,3},{4,36},{36... | collective-permute-start | bytes 1572872 | tf_op jit(solution)/shard_map/ppermute | solution.py:141
  62.3 18.3 %copy-start.12 = (s32[1,8]{1,0:T(1,128)S(1)}, s32[1,8]{1,0:T(1,128)}, u32[]{:S(2)}) copy-start(s32[1,8]{1,0:T(1,128)} %ids.1) | copy-start | bytes 100
  62.4 8.6 %copy-start.4 = (bf16[256,1024]{1,0:T(8,128)(2,1)}, bf16[256,1024]{1,0:T(8,128)(2,1)S(1)}, u32[]{:S(2)}) copy-start(bf16[256,1024]{1,0:T(8,128)(2,1)S(1)} %collective-permute-done.4.refs_1_) | copy-start | bytes 1572868
  62.4 8.6 %copy-start.6 = (bf16[256,1024]{1,0:T(8,128)(2,1)}, bf16[256,1024]{1,0:T(8,128)(2,1)S(1)}, u32[]{:S(2)}) copy-start(bf16[256,1024]{1,0:T(8,128)(2,1)S(1)} %collective-permute-done.10.refs_7_) | copy-start | bytes 1572868
  67.3 1.2 copy-start.8
  68.5 12.1 %copy-start.10 = (bf16[1,256,128]{2,1,0:T(8,128)(2,1)S(1)}, bf16[1,256,128]{2,1,0:T(8,128)(2,1)}, u32[]{:S(2)}) copy-start(bf16[1,256,128]{2,1,0:T(8,128)(2,1)} %param.6) | copy-start | bytes 196612
  68.5 12.1 %copy-start.11 = (bf16[1,256,128]{2,1,0:T(8,128)(2,1)S(1)}, bf16[1,256,128]{2,1,0:T(8,128)(2,1)}, u32[]{:S(2)}) copy-start(bf16[1,256,128]{2,1,0:T(8,128)(2,1)} %param.11) | copy-start | bytes 196612
  71.1 20.8 %copy-start.9 = (bf16[8,256,256]{2,1,0:T(8,128)(2,1)S(1)}, bf16[8,256,256]{2,1,0:T(8,128)(2,1)}, u32[]{:S(2)}) copy-start(bf16[8,256,256]{2,1,0:T(8,128)(2,1)} %all-gather.2.cloned.1.call-done.enc) | copy-start | bytes 3145732
  91.9 5.1 %copy-start.1 = (bf16[256,1024]{1,0:T(8,128)(2,1)S(1)}, bf16[256,1024]{1,0:T(8,128)(2,1)}, u32[]{:S(2)}) copy-start(bf16[256,1024]{1,0:T(8,128)(2,1)} %copy-done) | copy-start | bytes 1572868
  91.9 5.1 %copy-start.3 = (bf16[256,1024]{1,0:T(8,128)(2,1)S(1)}, bf16[256,1024]{1,0:T(8,128)(2,1)}, u32[]{:S(2)}) copy-start(bf16[256,1024]{1,0:T(8,128)(2,1)} %copy-done.2) | copy-start | bytes 1572868
  91.9 5.1 %copy-start.5 = (bf16[256,1024]{1,0:T(8,128)(2,1)S(1)}, bf16[256,1024]{1,0:T(8,128)(2,1)}, u32[]{:S(2)}) copy-start(bf16[256,1024]{1,0:T(8,128)(2,1)} %copy-done.4) | copy-start | bytes 1572868
  91.9 5.2 %copy-start.7 = (bf16[256,1024]{1,0:T(8,128)(2,1)S(1)}, bf16[256,1024]{1,0:T(8,128)(2,1)}, u32[]{:S(2)}) copy-start(bf16[256,1024]{1,0:T(8,128)(2,1)} %copy-done.6) | copy-start | bytes 1572868
  95.1 6.4 %collective-permute-start.11 = (bf16[16,256,256]{2,1,0:T(8,128)(2,1)}, bf16[16,256,256]{2,1,0:T(8,128)(2,1)}, u32[]{:S(2)}, u32[]{:S(2)}) collective-permute-start(bf16[16,256,256]{2,1,0:T(8,128)(2,1)} %get-tuple-element.14), channel_id=1, source_target_pairs={{0,32},{32,0},{1,33},{33,1},{2,34},{34,2},{3,35},{35,3},{4,36},{36... | collective-permute-start | bytes 6291464 | tf_op jit(solution)/shard_map/ppermute | solution.py:141
  103.8 18.2 %collective-permute-start.12 = (bf16[4,256,256]{2,1,0:T(8,128)(2,1)S(1)}, bf16[4,256,256]{2,1,0:T(8,128)(2,1)S(1)}, u32[]{:S(2)}, u32[]{:S(2)}) collective-permute-start(bf16[4,256,256]{2,1,0:T(8,128)(2,1)S(1)} %get-tuple-element.15), channel_id=1, source_target_pairs={{0,256},{128,384},{256,0},{384,128},{1,257},{129,385},{257,1},{385... | collective-permute-start | bytes 1572872 | tf_op jit(solution)/shard_map/ppermute | solution.py:185
  108.8 23.7 %collective-permute-start.14 = (bf16[4,256,256]{2,1,0:T(8,128)(2,1)S(1)}, bf16[4,256,256]{2,1,0:T(8,128)(2,1)S(1)}, u32[]{:S(2)}, u32[]{:S(2)}) collective-permute-start(bf16[4,256,256]{2,1,0:T(8,128)(2,1)S(1)} %get-tuple-element.16), channel_id=1, source_target_pairs={{0,384},{128,256},{256,128},{384,0},{1,385},{129,257},{257,129},{3... | collective-permute-start | bytes 1572872 | tf_op jit(solution)/shard_map/ppermute | solution.py:185
  111.8 20.6 %collective-permute-start.13 = (bf16[4,256,256]{2,1,0:T(8,128)(2,1)S(1)}, bf16[4,256,256]{2,1,0:T(8,128)(2,1)S(1)}, u32[]{:S(2)}, u32[]{:S(2)}) collective-permute-start(bf16[4,256,256]{2,1,0:T(8,128)(2,1)S(1)} %get-tuple-element.17), channel_id=1, source_target_pairs={{0,128},{128,0},{256,384},{384,256},{1,129},{129,1},{257,385},{385... | collective-permute-start | bytes 1572872 | tf_op jit(solution)/shard_map/ppermute | solution.py:185
  132.7 18.0 %collective-permute-start.17 = (bf16[256,256]{1,0:T(8,128)(2,1)S(1)}, bf16[256,256]{1,0:T(8,128)(2,1)S(1)}, u32[]{:S(2)}, u32[]{:S(2)}) collective-permute-start(bf16[256,256]{1,0:T(8,128)(2,1)S(1)} %get-tuple-element.20), channel_id=1, source_target_pairs={{65,0},{64,1},{449,16},{448,17},{1,64},{0,65},{385,80},{384,81},{1... | collective-permute-start | bytes 393224 | tf_op jit(solution)/shard_map/ppermute | solution.py:195
  138.6 19.2 %collective-permute-start.18 = (bf16[256,256]{1,0:T(8,128)(2,1)S(1)}, bf16[256,256]{1,0:T(8,128)(2,1)S(1)}, u32[]{:S(2)}, u32[]{:S(2)}) collective-permute-start(bf16[256,256]{1,0:T(8,128)(2,1)S(1)} %get-tuple-element.21), channel_id=1, source_target_pairs={{1,0},{0,1},{385,16},{384,17},{65,64},{64,65},{449,80},{448,81},{1... | collective-permute-start | bytes 393224 | tf_op jit(solution)/shard_map/ppermute | solution.py:195
  143.4 14.3 %collective-permute-start.16 = (bf16[256,256]{1,0:T(8,128)(2,1)S(1)}, bf16[256,256]{1,0:T(8,128)(2,1)S(1)}, u32[]{:S(2)}, u32[]{:S(2)}) collective-permute-start(bf16[256,256]{1,0:T(8,128)(2,1)S(1)} %get-tuple-element.22), channel_id=1, source_target_pairs={{0,0},{1,1},{384,16},{385,17},{64,64},{65,65},{448,80},{449,81},{1... | collective-permute-start | bytes 393224 | tf_op jit(solution)/shard_map/ppermute | solution.py:195
  147.1 11.1 %collective-permute-start.15 = (bf16[256,256]{1,0:T(8,128)(2,1)S(1)}, bf16[256,256]{1,0:T(8,128)(2,1)S(1)}, u32[]{:S(2)}, u32[]{:S(2)}) collective-permute-start(bf16[256,256]{1,0:T(8,128)(2,1)S(1)} %get-tuple-element.23), channel_id=1, source_target_pairs={{64,0},{65,1},{448,16},{449,17},{0,64},{1,65},{384,80},{385,81},{1... | collective-permute-start | bytes 393224 | tf_op jit(solution)/shard_map/ppermute | solution.py:195
Sparse Core Ops, SparseCore 0:
  10.1 57.1 all-gather.1
  100.8 56.6 reduce-scatter.1
